TPU v7x, 32 devices: a whole 2x2x4 slice. The times are simulated.
32 devices in a mesh: dp: 4 (over y, x), blk: 4 (over z), head: 2 (over core).
Axes of the slice: x: 2, y: 2, z: 4, core: 2. Of those that a mesh axis runs over, the one named last changes fastest.
Arguments:
- tokens: bfloat16 [4, 2048, 768], P('dp', ('blk', 'head')), may hold values from -6 to 6
- segment: int32 [4, 2048], P('dp'), may hold values from 0 to 7, as said below
- w_qkv: bfloat16 [768, 2304], P(('dp', 'blk', 'head')), may hold values from -0.21875 to 0.21875
- bias_query: bfloat16 [768], P(('dp', 'blk', 'head')), may hold values from -3 to 3
- bias_value: bfloat16 [768], P(('dp', 'blk', 'head')), may hold values from -3 to 3
- w_out: bfloat16 [768, 768], P(('dp', 'blk', 'head')), may hold values from -1.75 to 1.75
- bias_out: bfloat16 [768], P(('dp', 'blk', 'head')), may hold values from -3 to 3
- gain_attn: bfloat16 [768], P(('dp', 'blk', 'head')), may hold values from 0.099609375 to 1.8984375
- shift_attn: bfloat16 [768], P(('dp', 'blk', 'head')), may hold values from -3 to 3
- w_in: bfloat16 [768, 3072], P(('dp', 'blk', 'head')), may hold values from -0.21875 to 0.21875
- bias_in: bfloat16 [3072], P(('dp', 'blk', 'head')), may hold values from -3 to 3
- w_down: bfloat16 [3072, 768], P(('dp', 'blk', 'head')), may hold values from -0.109375 to 0.109375
- bias_down: bfloat16 [768], P(('dp', 'blk', 'head')), may hold values from -3 to 3
- gain_ffn: bfloat16 [768], P(('dp', 'blk', 'head')), may hold values from 0.099609375 to 1.8984375
- shift_ffn: bfloat16 [768], P(('dp', 'blk', 'head')), may hold values from -3 to 3
- cotangent: bfloat16 [4, 2048, 768], P('dp', ('blk', 'head')), may hold values from -6 to 6
Outputs:
- output: bfloat16 [4, 2048, 768], P('dp', ('blk', 'head'))
- grad_tokens: float32 [4, 2048, 768], P('dp', ('blk', 'head'))
- grad_w_qkv: float32 [768, 2304], P(('dp', 'blk', 'head'))
- grad_bias_query: float32 [768], P(('dp', 'blk', 'head'))
- grad_bias_value: float32 [768], P(('dp', 'blk', 'head'))
- grad_w_out: float32 [768, 768], P(('dp', 'blk', 'head'))
- grad_bias_out: float32 [768], P(('dp', 'blk', 'head'))
- grad_gain_attn: float32 [768], P(('dp', 'blk', 'head'))
- grad_shift_attn: float32 [768], P(('dp', 'blk', 'head'))
- grad_w_in: float32 [768, 3072], P(('dp', 'blk', 'head'))
- grad_bias_in: float32 [3072], P(('dp', 'blk', 'head'))
- grad_w_down: float32 [3072, 768], P(('dp', 'blk', 'head'))
- grad_bias_down: float32 [768], P(('dp', 'blk', 'head'))
- grad_gain_ffn: float32 [768], P(('dp', 'blk', 'head'))
- grad_shift_ffn: float32 [768], P(('dp', 'blk', 'head'))
Inputs may be any that keep to these rules, and one draw needn't show every extreme that they name: `segment`: document ids of the tokens of each sequence; ids never fall along a sequence (each document is one contiguous run of tokens), and every id of 0 to 7 occurs in every sequence. Among the 1 sequence of each index of dp, one (drawn from the seed) holds a document that covers tokens of the first and of the last of its 4 token blocks.
All inputs are finite; a program needn't handle non-finite values.
Results may differ from a plain program's by a relative error of at most 0.023.
Values may be sent and summed in bfloat16 or wider, within the bound.
A program may use at most 192 MiB of HBM per device.

v0:
```python
import jax
import jax.numpy as jnp
from jax import lax
from jax.sharding import PartitionSpec as P

HEADS = 12
HEAD_DIM = 64


NEG_FILL = -1e30


def layer_norm(hidden, gain, shift):
    centered = hidden - jnp.mean(hidden, axis=-1, keepdims=True)
    variance = jnp.mean(centered * centered, axis=-1, keepdims=True)
    return centered * lax.rsqrt(variance + 1e-12) * gain + shift


def gelu_exact(values):
    return jax.nn.gelu(values, approximate=False)


def matmul(left, right):
    return jnp.dot(left, right, preferred_element_type=jnp.float32)


def matmul_left_t(left, right):
    return lax.dot_general(
        left, right, (((0,), (0,)), ((), ())), preferred_element_type=jnp.float32
    )


def matmul_right_t(left, right):
    return lax.dot_general(
        left, right, (((1,), (1,)), ((), ())), preferred_element_type=jnp.float32
    )


def score_grads(
    query_blk, gctx_blk, lse_blk, delta_blk, keys_four, values_four, query_seg, key_seg, scale
):
    scores = (
        jnp.einsum("sqhd,skhd->sqhk", query_blk, keys_four, preferred_element_type=jnp.float32)
        * scale
    )
    scores = jnp.where(query_seg[:, :, None, None] == key_seg[:, None, None, :], scores, NEG_FILL)
    probs = jnp.exp(scores - lse_blk[..., None])
    grad_probs = jnp.einsum(
        "sqhd,skhd->sqhk", gctx_blk, values_four, preferred_element_type=jnp.float32
    )
    grad_scores = (probs * (grad_probs - delta_blk[..., None])).astype(jnp.bfloat16)
    return (probs, grad_scores)


def body(
    tokens,
    segment,
    w_qkv,
    bias_query,
    bias_value,
    w_out,
    bias_out,
    gain_attn,
    shift_attn,
    w_in,
    bias_in,
    w_down,
    bias_down,
    gain_ffn,
    shift_ffn,
    cotangent,
):
    (
        full_qkv,
        full_bq,
        full_bv,
        full_wout,
        full_bout,
        full_gain_one,
        full_shift_one,
        full_win,
        full_bin,
        full_wdown,
        full_bdown,
        full_gain_two,
        full_shift_two,
    ) = (
        lax.all_gather(w_qkv, ("dp", "blk", "head"), axis=0, tiled=True),
        lax.all_gather(bias_query, ("dp", "blk", "head"), axis=0, tiled=True),
        lax.all_gather(bias_value, ("dp", "blk", "head"), axis=0, tiled=True),
        lax.all_gather(w_out, ("dp", "blk", "head"), axis=0, tiled=True),
        lax.all_gather(bias_out, ("dp", "blk", "head"), axis=0, tiled=True),
        lax.all_gather(gain_attn, ("dp", "blk", "head"), axis=0, tiled=True),
        lax.all_gather(shift_attn, ("dp", "blk", "head"), axis=0, tiled=True),
        lax.all_gather(w_in, ("dp", "blk", "head"), axis=0, tiled=True),
        lax.all_gather(bias_in, ("dp", "blk", "head"), axis=0, tiled=True),
        lax.all_gather(w_down, ("dp", "blk", "head"), axis=0, tiled=True),
        lax.all_gather(bias_down, ("dp", "blk", "head"), axis=0, tiled=True),
        lax.all_gather(gain_ffn, ("dp", "blk", "head"), axis=0, tiled=True),
        lax.all_gather(shift_ffn, ("dp", "blk", "head"), axis=0, tiled=True),
    )
    seqs, tok_seq, width = tokens.shape
    head_split = lax.axis_size("head")
    cycle_size = lax.axis_size("blk")
    heads_local = HEADS // head_split
    local_width = heads_local * HEAD_DIM
    block_len = head_split * tok_seq
    rows = seqs * tok_seq
    scale = HEAD_DIM ** (-0.5)
    blk_index = lax.axis_index("blk")
    flat_in = tokens.reshape(rows, width)
    bias_q32 = full_bq.astype(jnp.float32)
    qkv_bias = jnp.concatenate([bias_q32, jnp.zeros_like(bias_q32), full_bv.astype(jnp.float32)])
    projected = (matmul(flat_in, full_qkv) + qkv_bias).astype(jnp.bfloat16)
    grouped = projected.reshape(seqs, tok_seq, 3, head_split, local_width)
    headed = lax.all_to_all(grouped, "head", split_axis=3, concat_axis=1, tiled=True)
    query = headed[:, :, 0, 0].reshape(seqs, block_len, heads_local, HEAD_DIM)
    stacked_keys = headed[None, :, :, 1, 0]
    stacked_values = headed[None, :, :, 2, 0]
    seg_blocks = segment.reshape(seqs, cycle_size, block_len)
    query_seg = seg_blocks[:, blk_index]
    allowed_base = query_seg[:, :, None, None]

    def masked_scores(key_piece, key_seg):
        keys_four = key_piece.reshape(seqs, block_len, heads_local, HEAD_DIM)
        scores = (
            jnp.einsum("sqhd,skhd->sqhk", query, keys_four, preferred_element_type=jnp.float32)
            * scale
        )
        return jnp.where(allowed_base == key_seg[:, None, None, :], scores, NEG_FILL)

    def stats_piece(state, pieces, key_seg):
        best, total = state
        scores = masked_scores(pieces[0], key_seg)
        new_best = jnp.maximum(best, jnp.max(scores, axis=-1))
        total = total * jnp.exp(best - new_best) + jnp.sum(
            jnp.exp(scores - new_best[..., None]), axis=-1
        )
        return (new_best, total)

    def run_blocks(state, stacks, piece_fn):
        count = stacks[0].shape[0]

        def fold_step(current, entries):
            pieces = entries[:-1]
            block_index = entries[-1]
            key_seg = seg_blocks[:, block_index]
            updated = piece_fn(current, pieces, key_seg)
            return (updated, None)

        state, unused = lax.scan(
            fold_step, state, tuple(stacks) + (jnp.arange(count, dtype=jnp.int32),)
        )
        return state

    stats_init = (
        jnp.full((seqs, block_len, heads_local), NEG_FILL, jnp.float32),
        jnp.zeros((seqs, block_len, heads_local), jnp.float32),
    )
    best, total = run_blocks(
        stats_init, (lax.all_gather(stacked_keys, "blk", axis=0, tiled=True),), stats_piece
    )
    log_sum = best + jnp.log(total)

    def context_piece(state, pieces, key_seg):
        accum, extra = state
        key_piece, value_piece = pieces
        values_four = value_piece.reshape(seqs, block_len, heads_local, HEAD_DIM)
        probs = jnp.exp(masked_scores(key_piece, key_seg) - log_sum[..., None])
        probs_low = probs.astype(jnp.bfloat16)
        rest_low = (probs - probs_low.astype(jnp.float32)).astype(jnp.bfloat16)
        accum = accum + jnp.einsum(
            "sqhk,skhd->sqhd", probs_low, values_four, preferred_element_type=jnp.float32
        )
        extra = extra + jnp.einsum(
            "sqhk,skhd->sqhd", rest_low, values_four, preferred_element_type=jnp.float32
        )
        return (accum, extra)

    zero_query = jnp.zeros((seqs, block_len, heads_local, HEAD_DIM), jnp.float32)
    context, extra = run_blocks(
        (zero_query, zero_query),
        (
            lax.all_gather(stacked_keys, "blk", axis=0, tiled=True),
            lax.all_gather(stacked_values, "blk", axis=0, tiled=True),
        ),
        context_piece,
    )
    context_exact = context + extra
    context_low = context.astype(jnp.bfloat16).reshape(seqs, block_len, 1, local_width)
    back_tokens = lax.all_to_all(context_low, "head", split_axis=1, concat_axis=2, tiled=True)
    context_flat = back_tokens.reshape(rows, width)
    attn_out = matmul(context_flat, full_wout) + full_bout.astype(jnp.float32)
    resid_one = flat_in.astype(jnp.float32) + attn_out
    normed_one, norm_one_pull = jax.vjp(
        layer_norm, resid_one, full_gain_one.astype(jnp.float32), full_shift_one.astype(jnp.float32)
    )
    normed_low = normed_one.astype(jnp.bfloat16)
    pre_act = matmul(normed_low, full_win) + full_bin.astype(jnp.float32)
    activated, gelu_pull = jax.vjp(gelu_exact, pre_act)
    act_low = activated.astype(jnp.bfloat16)
    ffn_out = matmul(act_low, full_wdown) + full_bdown.astype(jnp.float32)
    resid_two = normed_one + ffn_out
    result, norm_two_pull = jax.vjp(
        layer_norm, resid_two, full_gain_two.astype(jnp.float32), full_shift_two.astype(jnp.float32)
    )
    output = result.astype(jnp.bfloat16).reshape(seqs, tok_seq, width)
    grad_result = cotangent.reshape(rows, width).astype(jnp.float32)
    grad_resid_two, grad_gain_two, grad_shift_two = norm_two_pull(grad_result)
    grad_ffn = grad_resid_two.astype(jnp.bfloat16)
    grad_bias_down = jnp.sum(grad_ffn.astype(jnp.float32), axis=0)
    grad_w_down = matmul_left_t(act_low, grad_ffn)
    grad_act = matmul_right_t(grad_ffn, full_wdown)
    (grad_pre,) = gelu_pull(grad_act)
    grad_pre_low = grad_pre.astype(jnp.bfloat16)
    grad_bias_in = jnp.sum(grad_pre_low.astype(jnp.float32), axis=0)
    grad_w_in = matmul_left_t(normed_low, grad_pre_low)
    grad_normed = grad_resid_two + matmul_right_t(grad_pre_low, full_win)
    grad_resid_one, grad_gain_one, grad_shift_one = norm_one_pull(grad_normed)
    grad_attn = grad_resid_one.astype(jnp.bfloat16)
    grad_bias_out = jnp.sum(grad_attn.astype(jnp.float32), axis=0)
    grad_w_out = matmul_left_t(context_flat, grad_attn)
    grad_context = matmul_right_t(grad_attn, full_wout).astype(jnp.bfloat16)
    grad_headed = lax.all_to_all(
        grad_context.reshape(seqs, tok_seq, head_split, local_width),
        "head",
        split_axis=2,
        concat_axis=1,
        tiled=True,
    )
    grad_ctx_four = grad_headed.reshape(seqs, block_len, heads_local, HEAD_DIM)
    delta = jnp.sum(grad_ctx_four.astype(jnp.float32) * context_exact, axis=-1)
    all_keys, all_values = (
        lax.all_gather(stacked_keys, "blk", axis=0, tiled=True),
        lax.all_gather(stacked_values, "blk", axis=0, tiled=True),
    )

    def back_block(grad_query, key_piece, value_piece, key_seg):
        keys_four = key_piece.reshape(seqs, block_len, heads_local, HEAD_DIM)
        values_four = value_piece.reshape(seqs, block_len, heads_local, HEAD_DIM)
        probs, grad_scores = score_grads(
            query, grad_ctx_four, log_sum, delta, keys_four, values_four, query_seg, key_seg, scale
        )
        grad_query = grad_query + jnp.einsum(
            "sqhk,skhd->sqhd", grad_scores, keys_four, preferred_element_type=jnp.float32
        )
        grad_key = jnp.einsum(
            "sqhk,sqhd->skhd", grad_scores, query, preferred_element_type=jnp.float32
        )
        grad_value = jnp.einsum(
            "sqhk,sqhd->skhd",
            probs.astype(jnp.bfloat16),
            grad_ctx_four,
            preferred_element_type=jnp.float32,
        )
        return (
            grad_query,
            grad_key.reshape(seqs, block_len, local_width),
            grad_value.reshape(seqs, block_len, local_width),
        )

    def back_step(grad_query, entries):
        key_piece, value_piece, block_index = entries
        key_seg = seg_blocks[:, block_index]
        new_query, grad_key, grad_value = back_block(grad_query, key_piece, value_piece, key_seg)
        return (new_query, (grad_key, grad_value))

    grad_query, (key_terms, value_terms) = lax.scan(
        back_step, zero_query, (all_keys, all_values, jnp.arange(cycle_size, dtype=jnp.int32))
    )
    own_key, own_value = (
        lax.psum_scatter(
            key_terms.astype(jnp.bfloat16), "blk", scatter_dimension=0, tiled=True
        ).astype(jnp.float32),
        lax.psum_scatter(
            value_terms.astype(jnp.bfloat16), "blk", scatter_dimension=0, tiled=True
        ).astype(jnp.float32),
    )
    grad_k_low = (own_key[0] * scale).astype(jnp.bfloat16)
    grad_v_low = own_value[0].astype(jnp.bfloat16)
    grad_q_low = (grad_query * scale).astype(jnp.bfloat16).reshape(seqs, block_len, local_width)
    grad_stack = jnp.stack([grad_q_low, grad_k_low, grad_v_low], axis=2)[:, :, :, None]
    grad_back = lax.all_to_all(grad_stack, "head", split_axis=1, concat_axis=3, tiled=True)
    grad_projected = grad_back.reshape(rows, 3 * width)
    grad_proj_f32 = jnp.sum(grad_projected.astype(jnp.float32), axis=0)
    grad_bias_query = grad_proj_f32[:width]
    grad_bias_value = grad_proj_f32[2 * width :]
    grad_w_qkv = matmul_left_t(flat_in, grad_projected)
    grad_tokens = (grad_resid_one + matmul_right_t(grad_projected, full_qkv)).reshape(
        seqs, tok_seq, width
    )
    (
        sum_w_qkv,
        sum_bq,
        sum_bv,
        sum_w_out,
        sum_bout,
        sum_gain_one,
        sum_shift_one,
        sum_w_in,
        sum_bin,
        sum_w_down,
        sum_bdown,
        sum_gain_two,
        sum_shift_two,
    ) = (
        lax.psum_scatter(grad_w_qkv, ("dp", "blk", "head"), scatter_dimension=0, tiled=True),
        lax.psum_scatter(grad_bias_query, ("dp", "blk", "head"), scatter_dimension=0, tiled=True),
        lax.psum_scatter(grad_bias_value, ("dp", "blk", "head"), scatter_dimension=0, tiled=True),
        lax.psum_scatter(grad_w_out, ("dp", "blk", "head"), scatter_dimension=0, tiled=True),
        lax.psum_scatter(grad_bias_out, ("dp", "blk", "head"), scatter_dimension=0, tiled=True),
        lax.psum_scatter(grad_gain_one, ("dp", "blk", "head"), scatter_dimension=0, tiled=True),
        lax.psum_scatter(grad_shift_one, ("dp", "blk", "head"), scatter_dimension=0, tiled=True),
        lax.psum_scatter(grad_w_in, ("dp", "blk", "head"), scatter_dimension=0, tiled=True),
        lax.psum_scatter(grad_bias_in, ("dp", "blk", "head"), scatter_dimension=0, tiled=True),
        lax.psum_scatter(grad_w_down, ("dp", "blk", "head"), scatter_dimension=0, tiled=True),
        lax.psum_scatter(grad_bias_down, ("dp", "blk", "head"), scatter_dimension=0, tiled=True),
        lax.psum_scatter(grad_gain_two, ("dp", "blk", "head"), scatter_dimension=0, tiled=True),
        lax.psum_scatter(grad_shift_two, ("dp", "blk", "head"), scatter_dimension=0, tiled=True),
    )
    return (
        output,
        grad_tokens,
        sum_w_qkv,
        sum_bq,
        sum_bv,
        sum_w_out,
        sum_bout,
        sum_gain_one,
        sum_shift_one,
        sum_w_in,
        sum_bin,
        sum_w_down,
        sum_bdown,
        sum_gain_two,
        sum_shift_two,
    )


def solution(mesh):
    placed = (
        P("dp", ("blk", "head"), None),
        P("dp", None),
        P(("dp", "blk", "head"), None),
        P(("dp", "blk", "head")),
        P(("dp", "blk", "head")),
        P(("dp", "blk", "head"), None),
        P(("dp", "blk", "head")),
        P(("dp", "blk", "head")),
        P(("dp", "blk", "head")),
        P(("dp", "blk", "head"), None),
        P(("dp", "blk", "head")),
        P(("dp", "blk", "head"), None),
        P(("dp", "blk", "head")),
        P(("dp", "blk", "head")),
        P(("dp", "blk", "head")),
        P("dp", ("blk", "head"), None),
    )
    return jax.shard_map(
        body,
        mesh=mesh,
        in_specs=placed,
        out_specs=(
            P("dp", ("blk", "head"), None),
            P("dp", ("blk", "head"), None),
            P(("dp", "blk", "head"), None),
            P(("dp", "blk", "head")),
            P(("dp", "blk", "head")),
            P(("dp", "blk", "head"), None),
            P(("dp", "blk", "head")),
            P(("dp", "blk", "head")),
            P(("dp", "blk", "head")),
            P(("dp", "blk", "head"), None),
            P(("dp", "blk", "head")),
            P(("dp", "blk", "head"), None),
            P(("dp", "blk", "head")),
            P(("dp", "blk", "head")),
            P(("dp", "blk", "head")),
        ),
        check_vma=False,
    )
```

profile of v0, /device:TPU:0, one launch (start us, length us, event | category | flops | bytes accessed | tf_op | source)
XLA Modules:
  0.0 1030.9 jit_solution(11350028197781035227)
XLA Ops:
  15.5 42.4 %all-reduce.19 = (bf16[3072]{0:T(1024)(128)(2,1)S(1)}, bf16[768]{0:T(1024)(128)(2,1)S(1)}, bf16[768]{0:T(1024)(128)(2,1)S(1)}, bf16[768]{0:T(1024)(128)(2,1)S(1)...) all-reduce(bf16[3072]{0:T(1024)(128)(2,1)S(1)} %dynamic-update-slic, ...), channel_id=1, replica_groups=mesh['dp'=4,'blk'=4,'head'=2] {'dp','blk','head'}, use_global_device_ids=true, to_apply=%add.5 | all-reduce | flops 9216 | bytes 36864
  57.9 16.2 %all-gather.9.cloned.1.call-done = bf16[768,2304]{1,0:T(8,128)(2,1)} async-done(((bf16[24,2304]{1,0:T(8,128)(2,1)}), bf16[768,2304]{1,0:T(8,128)(2,1)}) %all-gather.9.cloned.1.call-update) | async-done | bytes 3538960 | tf_op jit(solution)/shard_map/all_gather | solution.py:88
  74.1 3.2 fusion.50
  77.8 4.7 all_to_all.63
  88.5 31.2 %all-gather.19.cloned.1.call-done = bf16[4,512,1,1,384]{4,1,3,2,0:T(8,128)(2,1)} async-done(((bf16[1,512,1,1,384]{4,1,3,2,0:T(8,128)(2,1)}), bf16[4,512,1,1,384]{4,1,3,2,0:T(8,128)(2,1)}) %all-gather.19.cloned.1.call-update) | async-done | bytes 1572880 | tf_op jit(solution)/shard_map/all_gather | solution.py:184
  122.3 47.2 %while.41 = (s32[]{:T(128)}, f32[1,512,6]{1,2,0:T(8,128)S(1)}, f32[1,512,6]{1,2,0:T(8,128)S(1)}, s32[1,512,1,1]{1,3,2,0:T(1,128)S(1)}, s32[4]{0:T(128)S(1)}, /*i...) while((s32[]{:T(128)}, f32[1,512,6]{1,2,0:T(8,128)S(1)}, ...), condition=%wide.region_3.4_spmd.clone, body=%wide.region_0.3_spmd.clone.sunk | while | flops 212614144 | bytes 15110318 | solution.py:151
  126.1 3.8 fusion.142
  129.9 4.1 exponential_reduce_fusion.2
  137.9 3.8 fusion.142
  141.7 4.1 exponential_reduce_fusion.2
  149.7 3.8 fusion.142
  153.6 4.1 exponential_reduce_fusion.2
  161.5 3.8 fusion.142
  165.3 4.1 exponential_reduce_fusion.2
  172.8 60.5 %while.42 = (s32[]{:T(128)}, f32[1,512,6,64]{1,3,2,0:T(8,128)S(1)}, f32[1,512,6,64]{1,3,2,0:T(8,128)S(1)}, bf16[4,1,512,384]{2,3,1,0:T(8,128)(2,1)}, s32[1,512,1...) while((s32[]{:T(128)}, f32[1,512,6,64]{1,3,2,0:T(8,128)S(1)}, ...), condition=%wide.region_5.6_spmd.clone, body=%wide.region_4.5_spmd.clone.sunk | while | flops 622329856 | bytes 51151060 | solution.py:151
  176.7 3.7 fusion.149
  180.4 4.9 fusion.151
  191.8 3.7 fusion.149
  195.5 4.9 fusion.151
  207.0 3.7 fusion.149
  210.6 5.0 fusion.151
  222.1 3.7 fusion.149
  225.8 4.9 fusion.151
  235.9 3.0 reduce.10
  239.0 4.2 all_to_all.64
  246.2 32.6 %all-gather.13.cloned.1.call-done = bf16[768,3072]{1,0:T(8,128)(2,1)} async-done(((bf16[24,3072]{1,0:T(8,128)(2,1)}), bf16[768,3072]{1,0:T(8,128)(2,1)}) %all-gather.13.cloned.1.call-update) | async-done | bytes 4718608 | tf_op jit(solution)/shard_map/all_gather | solution.py:95
  278.8 11.6 %multiply_convert_fusion = (bf16[256,3072]{1,0:T(8,128)(2,1)}, f32[256,3072]{1,0:T(8,128)}, f32[256,3072]{1,0:T(8,128)}) fusion(f32[3072]{0:T(1024)S(1)} %convert_element_type.152, bf16[768,3072]{1,0:T(8,128)(2,1)} %all-gather.13.cloned.1.call-done, f32[256,768]{1,0:T(8,128)S(1)} %get-tuple-element.643, f32[768]{0:T(1024)S(1)} %convert_element_type.150, ...), kind=kOutput, calls=%fused_computation.71 | convolution fusion | flops 1260847104 | bytes 13389824 | tf_op jit(solution)/shard_map/dot_general | solution.py:24
  290.4 53.8 %all-gather.15.cloned.1.call-done = bf16[3072,768]{1,0:T(8,128)(2,1)} async-done(((bf16[96,768]{1,0:T(8,128)(2,1)}), bf16[3072,768]{1,0:T(8,128)(2,1)}) %all-gather.15.cloned.1.call-update) | async-done | bytes 4718608 | tf_op jit(solution)/shard_map/all_gather | solution.py:97
  344.2 4.5 fusion.82
  360.2 4.4 all_to_all.65
  368.6 72.0 %while.43 = (s32[]{:T(128)}, f32[1,512,6,64]{1,3,2,0:T(8,128)}, bf16[4,1,512,384]{2,3,1,0:T(8,128)(2,1)}, bf16[4,1,512,384]{2,3,1,0:T(8,128)(2,1)}, bf16[4,1,512...) while((s32[]{:T(128)}, f32[1,512,6,64]{1,3,2,0:T(8,128)}, ...), condition=%wide.region_16.17_spmd.clone, body=%wide.region_15.16_spmd.clone.sunk | while | flops 1023016960 | bytes 38974196 | solution.py:268
  375.8 3.3 fusion.163
  393.7 3.3 fusion.163
  411.7 3.3 fusion.163
  429.8 3.3 fusion.163
  443.8 5.2 fusion.73
  450.4 5.1 fusion.84
  456.7 18.2 %reduce-scatter.9.cloned.1.call-done = bf16[1,1,512,384]{2,3,1,0:T(8,128)(2,1)} async-done(((bf16[4,1,512,384]{2,3,1,0:T(8,128)(2,1)}), bf16[1,1,512,384]{2,3,1,0:T(8,128)(2,1)}) %reduce-scatter.9.cloned.1.call-update) | async-done | bytes 393232 | tf_op jit(solution)/shard_map/reduce_scatter | solution.py:272
  476.0 35.5 %reduce-scatter.11.cloned.1.call-done = bf16[1,1,512,384]{2,3,1,0:T(8,128)(2,1)} async-done(((bf16[4,1,512,384]{2,3,1,0:T(8,128)(2,1)}), bf16[1,1,512,384]{2,3,1,0:T(8,128)(2,1)}) %reduce-scatter.11.cloned.1.call-update) | async-done | bytes 393232 | tf_op jit(solution)/shard_map/reduce_scatter | solution.py:275
  514.1 5.2 all_to_all.66
  520.2 3.9 convolution_bitcast_fusion.1
  524.1 8.1 copy.168
  533.6 40.3 %all-reduce.18 = (f32[768]{0:T(1024)S(1)}, f32[768]{0:T(1024)S(1)}, f32[768]{0:T(1024)S(1)}, f32[768]{0:T(1024)S(1)}, f32[768]{0:T(1024)S(1)}, /*index=5*/f32[30...) all-reduce(f32[768]{0:T(1024)S(1)} %slice.25, ...), channel_id=7, replica_groups=mesh['dp'=4,'blk'=4,'head'=2] {'dp','blk','head'}, use_global_device_ids=true, to_apply=%region_21.22.clone | all-reduce | flops 9216 | bytes 73728
  579.1 4.0 fusion.58
  583.2 32.4 %reduce-scatter.13.cloned.1.call-done = f32[24,768]{1,0:T(8,128)} async-done(((f32[768,768]{1,0:T(8,128)}), f32[24,768]{1,0:T(8,128)}) %reduce-scatter.13.cloned.1.call-update) | async-done | bytes 73744 | tf_op jit(solution)/shard_map/reduce_scatter | solution.py:310
  615.5 142.0 %reduce-scatter.15.cloned.1.call-done = f32[24,3072]{1,0:T(8,128)} async-done(((f32[768,3072]{1,0:T(8,128)}), f32[24,3072]{1,0:T(8,128)}) %reduce-scatter.15.cloned.1.call-update) | async-done | bytes 294928 | tf_op jit(solution)/shard_map/reduce_scatter | solution.py:314
  757.6 141.1 %reduce-scatter.17.cloned.1.call-done = f32[96,768]{1,0:T(8,128)} async-done(((f32[3072,768]{1,0:T(8,128)}), f32[96,768]{1,0:T(8,128)}) %reduce-scatter.17.cloned.1.call-update) | async-done | bytes 294928 | tf_op jit(solution)/shard_map/reduce_scatter | solution.py:316
  898.6 125.2 %reduce-scatter.19.cloned.1.call-done = f32[24,2304]{1,0:T(8,128)} async-done(((f32[768,2304]{1,0:T(8,128)}), f32[24,2304]{1,0:T(8,128)}) %reduce-scatter.19.cloned.1.call-update) | async-done | bytes 221200
  (308 shorter events, 134.5 us)
Async XLA Ops:
  7.2 66.9 %all-gather.9.cloned.1.call-start = ((), (), s32[]{:S(2)}) async-start(), calls=%async_computation.10 | async-start | bytes 3649536 | tf_op jit(solution)/shard_map/all_gather | solution.py:88
  7.9 111.8 %all-gather.19.cloned.1.call-start = ((), (), s32[]{:S(2)}) async-start(), calls=%async_computation.20 | async-start | bytes 1966080 | tf_op jit(solution)/shard_map/all_gather | solution.py:184
  82.5 4.5 copy-start.30
  83.7 85.9 %all-gather.17.cloned.1.call-start = ((), (), s32[]{:S(2)}) async-start(), calls=%async_computation.19 | async-start | bytes 1966080 | tf_op jit(solution)/shard_map/all_gather | solution.py:185
  84.4 159.5 %all-gather.11.cloned.1.call-start = ((), (), s32[]{:S(2)}) async-start(), calls=%async_computation.11 | async-start | bytes 1216512 | tf_op jit(solution)/shard_map/all_gather | solution.py:91
  85.0 193.8 %all-gather.13.cloned.1.call-start = ((), (), s32[]{:S(2)}) async-start(), calls=%async_computation.12 | async-start | bytes 4866048 | tf_op jit(solution)/shard_map/all_gather | solution.py:95
  85.6 258.6 %all-gather.15.cloned.1.call-start = ((), (), s32[]{:S(2)}) async-start(), calls=%async_computation.13 | async-start | bytes 4866048 | tf_op jit(solution)/shard_map/all_gather | solution.py:97
  86.1 388.8 %reduce-scatter.9.cloned.1.call-start = ((), (), s32[]{:S(2)}) async-start(), calls=%async_computation.14 | async-start | bytes 1966080 | tf_op jit(solution)/shard_map/reduce_scatter | solution.py:272
  180.4 4.9 copy-start
  195.5 4.9 copy-start
  210.6 5.0 copy-start
  225.8 4.9 copy-start
  235.3 8.6 copy-start.17
  243.9 46.5 %copy-start.6 = (bf16[1,256,2,1,384]{1,4,2,3,0:T(8,128)(2,1)}, bf16[1,256,2,1,384]{1,4,2,3,0:T(8,128)(2,1)S(1)}, u32[]{:S(2)}) copy-start(bf16[1,256,2,1,384]{1,4,2,3,0:T(8,128)(2,1)S(1)} %copy.154) | copy-start | bytes 1179652
  245.9 110.9 %copy-start.3 = (f32[256,768]{1,0:T(8,128)}, f32[256,768]{1,0:T(8,128)S(1)}, u32[]{:S(2)}) copy-start(f32[256,768]{1,0:T(8,128)S(1)} %get-tuple-element.643) | copy-start | bytes 2359300
  245.9 110.9 %copy-start.23 = (f32[256]{0:T(256)}, f32[256]{0:T(256)S(1)}, u32[]{:S(2)}) copy-start(f32[256]{0:T(256)S(1)} %broadcast_multiply_fusion.1) | copy-start | bytes 3076
  246.1 110.7 %copy-start.28 = (f32[256]{0:T(256)}, f32[256]{0:T(256)S(1)}, u32[]{:S(2)}) copy-start(f32[256]{0:T(256)S(1)} %fusion.71) | copy-start | bytes 3076
  344.2 7.6 slice-start.2
  344.2 4.7 copy-start.8
  344.2 7.6 slice-start.3
  344.2 7.6 copy-start.33
  348.6 3.1 copy-start.32
  351.0 3.5 slice-start
  351.7 2.8 copy-start.15
  351.8 2.8 slice-start.1
  354.5 2.3 copy-start.19
  356.8 2.8 copy-start.5
  357.2 8.1 copy-start.31
  358.8 7.5 copy-start.22
  373.7 1.0 copy-start.1
  409.6 1.0 copy-start.1
  440.6 1.1 copy-start.11
  440.7 70.9 %reduce-scatter.11.cloned.1.call-start = ((), (), s32[]{:S(2)}) async-start(), calls=%async_computation.15 | async-start | bytes 1966080 | tf_op jit(solution)/shard_map/reduce_scatter | solution.py:275
  441.4 2.3 copy-start.4
  441.4 2.3 copy-start.20
  441.4 2.3 copy-start.24
  441.4 2.3 copy-start.29
  441.5 174.1 %reduce-scatter.13.cloned.1.call-start = ((), (), s32[]{:S(2)}) async-start(), calls=%async_computation.16 | async-start | bytes 2433024 | tf_op jit(solution)/shard_map/reduce_scatter | solution.py:310
  443.7 313.9 %reduce-scatter.15.cloned.1.call-start = ((), (), s32[]{:S(2)}) async-start(), calls=%async_computation.17 | async-start | bytes 9732096 | tf_op jit(solution)/shard_map/reduce_scatter | solution.py:314
  449.0 1.4 copy-start.14
  449.0 1.5 copy-start.16
  449.0 449.6 %reduce-scatter.17.cloned.1.call-start = ((), (), s32[]{:S(2)}) async-start(), calls=%async_computation.18 | async-start | bytes 9732096 | tf_op jit(solution)/shard_map/reduce_scatter | solution.py:316
  455.5 1.1 copy-start.2
  455.6 568.3 %reduce-scatter.19.cloned.1.call-start = ((), (), s32[]{:S(2)}) async-start(), calls=%async_computation.21 | async-start | bytes 7299072
  532.2 1.3 copy-start.25
  532.2 1.3 copy-start.26
  532.2 1.3 copy-start.27
  532.2 46.9 %copy-start.13 = (f32[256,768]{1,0:T(8,128)S(1)}, f32[256,768]{1,0:T(8,128)}, u32[]{:S(2)}) copy-start(f32[256,768]{1,0:T(8,128)} %copy-done.12) | copy-start | bytes 2359300
  (8 other events, 7.6 us)
Sparse Core Ops, SparseCore 0:
  11.0 63.0 all-gather.8
  83.8 35.8 all-gather.18
  121.3 35.9 all-gather.16
  160.2 53.0 all-gather.10
  216.1 62.6 all-gather.12
  281.6 62.4 all-gather.14
  440.8 34.0 reduce-scatter.8
  477.2 34.2 reduce-scatter.10
  517.4 98.1 reduce-scatter.12
  622.9 134.6 reduce-scatter.14
  764.0 134.5 reduce-scatter.16
  905.7 118.1 reduce-scatter.18
where the time goes:
time: 1040 us; the launch traced here: 1030 us
  waiting for transfers between devices  632 us (61%)
  matrix products  150 us (14%)
  blocking collectives  101 us (10%)
  local copies, waits for them, and re-layouts  72.9 us (7%)
  other arithmetic  34.9 us (3%)
  loops' own time  23.9 us (2%)
  between operations  15.1 us (1%)
    reduce_scatter x1, waiting for transfers between devices, body(): lax.psum_scatter(grad_w_in, ('dp', 'blk', 'head'), scatter_dimension=0, t...  142 us
    reduce_scatter x1, waiting for transfers between devices, body(): lax.psum_scatter(grad_w_down, ('dp', 'blk', 'head'), scatter_dimension=0,...  141 us
    unnamed x13, waiting for transfers between devices  129 us
    unnamed x2, blocking collectives  82.7 us
    all_gather x1, waiting for transfers between devices, body(): lax.all_gather(w_down, ('dp', 'blk', 'head'), axis=0, tiled=True)  53.8 us
    reduce_scatter x1, waiting for transfers between devices, body(): lax.psum_scatter(value_terms.astype(jnp.bfloat16), 'blk', scatter_dimensi...  35.5 us
    unnamed x107, local copies, waits for them, and re-layouts  34 us
    all_gather x1, waiting for transfers between devices, body(): lax.all_gather(w_in, ('dp', 'blk', 'head'), axis=0, tiled=True)  32.6 us
  transfers between devices with their start and end apart: 12, of which 10 were waited for; matrix products, arithmetic and copies ran while one was open for 16% of the time, Pallas kernels for 0%

commit v1 on v0

v1 whole, which is shorter than its diff:
```python
import functools

import jax
import jax.numpy as jnp
from jax import lax
from jax.experimental import pallas as pl
from jax.experimental.pallas import tpu as pltpu
from jax.sharding import PartitionSpec as P

MESH = pl.DeviceIdType.MESH
F32, BF16 = jnp.float32, jnp.bfloat16
HD = 64
HEADS = 12
BIG = 2.0**30

class Net:
    def __init__(self, nd, nb, nc):
        self.nd, self.nb, self.nc = nd, nb, nc
        self.levels = nd.bit_length() - 1
        self.d, self.b, self.c = (lax.axis_index(a) for a in ("dp", "blk", "head"))
        top = self.levels - 1
        self.stride = [(1 - self.c) * 2**k + self.c * 2 ** (top - k) for k in range(self.levels)]
        self.sibling = (self.d, self.b, self.nc - 1 - self.c)

    def flip(self, d, k):
        s = self.stride[k]
        return d + s * (1 - 2 * ((d // s) % 2))

    def flips(self, mask):
        d = self.d
        for k in range(self.levels):
            if (mask >> k) & 1:
                d = self.flip(d, k)
        return d

    def across(self, k):
        return (self.flip(self.d, k), self.b, self.c)

    def near(self, e):
        order = [sorted(range(self.nb), key=lambda j: (abs(j - i), -j)) for i in range(self.nb)]
        got = order[0][e]
        for i in range(1, self.nb):
            got = jnp.where(self.b == i, order[i][e], got)
        return got

    def slot(self, mask, blk):
        return (self.flips(mask) * self.nb + blk) * self.nc + self.c

    def peers(self):
        out = [(self.d, (self.b + u) % self.nb, self.c) for u in range(1, self.nb)]
        out += [self.across(k) for k in range(self.levels)]
        return out + [self.sibling]

    def barrier(self):
        bar = pltpu.get_barrier_semaphore()
        ps = self.peers()
        for p in ps:
            pl.semaphore_signal(bar, inc=1, device_id=p, device_id_type=MESH)
        pl.semaphore_wait(bar, len(ps))


def remote(src, dst, send, recv, dev):
    return pltpu.make_async_remote_copy(src_ref=src, dst_ref=dst, send_sem=send, recv_sem=recv, device_id=dev, device_id_type=MESH)


class Gather:
    def __init__(self, net, mine, full, sems, narrow=False):
        self.net, self.mine, self.full, self.narrow = net, mine, full, narrow
        self.zsend, self.xsend, self.ssend, self.srecv, self.recv = sems

    def at(self, mask, blk):
        n = self.net
        if self.narrow:
            return self.full.at[blk * n.nc + n.c]
        return self.full.at[n.slot(mask, blk)]

    def rsem(self, mask, blk):
        return self.recv.at[mask * self.net.nb + blk]

    def spread(self, mask, blk, src, dst):
        n = self.net
        if not self.narrow:
            for k in range(n.levels):
                if mask < (1 << k):
                    remote(src, dst, self.xsend, self.rsem(mask + (1 << k), blk), n.across(k)).start()
        remote(src, dst, self.ssend, self.srecv, n.sibling).start()

    def z(self, e):
        n = self.net
        blk = n.near(e)
        dst = self.at(0, blk)
        src = self.mine if e == 0 else dst
        sem = self.rsem(0, blk)
        if e:
            pltpu.make_async_copy(dst, dst, sem).wait()
        right = (n.d, n.b + 1, n.c)
        left = (n.d, n.b - 1, n.c)

        @pl.when((n.b < n.nb - 1) & (blk <= n.b))
        def _():
            remote(src, dst, self.zsend, sem, right).start()

        @pl.when((n.b > 0) & (blk >= n.b))
        def _():
            remote(src, dst, self.zsend, sem, left).start()

        self.spread(0, blk, src, dst)

    def x(self, mask, e):
        n = self.net
        blk = n.near(e)
        dst = self.at(mask, blk)
        pltpu.make_async_copy(dst, dst, self.rsem(mask, blk)).wait()
        self.spread(mask, blk, dst, dst)

    def own(self, sem):
        n = self.net
        return pltpu.make_async_copy(self.mine, self.at(0, n.b), sem)

    def wait_sibling(self):
        n = self.net
        half = self.full.at[pl.ds(0, n.nb if self.narrow else n.nd * n.nb)]
        pltpu.make_async_copy(half, half, self.srecv).wait()

    def drain(self):
        n = self.net
        half = self.full.at[pl.ds(0, n.nb if self.narrow else n.nd * n.nb)]
        pltpu.make_async_copy(half, half, self.ssend).wait()
        if not self.narrow:
            part = self.full.at[pl.ds(0, (n.nd - 1) * n.nb)]
            pltpu.make_async_copy(part, part, self.xsend).wait()
        edge = (n.b == 0) | (n.b == n.nb - 1)

        @pl.when(edge)
        def _():
            one = self.full.at[pl.ds(0, 1)]
            pltpu.make_async_copy(one, one, self.zsend).wait()

        @pl.when(jnp.logical_not(edge))
        def _():
            many = self.full.at[pl.ds(0, n.nb + 1)]
            pltpu.make_async_copy(many, many, self.zsend).wait()


def gather_sems(n_pieces, nd, nb):
    return [pltpu.SemaphoreType.DMA((n_pieces, 4)), pltpu.SemaphoreType.DMA((n_pieces, nd * nb)), pltpu.SemaphoreType.DMA]


class Scatter:
    def __init__(self, net, full, sib, xrecv, zrecv, out, sems, narrow=False, joined=False):
        self.net, self.full, self.sib, self.xbuf, self.zbuf, self.out = net, full, sib, xrecv, zrecv, out
        self.sib_send, self.x_send, self.z_send, self.sib_sem, self.x_sem, self.z_sem = sems
        self.narrow, self.joined = narrow, joined
        self.nd = 1 if narrow else net.nd
        self.levels = 0 if narrow else net.levels

    def home(self, mask):
        return 0 if self.narrow else self.net.flips(mask)

    def start(self):
        n = self.net
        for mask in range(self.nd - 1, -1, -1):
            mirrored = sum(1 << (self.levels - 1 - k) for k in range(self.levels) if (mask >> k) & 1)
            d = self.home(mirrored)
            rows = pl.ds(d * n.nb, n.nb)
            if self.joined:
                remote(self.sib.at[rows], self.full.at[rows, n.c], self.sib_send, self.sib_sem.at[mask], n.sibling).start()
            else:
                for blk in range(n.nb):
                    at = d * n.nb + blk
                    remote(
                        self.full.at[at * n.nc + n.nc - 1 - n.c], self.sib.at[at], self.sib_send, self.sib_sem.at[mask], n.sibling
                    ).start()

    def wait_sibling(self, mask):
        n = self.net
        some = self.sib.at[pl.ds(0, n.nb)]
        pltpu.make_async_copy(some, some, self.sib_sem.at[mask]).wait()

    def x_at(self, k, mask, blk):
        return ((1 << k) - 1 + mask) * self.net.nb + blk

    def reduce(self, mask, e):
        n = self.net
        if e == n.nb - 1:
            self.wait_sibling(mask)
        blk = n.near(e)
        at = self.home(mask) * n.nb + blk
        place = self.full.at[at] if self.joined else self.full.at[at * n.nc + n.c]
        terms = [place] if self.joined else [place, self.sib.at[at]]
        for k in range(self.levels - 1, -1, -1):
            if mask < (1 << k):
                i = self.x_at(k, mask, blk)
                got = self.xbuf.at[i]
                pltpu.make_async_copy(got, got, self.x_sem.at[i]).wait()
                terms.append(got)
        if mask:
            k = mask.bit_length() - 1
            add_up(terms, place)
            i = self.x_at(k, mask - (1 << k), blk)
            remote(place, self.xbuf.at[i], self.x_send, self.x_sem.at[i], n.across(k)).start()
            return

        def arrived(side, there):
            i = self.z_at(side, blk, n.b)
            got = self.zbuf.at[i]

            @pl.when(there)
            def _():
                pltpu.make_async_copy(got, got, self.z_sem.at[i]).wait()

            terms.append(got)

        if e == 0:
            arrived(0, n.b > 0)
            arrived(1, n.b < n.nb - 1)
            add_up(terms, self.out)
            return
        side = jnp.where(blk > n.b, 0, 1)
        arrived(side, jnp.where(blk > n.b, n.b, n.nb - 1 - n.b) > 0)
        add_up(terms, place)
        to = n.b + 1 - 2 * side
        i = self.z_at(side, blk, to)
        remote(place, self.zbuf.at[i], self.z_send, self.z_sem.at[i], (n.d, to, n.c)).start()

    def z_at(self, side, blk, owner):
        return blk + side * jnp.where(blk == owner, self.net.nb - blk, 0)

    def clear_edges(self):
        n = self.net

        def clear(i, carry):
            self.zbuf[i] = jnp.zeros(self.zbuf.shape[1:], self.zbuf.dtype)
            return carry

        @pl.when(n.b == 0)
        def _():
            lax.fori_loop(0, n.nb, clear, 0)

        @pl.when(n.b == n.nb - 1)
        def _():
            lax.fori_loop(0, n.nb - 1, clear, 0)
            clear(n.nb, 0)

    def drain(self):
        n = self.net
        some = self.sib.at[pl.ds(0, self.nd * n.nb)]
        pltpu.make_async_copy(some, some, self.sib_send).wait()
        if not self.narrow:
            some = self.xbuf.at[pl.ds(0, (n.nd - 1) * n.nb)]
            pltpu.make_async_copy(some, some, self.x_send).wait()
        some = self.zbuf.at[pl.ds(0, n.nb - 1)]
        pltpu.make_async_copy(some, some, self.z_send).wait()


def add_up(terms, to):
    shape = to.shape
    rows = shape[-2]
    step = rows
    while step % 2 == 0 and step > 32:
        step //= 2
    lead = [()] if len(shape) == 2 else [(g,) for g in range(shape[0])]
    for g in lead:
        for r in range(0, rows, step):
            at = g + (slice(r, r + step),)
            total = terms[0][at].astype(F32)
            for t in terms[1:]:
                total = total + t[at].astype(F32)
            to[at] = total.astype(to.dtype)


class AllSum:
    def __init__(self, net, value, got, send, recv):
        self.net, self.value, self.got, self.send, self.recv = net, value, got, send, recv

    def copy(self, stage, dev, src, slot):
        return remote(self.value.at[src], self.got.at[slot], self.send.at[slot], self.recv.at[slot], dev)

    def stages(self):
        n = self.net
        devs = [n.sibling] + [n.across(k) for k in range(n.levels)]
        steps = []
        for i, dev in enumerate(devs):
            steps.append(functools.partial(self.one, i, dev))
        steps.append(self.line_start)
        steps.append(self.line_end)
        return [lambda: self.copy(0, devs[0], 0, 0).start()] + steps

    def one(self, i, dev):
        n = self.net
        self.copy(i, dev, i, i).wait()
        self.value[i + 1] = self.value[i] + self.got[i]
        if i + 1 <= n.levels:
            self.copy(i + 1, n.across(i), i + 1, i + 1).start()

    def line_copy(self, u):
        n = self.net
        return self.copy(None, (n.d, (n.b + u) % n.nb, n.c), n.levels + 1, n.levels + u)

    def line_start(self):
        for u in range(1, self.net.nb):
            self.line_copy(u).start()

    def line_end(self):
        n = self.net
        for u in range(1, n.nb):
            self.line_copy(u).wait()
        total = self.value[n.levels + 1]
        for u in range(1, n.nb):
            total = total + self.got[n.levels + u]
        self.value[0] = total


def scatter_sems(n_pieces, nd, nb):
    return [
        pltpu.SemaphoreType.DMA((n_pieces, 3)),
        pltpu.SemaphoreType.DMA((n_pieces, nd)),
        pltpu.SemaphoreType.DMA((n_pieces, (nd - 1) * nb)),
        pltpu.SemaphoreType.DMA((n_pieces, nb + 1)),
    ]


def dot(a, b, dims=((1,), (0,))):
    return lax.dot_general(a, b, (dims, ((), ())), preferred_element_type=F32)


def mask_lanes(seg_row, count):
    lanes = lax.broadcasted_iota(jnp.int32, (128, count), 0)
    return jnp.transpose(jnp.where(lanes == seg_row, -1.0, 0.0).astype(F32), (1, 0))


def project(tok, w, bias, seg, qaug, kaug, v_scr, q_scr, blk, c, qlen, width):
    total = tok.shape[0]
    pairs = width // 128
    step = min(512, total)
    d_model = tok.shape[1]

    def cols(part):
        return w[:, pl.ds(pl.multiple_of((part * 2 + c) * width, 128), width)]

    wk, wv = cols(1), cols(2)
    bias_v = bias[1:2, :]

    def rows(i, carry):
        at = pl.ds(pl.multiple_of(i * step, step), step)
        piece = tok[at, :]
        keys = dot(piece, wk).astype(BF16)
        vals = (dot(piece, wv) + bias_v).astype(BF16)
        seg_row = seg[:, at]
        lanes = mask_lanes(seg_row, step).astype(BF16)
        for p in range(pairs):
            kaug[p, at, 0:128] = keys[:, p * 128:(p + 1) * 128]
            kaug[p, at, 128:256] = lanes
            v_scr[p, at, :] = vals[:, p * 128:(p + 1) * 128]
        return carry

    lax.fori_loop(0, total // step, rows, 0)
    mine = pl.ds(pl.multiple_of(blk * qlen, qlen), qlen)
    query = (dot(tok[mine, :], cols(0)) + bias[0:1, :]).astype(BF16)
    q_scr[...] = query
    seg_q = seg[:, mine]
    lane = lax.broadcasted_iota(jnp.int32, (qlen, 128), 1)
    feat = jnp.where(lane < 8, BIG * (1.0 + mask_lanes(seg_q, qlen)), 0.0).astype(BF16)
    for p in range(pairs):
        q_pair = query[:, p * 128:(p + 1) * 128].astype(F32) * HD**-0.5
        for half in range(2):
            keep = (lane >= 64) if half else (lane < 64)
            qaug[2 * p + half, :, 0:128] = jnp.where(keep, q_pair, 0.0).astype(BF16)
            qaug[2 * p + half, :, 128:256] = feat


def attend_chunk(i, qaug, kaug, v_scr, o_scr, lse_scr, chunk, per_head):
    h = i // per_head
    at = pl.ds(pl.multiple_of((i % per_head) * chunk, chunk), chunk)
    s = dot(qaug[h, at, :], kaug[h // 2], ((1,), (1,)))
    top = jnp.max(s, axis=-1, keepdims=True)
    p = jnp.exp(s - top)
    total = jnp.sum(p, axis=-1, keepdims=True)
    o = dot(p.astype(BF16), v_scr[h // 2])
    o_scr[h, at, :] = o / total
    lse_scr[h, at, :] = jnp.broadcast_to(top + jnp.log(total), (chunk, 128))


def join_heads(o_scr, p):
    lane = lax.broadcasted_iota(jnp.int32, o_scr.shape[1:], 1)
    return jnp.where(lane < 64, o_scr[2 * p], o_scr[2 * p + 1])


def fwd_kernel(tok, w, bias, seg, ctx, q_out, kaug, v_scr, qaug, lse_scr, o_scr, chunk=256):
    blk, c = lax.axis_index("blk"), lax.axis_index("head")
    qlen, width = ctx.shape
    project(tok, w, bias, seg, qaug, kaug, v_scr, q_out, blk, c, qlen, width)
    per_head = qlen // chunk

    def step(i, carry):
        attend_chunk(i, qaug, kaug, v_scr, o_scr, lse_scr, chunk, per_head)
        return carry

    lax.fori_loop(0, (width // HD) * per_head, step, 0)
    for p in range(width // 128):
        ctx[:, p * 128:(p + 1) * 128] = join_heads(o_scr, p).astype(BF16)


def split3(x):
    hi = x.astype(BF16)
    mid = (x - hi.astype(F32)).astype(BF16)
    low = (x - hi.astype(F32) - mid.astype(F32)).astype(BF16)
    return hi, mid, low


def bwd_head(h, pair, qaug, kaug, v_scr, do_m, lse_row, p_scr, dp_scr, dk_scr, dv_scr, dq_scr, kc, qc, nq):
    total = kaug.shape[1]
    for j in range(nq):
        at = pl.ds(j * qc, qc)
        lse = lse_row[h, 0:1, at]
        q_part = qaug[h, at, :]
        do_part = do_m[h, at, :]

        def first(i, delta):
            rows = pl.ds(pl.multiple_of(i * kc, kc), kc)
            s = dot(kaug[pair, rows, :], q_part, ((1,), (1,)))
            p = jnp.exp(s - lse)
            dp = dot(v_scr[pair, rows, :], do_part, ((1,), (1,)))
            p_scr[rows, :] = p
            dp_scr[rows, :] = dp
            dv = dot(p.astype(BF16), do_part)
            if j:
                dv = dv + dv_scr[h, rows, :].astype(F32)
            dv_scr[h, rows, :] = dv.astype(dv_scr.dtype)
            return delta + jnp.sum((p * dp).reshape(kc // 8, 8, qc), axis=0)

        delta = lax.fori_loop(0, total // kc, first, jnp.zeros((8, qc), F32))
        delta = jnp.sum(delta, axis=0, keepdims=True)
        q_low = q_part[:, 0:128]

        def second(i, dq):
            rows = pl.ds(pl.multiple_of(i * kc, kc), kc)
            ds = (p_scr[rows, :] * (dp_scr[rows, :] - delta)).astype(BF16)
            dk = dot(ds, q_low)
            if j:
                dk = dk + dk_scr[h, rows, :].astype(F32)
            dk_scr[h, rows, :] = dk.astype(dk_scr.dtype)
            return dq + dot(kaug[pair, rows, 0:128], ds, ((0,), (0,)))

        dq = lax.fori_loop(0, total // kc, second, jnp.zeros((128, qc), F32))
        dq_scr[h, at, :] = jnp.transpose(dq, (1, 0))


VMEM = pl.BlockSpec(memory_space=pltpu.VMEM)
HBM = pl.BlockSpec(memory_space=pl.ANY)


def params(limit, collective=None):
    more = {} if collective is None else dict(collective_id=collective, has_side_effects=True)
    return pltpu.CompilerParams(vmem_limit_bytes=limit << 20, **more)


def gather_order(keys, narrow, nd, nb):
    events = []
    for p, (begin, dz, dx) in enumerate(keys):
        for e in range(nb):
            events.append((begin + e * dz, ("z", p, e)))
            if not narrow[p]:
                for mask in range(1, nd):
                    events.append((begin + e * dz + dx * mask.bit_length(), ("x", p, mask, e)))
    events.sort(key=lambda q: q[0])
    return [ev for _, ev in events]


def gather_all(shards, narrow, keys, nd, nb, nc):
    count = len(shards)

    def kernel(*refs):
        mine, full = refs[:count], refs[count:2 * count]
        four, recv, own_sem = refs[2 * count:]
        net = Net(nd, nb, nc)
        pieces = [
            Gather(net, mine[p], full[p], [four.at[p, i] for i in range(4)] + [recv.at[p]], narrow[p]) for p in range(count)
        ]
        net.barrier()
        for ev in gather_order(keys, narrow, nd, nb):
            if ev[0] == "z":
                pieces[ev[1]].z(ev[2])
            else:
                pieces[ev[1]].x(ev[2], ev[3])
        for piece in pieces:
            own = piece.own(own_sem)
            own.start()
            own.wait()
        for piece in pieces:
            piece.wait_sibling()
        for piece in pieces:
            piece.drain()

    outs = [
        jax.ShapeDtypeStruct(((nb * nc if thin else nd * nb * nc),) + s.shape, s.dtype) for s, thin in zip(shards, narrow)
    ]
    return pl.pallas_call(
        kernel,
        out_shape=outs,
        in_specs=[VMEM] * count,
        out_specs=[HBM] * count,
        scratch_shapes=gather_sems(count, nd, nb),
        compiler_params=params(56, 0),
    )(*shards)


def attend_forward(tok, w, bias, seg, qlen, width):
    total = tok.shape[0]
    heads = width // HD
    chunk = min(256, qlen)
    return pl.pallas_call(
        functools.partial(fwd_kernel, chunk=chunk),
        out_shape=[
            jax.ShapeDtypeStruct((qlen, width), BF16),
            jax.ShapeDtypeStruct((qlen, width), BF16),
            jax.ShapeDtypeStruct((width // 128, total, 256), BF16),
            jax.ShapeDtypeStruct((width // 128, total, 128), BF16),
            jax.ShapeDtypeStruct((heads, qlen, 256), BF16),
            jax.ShapeDtypeStruct((heads, qlen, 128), F32),
        ],
        in_specs=[VMEM] * 4,
        out_specs=[VMEM] * 6,
        scratch_shapes=[pltpu.VMEM((heads, qlen, 128), F32)],
        compiler_params=params(56),
    )(tok, w, bias, seg)


def pair_bwd_kernel(qaug, kaug, v_scr, lse_b, gctx, dk, dv, dq, p_scr, dp_scr, do_m, lse_row, dk_scr, dv_scr, dq_scr, kc, qc):
    qlen = qaug.shape[1]
    lane = lax.broadcasted_iota(jnp.int32, (qlen, 128), 1)
    for h in range(2):
        keep = (lane >= 64) if h else (lane < 64)
        piece = gctx[...]
        do_m[h] = jnp.where(keep, piece, jnp.zeros_like(piece))
        lse_row[h] = jnp.transpose(lse_b[h], (1, 0))[0:8, :]

    def head(h, carry):
        bwd_head(h, 0, qaug, kaug, v_scr, do_m, lse_row, p_scr, dp_scr, dk_scr, dv_scr, dq_scr, kc, qc, qlen // qc)
        return carry

    lax.fori_loop(0, 2, head, 0)
    dk[...] = pair_of(dk_scr).astype(BF16)
    dv[...] = pair_of(dv_scr).astype(BF16)
    dq[...] = (pair_of(dq_scr) * HD**-0.5).astype(BF16)


def pair_of(scr):
    first, second = scr[0], scr[1]
    lane = lax.broadcasted_iota(jnp.int32, first.shape, 1)
    return jnp.where(lane < 64, first, second)


def finish_kernel(tok, dk, dv, tok_mine, dq, w, dtok, dw, dbias, own):
    i, c = pl.program_id(0), lax.axis_index("head")
    blk = lax.axis_index("blk")
    step, width = dk.shape
    qlen = dq.shape[0]

    def cols(part):
        return w[:, pl.ds(pl.multiple_of((part * 2 + c) * width, 128), width)]

    piece, grad_k, grad_v = tok[...], dk[...], dv[...]

    @pl.when(i == 0)
    def _():
        dw[:, 0:width] = dot(tok_mine[...], dq[...], ((0,), (0,)))
        dw[:, width:3 * width] = jnp.zeros((dw.shape[0], 2 * width), F32)
        dbias[0:1, :] = jnp.sum(dq[...].astype(F32), axis=0, keepdims=True)
        dbias[1:2, :] = jnp.zeros((1, width), F32)
        own[...] = dot(dq[...], cols(0), ((1,), (1,)))

    dw[:, width:2 * width] += dot(piece, grad_k, ((0,), (0,)))
    dw[:, 2 * width:3 * width] += dot(piece, grad_v, ((0,), (0,)))
    dbias[1:2, :] += jnp.sum(grad_v.astype(F32), axis=0, keepdims=True)
    grad = dot(grad_k, cols(1), ((1,), (1,))) + dot(grad_v, cols(2), ((1,), (1,)))
    per = qlen // step
    mine = i // per == blk
    at = pl.ds(pl.multiple_of((i % per) * step, step), step)
    dtok[...] = (grad + jnp.where(mine, own[at, :], 0.0)).astype(BF16)


def attend_backward(tok, tok_mine, w, qaug, kaug, v_scr, lse_b, gctx):
    heads, qlen, _ = qaug.shape
    total, d_model = tok.shape
    width = heads * HD
    qc = qlen
    while total * qc > 2048 * 512:
        qc //= 2
    kc = min(512, total)
    pair3 = lambda p: (p, 0, 0)
    lanes = lambda p: (0, p)
    dk, dv, dq = pl.pallas_call(
        functools.partial(pair_bwd_kernel, kc=kc, qc=qc),
        grid=(heads // 2,),
        out_shape=[
            jax.ShapeDtypeStruct((total, width), BF16),
            jax.ShapeDtypeStruct((total, width), BF16),
            jax.ShapeDtypeStruct((qlen, width), BF16),
        ],
        in_specs=[
            pl.BlockSpec((2, qlen, 256), pair3),
            pl.BlockSpec((1, total, 256), pair3),
            pl.BlockSpec((1, total, 128), pair3),
            pl.BlockSpec((2, qlen, 128), pair3),
            pl.BlockSpec((qlen, 128), lanes),
        ],
        out_specs=[pl.BlockSpec((total, 128), lanes)] * 2 + [pl.BlockSpec((qlen, 128), lanes)],
        scratch_shapes=[
            pltpu.VMEM((total, qc), F32),
            pltpu.VMEM((total, qc), F32),
            pltpu.VMEM((2, qlen, 128), BF16),
            pltpu.VMEM((2, 8, qlen), F32),
            pltpu.VMEM((2, total, 128), BF16),
            pltpu.VMEM((2, total, 128), BF16),
            pltpu.VMEM((2, qlen, 128), F32),
        ],
        compiler_params=params(56),
    )(qaug, kaug, v_scr, lse_b, gctx)
    step = min(512, qlen)
    whole = lambda i: (0, 0)
    rows = lambda i: (i, 0)
    return pl.pallas_call(
        finish_kernel,
        grid=(total // step,),
        out_shape=[
            jax.ShapeDtypeStruct((total, d_model), BF16),
            jax.ShapeDtypeStruct((d_model, 3 * width), F32),
            jax.ShapeDtypeStruct((2, width), F32),
        ],
        in_specs=[
            pl.BlockSpec((step, d_model), rows),
            pl.BlockSpec((step, width), rows),
            pl.BlockSpec((step, width), rows),
            pl.BlockSpec((qlen, d_model), whole),
            pl.BlockSpec((qlen, width), whole),
            pl.BlockSpec((d_model, w.shape[1]), whole),
        ],
        out_specs=[
            pl.BlockSpec((step, d_model), rows),
            pl.BlockSpec((d_model, 3 * width), whole),
            pl.BlockSpec((2, width), whole),
        ],
        scratch_shapes=[pltpu.VMEM((qlen, d_model), F32)],
        compiler_params=params(56),
    )(tok, dk, dv, tok_mine, dq, w)


def scatter_all(arrays, narrow, joined, small, nd, nb, nc):
    count = len(arrays)
    flat = []
    for a, j in zip(arrays, joined):
        flat += list(a) if j else [a]
    n_in = len(flat) + 1

    def kernel(*refs):
        ins, small_in = list(refs[:n_in - 1]), refs[n_in - 1]
        outs, small_out = refs[n_in:n_in + count], refs[n_in + count]
        rest = list(refs[n_in + count + 1:])
        net = Net(nd, nb, nc)
        s3, sib_sem, x_sem, z_sem, sum_send, sum_recv = rest[-6:]
        value, got = rest[-8:-6]
        bufs = rest[:-8]
        pieces = []
        for p in range(count):
            first = ins.pop(0)
            sib = ins.pop(0) if joined[p] else bufs.pop(0)
            xbuf = None if narrow[p] else bufs.pop(0)
            zbuf = bufs.pop(0)
            sems = [s3.at[p, i] for i in range(3)] + [sib_sem.at[p], x_sem.at[p], z_sem.at[p]]
            pieces.append(Scatter(net, first, sib, xbuf, zbuf, outs[p], sems, narrow[p], joined[p]))
        sums = AllSum(net, value, got, sum_send, sum_recv)
        for piece in pieces:
            piece.clear_edges()
        value[0] = small_in[...]
        net.barrier()
        events = [(0.0, s) for s in [pieces[0].start]]
        for p, piece in enumerate(pieces):
            t = 0.5 * p
            events.append((t - 0.4, piece.start) if p else (t - 1, lambda: None))
            for mask in range(piece.nd - 1, -1, -1):
                for e in range(nb - 1, -1, -1):
                    when = t + (piece.levels - mask.bit_length()) + 0.01 * (nb - 1 - e)
                    events.append((when, functools.partial(piece.reduce, mask, e)))
        for i, s in enumerate(sums.stages()):
            events.append((0.3 * i, s))
        events.sort(key=lambda q: q[0])
        for _, ev in events:
            ev()
        small_out[...] = value[0]
        for piece in pieces:
            piece.drain()

    outs, scratch = [], []
    for a, thin, j in zip(arrays, narrow, joined):
        full = a[0] if j else a
        block = full.shape[1:]
        outs.append(jax.ShapeDtypeStruct(block, F32))
        n_dp = 1 if thin else nd
        if not j:
            scratch.append(pltpu.VMEM((n_dp * nb,) + block, BF16))
        if not thin:
            scratch.append(pltpu.VMEM(((nd - 1) * nb,) + block, BF16))
        scratch.append(pltpu.VMEM((nb + 1,) + block, BF16))
    levels = nd.bit_length() - 1
    scratch += [pltpu.VMEM((levels + 2,) + small.shape, F32), pltpu.VMEM((levels + nb,) + small.shape, F32)]
    scratch += scatter_sems(count, nd, nb)
    scratch += [pltpu.SemaphoreType.DMA((levels + nb,))] * 2
    outs.append(jax.ShapeDtypeStruct(small.shape, F32))
    return pl.pallas_call(
        kernel,
        out_shape=outs,
        in_specs=[VMEM] * n_in,
        out_specs=[VMEM] * (count + 1),
        scratch_shapes=scratch,
        compiler_params=params(60, 1),
    )(*flat, small)


def layer_norm(hidden, gain, shift):
    centered = hidden - jnp.mean(hidden, axis=-1, keepdims=True)
    variance = jnp.mean(centered * centered, axis=-1, keepdims=True)
    return centered * lax.rsqrt(variance + 1e-12) * gain + shift


def gelu_exact(values):
    return jax.nn.gelu(values, approximate=False)


def matmul(left, right):
    return jnp.dot(left, right, preferred_element_type=F32)


def matmul_left_t(left, right):
    return dot(left, right, ((0,), (0,)))


def matmul_right_t(left, right):
    return dot(left, right, ((1,), (1,)))


def body(
    tokens,
    segment,
    w_qkv,
    bias_query,
    bias_value,
    w_out,
    bias_out,
    gain_attn,
    shift_attn,
    w_in,
    bias_in,
    w_down,
    bias_down,
    gain_ffn,
    shift_ffn,
    cotangent,
):
    nd, nb, nc = lax.axis_size("dp"), lax.axis_size("blk"), lax.axis_size("head")
    n_dev = nd * nb * nc
    d_idx, b_idx, c_idx = lax.axis_index("dp"), lax.axis_index("blk"), lax.axis_index("head")
    me = (d_idx * nb + b_idx) * nc + c_idx
    seqs, rows, width = tokens.shape
    ff = w_in.shape[1]
    half_w = width // nc
    qlen = nc * rows
    r = w_qkv.shape[0]
    r_ff = w_down.shape[0]
    vectors = [bias_query, bias_value, bias_out, gain_attn, shift_attn, bias_down, gain_ffn, shift_ffn]
    packed = jnp.concatenate(vectors + [bias_in])
    used = packed.shape[0]
    lanes = -(-used // 128) * 128
    packed = jnp.broadcast_to(jnp.pad(packed, (0, lanes - used))[None], (8, lanes))
    flat_in = tokens.reshape(rows, width)
    n4 = 4
    parts = [flat_in[i * (rows // n4):(i + 1) * (rows // n4)] for i in range(n4)]
    shards = [packed, w_qkv] + parts + [w_out, w_in, w_down]
    narrow = [False, False] + [True] * n4 + [False] * 3
    keys = [(-1, 3, 3), (0, 3, 3), (7, 9, 0), (10, 9, 0), (13, 9, 0), (16, 9, 0), (2, 4, 4), (9, 6, 5), (22, 6, 5)]
    small, g_qkv, t0, t1, t2, t3, g_out, g_in, g_down = gather_all(shards, narrow, keys, nd, nb, nc)
    full_small = small[:, 0, :used]
    vecs = full_small[:, :8 * r].reshape(n_dev, 8, r).transpose(1, 0, 2).reshape(8, width).astype(F32)
    full_bin = full_small[:, 8 * r:].reshape(ff).astype(F32)
    bq, bv, bout, gain_one, shift_one, bdown, gain_two, shift_two = (vecs[i] for i in range(8))
    full_qkv = g_qkv.reshape(width, 3 * width)
    full_wout = g_out.reshape(width, width)
    full_win = g_in.reshape(width, ff)
    full_wdown = g_down.reshape(ff, width)
    tok_all = jnp.stack([t0, t1, t2, t3], axis=1).reshape(nb * qlen, width)
    my_bias = lax.dynamic_slice(vecs, (0, c_idx * half_w), (2, half_w))
    ctx, _, kaug, v_scr, qaug, lse_b = attend_forward(tok_all, full_qkv, my_bias, segment, qlen, half_w)
    context_low = ctx.reshape(seqs, qlen, 1, half_w)
    back_tokens = lax.all_to_all(context_low, "head", split_axis=1, concat_axis=2, tiled=True)
    context_flat = back_tokens.reshape(rows, width)
    attn_out = matmul(context_flat, full_wout) + bout
    resid_one = flat_in.astype(F32) + attn_out
    normed_one, norm_one_pull = jax.vjp(layer_norm, resid_one, gain_one, shift_one)
    normed_low = normed_one.astype(BF16)
    pre_act = matmul(normed_low, full_win) + full_bin
    activated, gelu_pull = jax.vjp(gelu_exact, pre_act)
    act_low = activated.astype(BF16)
    ffn_out = matmul(act_low, full_wdown) + bdown
    resid_two = normed_one + ffn_out
    result, norm_two_pull = jax.vjp(layer_norm, resid_two, gain_two, shift_two)
    output = result.astype(BF16).reshape(seqs, rows, width)
    grad_result = cotangent.reshape(rows, width).astype(F32)
    grad_resid_two, grad_gain_two, grad_shift_two = norm_two_pull(grad_result)
    grad_ffn = grad_resid_two.astype(BF16)
    grad_bias_down = jnp.sum(grad_ffn.astype(F32), axis=0)
    grad_w_down = matmul_left_t(act_low, grad_ffn)
    grad_act = matmul_right_t(grad_ffn, full_wdown)
    (grad_pre,) = gelu_pull(grad_act)
    grad_pre_low = grad_pre.astype(BF16)
    grad_bias_in = jnp.sum(grad_pre_low.astype(F32), axis=0)
    grad_w_in = matmul_left_t(normed_low, grad_pre_low)
    grad_normed = grad_resid_two + matmul_right_t(grad_pre_low, full_win)
    grad_resid_one, grad_gain_one, grad_shift_one = norm_one_pull(grad_normed)
    grad_attn = grad_resid_one.astype(BF16)
    grad_bias_out = jnp.sum(grad_attn.astype(F32), axis=0)
    grad_w_out = matmul_left_t(context_flat, grad_attn)
    grad_context = matmul_right_t(grad_attn, full_wout).astype(BF16)
    grad_headed = lax.all_to_all(
        grad_context.reshape(seqs, rows, nc, half_w), "head", split_axis=2, concat_axis=1, tiled=True
    )
    gctx = grad_headed.reshape(qlen, half_w)
    tok_mine = lax.dynamic_slice(tok_all, (b_idx * qlen, 0), (qlen, width))
    dtok, dw, dbias = attend_backward(tok_all, tok_mine, full_qkv, qaug, kaug, v_scr, lse_b, gctx)
    dw = dw.astype(BF16).reshape(nd * nb, nc, r, 3 * half_w)
    ours = lax.dynamic_index_in_dim(dw, c_idx, 1, keepdims=False)
    theirs = lax.dynamic_index_in_dim(dw, 1 - c_idx, 1, keepdims=False)
    joined_full = jnp.stack([ours, ours], axis=1)
    my_rows = lax.dynamic_update_slice(jnp.zeros((2, width), F32), dbias, (0, c_idx * half_w))
    sums = jnp.concatenate(
        [
            my_rows,
            jnp.stack([grad_bias_out, grad_gain_one, grad_shift_one, grad_bias_down, grad_gain_two, grad_shift_two]),
            grad_bias_in.reshape(ff // width, width),
        ]
    )
    sums = jnp.pad(sums, ((0, -sums.shape[0] % 8), (0, 0)))
    o_down, o_in, o_out, o_tok, o_qkv, total = scatter_all(
        [
            grad_w_down.astype(BF16).reshape(n_dev, r_ff, width),
            grad_w_in.astype(BF16).reshape(n_dev, r, ff),
            grad_w_out.astype(BF16).reshape(n_dev, r, width),
            dtok.reshape(nb * nc, rows, width),
            (joined_full, theirs),
        ],
        [False, False, False, True, False],
        [False, False, False, False, True],
        sums,
        nd,
        nb,
        nc,
    )
    grad_tokens = (grad_resid_one + o_tok).reshape(seqs, rows, width)
    o_qkv = o_qkv.reshape(2, r, 3, half_w).transpose(1, 2, 0, 3).reshape(r, 3 * width)
    mine = lax.dynamic_slice(total, (0, me * r), (8, r))
    mine_in = lax.dynamic_slice(total[8:8 + ff // width].reshape(ff), (me * r_ff,), (r_ff,))
    g_bq, g_bv, g_bo, g_g1, g_s1, g_bd, g_g2, g_s2 = (mine[i] for i in range(8))
    return (
        output,
        grad_tokens,
        o_qkv,
        g_bq,
        g_bv,
        o_out,
        g_bo,
        g_g1,
        g_s1,
        o_in,
        mine_in,
        o_down,
        g_bd,
        g_g2,
        g_s2,
    )


def solution(mesh):
    weight, vector = P(("dp", "blk", "head"), None), P(("dp", "blk", "head"))
    token = P("dp", ("blk", "head"), None)
    return jax.shard_map(
        body,
        mesh=mesh,
        in_specs=(
            token,
            P("dp", None),
            weight,
            vector,
            vector,
            weight,
            vector,
            vector,
            vector,
            weight,
            vector,
            weight,
            vector,
            vector,
            vector,
            token,
        ),
        out_specs=(
            token,
            token,
            weight,
            vector,
            vector,
            weight,
            vector,
            vector,
            vector,
            weight,
            vector,
            weight,
            vector,
            vector,
            vector,
        ),
        check_vma=False,
    )
```

time: 1040 us -> 373 us (0.36)
  waiting for transfers between devices: 632 us -> 1.26 us
  Pallas kernels: 0 us -> 279 us
  matrix products: 150 us -> 37.1 us
  blocking collectives: 101 us -> 0 us
  local copies, waits for them, and re-layouts: 72.9 us -> 31 us
  loops' own time: 23.9 us -> 0 us
  other arithmetic: 34.9 us -> 15.4 us
  between operations: 15.1 us -> 1.13 us
    reduce_scatter x5 -> x0, waiting for transfers between devices: 369 us -> none  [the longest x1 142 us: body(): lax.psum_scatter(grad_w_in, ('dp', 'blk', 'head'), scatter_dimension=0, t...]
    pallas_call x0 -> x5, Pallas kernels: none -> 279 us  [the longest x1 126 us: scatter_all(): pl.pallas_call(kernel, out_shape=outs, in_specs=[VMEM] * n_in, out_specs=...]
    all_gather x6 -> x0, waiting for transfers between devices: 134 us -> none  [the longest x1 53.8 us: body(): lax.all_gather(w_down, ('dp', 'blk', 'head'), axis=0, tiled=True)]
    unnamed x13 -> x0, waiting for transfers between devices: 129 us -> none
    dot_general x48 -> x9, matrix products: 150 us -> 37.1 us  [the longest x6 20.8 us: dot(): return lax.dot_general(a, b, (dims, ((), ())), preferred_element_type=F32)]
    unnamed x2 -> x0, blocking collectives: 82.7 us -> none
    unnamed x107 -> x52, local copies, waits for them, and re-layouts: 34 us -> 4.85 us
    another operation x3 -> x0, loops' own time: 23.9 us -> none  [the longest x2 16 us: run_blocks(): lax.scan(fold_step, state, tuple(stacks) + (jnp.arange(count, dtype=jnp.i...]
  transfers between devices with their start and end apart: 12 -> 2, of which waited for: 10 -> 1; matrix products, arithmetic and copies ran while one was open for 16% -> 4% of each run, Pallas kernels for 0% -> 0%
where the time goes in v1:
time: 373 us; the launch traced here: 372 us
  Pallas kernels  279 us (75%)
  matrix products  37.1 us (10%)
  local copies, waits for them, and re-layouts  31 us (8%)
  other arithmetic  15.4 us (4%)
  starting transfers between devices  7.15 us (2%)
    pallas_call x1, Pallas kernels, scatter_all(): pl.pallas_call(kernel, out_shape=outs, in_specs=[VMEM] * n_in, out_specs=...  126 us
    pallas_call x1, Pallas kernels, gather_all(): pl.pallas_call(kernel, out_shape=outs, in_specs=[VMEM] * count, out_specs...  87.1 us
    pallas_call x1, Pallas kernels, attend_backward(): pl.pallas_call(functools.partial(pair_bwd_kernel, kc=kc, qc=qc), grid=(he...  29.4 us
    pallas_call x1, Pallas kernels, attend_forward(): pl.pallas_call(functools.partial(fwd_kernel, chunk=chunk), out_shape=[jax...  23.6 us
    dot_general x6, matrix products, dot(): return lax.dot_general(a, b, (dims, ((), ())), preferred_element_type=F32)  20.8 us
    dot_general x3, matrix products, matmul(): return jnp.dot(left, right, preferred_element_type=F32)  16.3 us
    pallas_call x1, Pallas kernels, attend_backward(): pl.pallas_call(finish_kernel, grid=(total // step,), out_shape=[jax.Shape...  13.8 us
  transfers between devices with their start and end apart: 2, of which 1 were waited for; matrix products, arithmetic and copies ran while one was open for 4% of the time, Pallas kernels for 0%

profile of v1, /device:TPU:0, one launch (start us, length us, event | category | flops | bytes accessed | tf_op | source)
XLA Modules:
  0.0 372.5 jit_solution(16982703707946069223)
XLA Ops:
  0.6 1.8 slice_bitcast_fusion
  2.4 6.1 %concatenate.6 = bf16[288]{0:T(512)(128)(2,1)S(1)} concatenate(bf16[24]{0:T(256)(128)(2,1)} %param.19, bf16[24]{0:T(256)(128)(2,1)} %param.20, bf16[24]{0:T(256)(128)(2,1)} %param.22, bf16[24]{0:T(256)(128)(2,1)} %param.23, bf16[24]{0:T(256)(128)(2,1)} %param.24, bf16[24]{0:T(256)(128)(2,1)} %param.28, bf16[24]{0:T(256)(128)(2,1)} %param.29, bf16[24]{0:T(256)(128)(2,1)} %param.30, ...), dimensions={0} | concatenate | bytes 1152 | tf_op jit(solution)/shard_map/concatenate | solution.py:771
  8.5 0.6 broadcast_in_dim.12.refs_0_
  9.1 87.1 %shard_map.271 = (bf16[32,8,384]{2,1,0:T(8,128)(2,1)}, bf16[32,24,2304]{2,1,0:T(8,128)(2,1)}, bf16[8,64,768]{2,1,0:T(8,128)(2,1)}, bf16[8,64,768]{2,1,0:T(8,128)...) custom-call(bf16[8,384]{1,0:T(8,128)(2,1)} %broadcast_in_dim.12.refs, ...), custom_call_target="tpu_custom_call" | custom-call | tf_op jit(solution)/shard_map/pallas_call | solution.py:498
  96.2 2.0 pad_maximum_fusion
  98.3 2.0 copy.49
  100.3 1.0 slice.92
  101.5 0.6 constant_dynamic-slice_fusion.3.bias
  102.1 23.6 %shard_map.272 = (bf16[512,384]{1,0:T(8,128)(2,1)}, bf16[512,384]{1,0:T(8,128)(2,1)}, bf16[3,2048,256]{2,1,0:T(8,128)(2,1)}, bf16[3,2048,128]{2,1,0:T(8,128)(2,1...) custom-call(bf16[2048,768]{1,0:T(8,128)(2,1)} %bitcast.99, bf16[768,2304]{1,0:T(8,128)(2,1)} %bitcast.104, ...), custom_call_target="tpu_custom_call" | custom-call | tf_op jit(solution)/shard_map/pallas_call | solution.py:512
  125.7 1.6 copy.60
  127.8 3.0 reduce.25
  130.9 0.9 reshape.254
  131.7 3.5 all-to-all-start
  135.6 1.3 all-to-all-done
  137.6 0.6 fusion.23
  138.7 11.3 %multiply_convert_fusion = (bf16[256,3072]{1,0:T(8,128)(2,1)S(1)}, f32[256,3072]{1,0:T(8,128)}, f32[256,3072]{1,0:T(8,128)}) fusion(f32[3072]{0:T(1024)S(1)} %reshape.220, bf16[768,3072]{1,0:T(8,128)(2,1)} %bitcast.127, f32[256,768]{1,0:T(8,128)S(1)} %get-tuple-element.106, f32[768]{0:T(1024)S(1)} %add.117, f32[768]{0:T(1024)S(1)} %mul.163, ...), kind=kOutput, calls=%fused_computation.8 | convolution fusion | flops 1260847104 | bytes 13389824 | tf_op jit(solution)/shard_map/dot_general | solution.py:731
  150.0 4.4 %fusion.24 = (f32[256]{0:T(256)S(1)}, f32[256,768]{1,0:T(8,128)S(1)}) fusion(f32[768]{0:T(1024)S(1)} %add.122, bf16[256,3072]{1,0:T(8,128)(2,1)S(1)} %get-tuple-element.88, bf16[3072,768]{1,0:T(8,128)(2,1)} %bitcast.131, f32[768]{0:T(1024)S(1)} %add.117, f32[768]{0:T(1024)S(1)} %mul.163, f32[256]{0:T(256)S(1)} %fusion.16, ...), kind=kOutput, calls=%fused_computation.93 | convolution fusion | flops 1209335552 | bytes 7876608 | tf_op jit(solution)/shard_map/dot_general | solution.py:731
  155.3 1.1 fusion.21
  156.4 0.7 convert_reduce_fusion.2
  157.2 6.9 %convert_reduce_fusion = (f32[3072]{0:T(1024)}, bf16[256,3072]{1,0:T(8,128)(2,1)S(1)}) fusion(f32[256,3072]{1,0:T(8,128)} %get-tuple-element.89, f32[256,3072]{1,0:T(8,128)} %get-tuple-element.107, bf16[256,768]{1,0:T(8,128)(2,1)S(1)} %get-tuple-element.81, bf16[3072,768]{1,0:T(8,128)(2,1)} %bitcast.132), kind=kOutput, calls=%fused_computation.6 | convolution fusion | flops 1220539392 | bytes 12988416 | tf_op jit(solution)/shard_map/dot_general | solution.py:324
  164.1 2.2 multiply_reduce_fusion
  166.7 0.7 convert_reduce_fusion.3
  167.6 1.3 convolution_convert_fusion.3
  168.8 1.1 reshape.206
  169.9 0.8 copy.53
  170.7 3.7 all-to-all-start.1
  174.4 0.7 convert_reduce_fusion.1
  175.1 1.5 convolution_convert_fusion.2
  176.6 5.4 %convolution_convert_fusion = bf16[768,3072]{1,0:T(8,128)(2,1)} fusion(bf16[256,3072]{1,0:T(8,128)(2,1)} %copy-done.7, f32[256,768]{1,0:T(8,128)S(1)} %get-tuple-element.106, f32[768]{0:T(1024)S(1)} %add.117, f32[768]{0:T(1024)S(1)} %mul.163, f32[256]{0:T(256)} %copy-done.14, f32[256]{0:T(256)S(1)} %broadcast_multiply_fusion.1), kind=kOutput, calls=%fused_computation | convolution fusion | flops 1211301888 | bytes 7086080 | tf_op jit(solution)/shard_map/dot_general | solution.py:324
  182.0 3.5 convolution_convert_fusion.1
  185.6 2.1 constant_dynamic-slice_fusion.2.tok_mine
  187.8 0.7 copy-done.5
  188.5 29.4 %shard_map.273 = (bf16[2048,384]{1,0:T(8,128)(2,1)}, bf16[2048,384]{1,0:T(8,128)(2,1)}, bf16[512,384]{1,0:T(8,128)(2,1)}) custom-call(bf16[6,512,256]{2,1,0:T(8,128)(2,1)} %get-tuple-element.51.qaug, bf16[3,2048,256]{2,1,0:T(8,128)(2,1)} %get-tuple-element.52.kaug, bf16[3,2048,128]{2,1,0:T(8,128)(2,1)} %get-tuple-element.53.v_scr, ...), custom_call_target="tpu_custom_call" | custom-call | tf_op jit(solution)/shard_map/pallas_call | solution.py:593
  218.0 13.8 %shard_map.274 = (bf16[2048,768]{1,0:T(8,128)(2,1)}, f32[768,1152]{1,0:T(8,128)}, f32[2,384]{1,0:T(2,128)}) custom-call(bf16[2048,768]{1,0:T(8,128)(2,1)} %bitcast.101, bf16[2048,384]{1,0:T(8,128)(2,1)} %get-tuple-element.55.dk, bf16[2048,384]{1,0:T(8,128)(2,1)} %get-tuple-element.56.dv, bf16[512,768]{1,0:T(8,128)(2,1)} %constant_dynamic-slice_fusion.2.tok_mine, ...), custom_call_target="tpu_custom_call" | custom-call | tf_op jit(solution)/shard_map/pallas_call | solution.py:623
  231.7 0.7 constant_dynamic-update-slice_fusion
  232.5 0.6 pad.9.refs_6_
  233.1 2.2 convert_element_type.100
  235.3 1.2 dynamic-slice_bitcast_fusion
  236.5 1.4 pad_maximum_fusion.1.refs_4_
  237.9 125.5 %shard_map.275 = (f32[96,768]{1,0:T(8,128)}, f32[24,3072]{1,0:T(8,128)}, f32[24,768]{1,0:T(8,128)}, f32[256,768]{1,0:T(8,128)}, f32[2,24,1152]{2,1,0:T(8,128)}, /*index=5*/f32[16,768]{1,0:T(8,128)}) custom-call(bf16[32,96,768]{2,1,0:T(8,128)(2,1)} %bitcast.102, bf16[32,24,3072]{2,1,0:T(8,128)(2,1)} %bitcast.103, bf16[32,24,768]{2,1,0:T(8,128)(2,1)} %bitcast.107, ...), custom_call_target="tpu_custom_call" | custom-call | tf_op jit(solution)/shard_map/pallas_call | solution.py:710
  363.5 2.2 add_bitcast_fusion
  365.7 1.0 reshape.216
  366.9 0.9 reshape.217
  367.7 0.7 slice.106
  368.5 0.8 constant_dynamic-slice_fusion
  370.4 0.6 copy.65
  371.0 0.7 copy.66
  371.8 0.7 copy.67
  (89 shorter events, 5.2 us)
Async XLA Ops:
  127.3 10.2 %copy-start = (bf16[32,24,768]{2,1,0:T(8,128)(2,1)S(1)}, bf16[32,24,768]{2,1,0:T(8,128)(2,1)}, u32[]{:S(2)}) copy-start(bf16[32,24,768]{2,1,0:T(8,128)(2,1)} %get-tuple-element.48) | copy-start | bytes 3538948
  127.3 10.2 %copy-start.6 = (bf16[1,256,768]{2,1,0:T(8,128)(2,1)S(1)}, bf16[1,256,768]{2,1,0:T(8,128)(2,1)}, u32[]{:S(2)}) copy-start(bf16[1,256,768]{2,1,0:T(8,128)(2,1)} %param.16) | copy-start | bytes 1179652
  131.7 5.1 %all-to-all-start = ((bf16[2,2,49152]{2,1,0:T(2,128)(2,1)}), bf16[2,2,49152]{2,1,0:T(2,128)(2,1)S(1)}, u32[]{:S(2)}, u32[]{:S(2)}) async-start(bf16[2,2,49152]{2,1,0:T(2,128)(2,1)} %reshape.254), calls=%async_computation | async-start | bytes 786432 | tf_op jit(solution)/shard_map/all_to_all | solution.py:794
  138.4 28.0 %copy-start.14 = (f32[256]{0:T(256)}, f32[256]{0:T(256)S(1)}, u32[]{:S(2)}) copy-start(f32[256]{0:T(256)S(1)} %fusion.16) | copy-start | bytes 3076
  150.0 4.4 %copy-start.3 = (bf16[256,3072]{1,0:T(8,128)(2,1)}, bf16[256,3072]{1,0:T(8,128)(2,1)S(1)}, u32[]{:S(2)}) copy-start(bf16[256,3072]{1,0:T(8,128)(2,1)S(1)} %get-tuple-element.88) | copy-start | bytes 4718596
  150.0 4.8 %copy-start.2 = (bf16[1,256,768]{2,1,0:T(8,128)(2,1)S(1)}, bf16[1,256,768]{2,1,0:T(8,128)(2,1)}, u32[]{:S(2)}) copy-start(bf16[1,256,768]{2,1,0:T(8,128)(2,1)} %param.31) | copy-start | bytes 1179652
  155.3 8.8 %slice-start = ((s8[4718592]{0:T(1024)(128)(4,1)}), s8[4194304]{0:T(1024)(128)(4,1)S(1)}, s32[]{:S(2)}) async-start(s8[4718592]{0:T(1024)(128)(4,1)} %bitcast.128), calls=%async_computation.2 | async-start | bytes 8388608
  157.2 6.9 %slice-start.1 = ((s8[4718592]{0:T(1024)(128)(4,1)}), s8[524288]{0:T(1024)(128)(4,1)S(1)}, s32[]{:S(2)}) async-start(s8[4718592]{0:T(1024)(128)(4,1)} %bitcast.128), calls=%async_computation.3 | async-start | bytes 1048576
  164.1 2.3 copy-start.7
  166.3 1.3 copy-start.1
  166.7 0.7 copy-start.16
  170.7 17.0 %all-to-all-start.1 = ((bf16[1,256,2,384]{3,1,0,2:T(8,128)(2,1)}), bf16[1,256,2,384]{3,1,0,2:T(8,128)(2,1)S(1)}, u32[]{:S(2)}, u32[]{:S(2)}) async-start(bf16[1,256,2,384]{3,1,0,2:T(8,128)(2,1)} %copy.53), calls=%async_computation.1 | async-start | bytes 786432 | tf_op jit(solution)/shard_map/all_to_all | solution.py:823
  176.6 5.4 %copy-start.4 = (bf16[256,3072]{1,0:T(8,128)(2,1)S(1)}, bf16[256,3072]{1,0:T(8,128)(2,1)}, u32[]{:S(2)}) copy-start(bf16[256,3072]{1,0:T(8,128)(2,1)} %copy-done.3) | copy-start | bytes 4718596
  182.0 5.7 %copy-start.13 = (f32[768]{0:T(1024)S(1)}, f32[768]{0:T(1024)}, u32[]{:S(2)}) copy-start(f32[768]{0:T(1024)} %get-tuple-element.82) | copy-start | bytes 9220
  182.0 5.7 %copy-start.19 = (f32[768]{0:T(1024)S(1)}, f32[768]{0:T(1024)}, u32[]{:S(2)}) copy-start(f32[768]{0:T(1024)} %get-tuple-element.67) | copy-start | bytes 9220
  182.0 5.7 %copy-start.18 = (f32[768]{0:T(1024)S(1)}, f32[768]{0:T(1024)}, u32[]{:S(2)}) copy-start(f32[768]{0:T(1024)} %get-tuple-element.71) | copy-start | bytes 9220
  182.0 5.7 %copy-start.15 = (f32[3072]{0:T(1024)S(1)}, f32[3072]{0:T(1024)}, u32[]{:S(2)}) copy-start(f32[3072]{0:T(1024)} %get-tuple-element.78) | copy-start | bytes 36868
  182.0 5.7 %copy-start.11 = (f32[768]{0:T(1024)S(1)}, f32[768]{0:T(1024)}, u32[]{:S(2)}) copy-start(f32[768]{0:T(1024)} %get-tuple-element.80) | copy-start | bytes 9220
  182.0 5.7 %copy-start.12 = (f32[768]{0:T(1024)S(1)}, f32[768]{0:T(1024)}, u32[]{:S(2)}) copy-start(f32[768]{0:T(1024)} %convert_reduce_fusion.1) | copy-start | bytes 9220
  187.8 0.8 copy-start.5
  237.9 125.6 %copy-start.17 = (f32[256]{0:T(256)S(1)}, f32[256]{0:T(256)}, u32[]{:S(2)}) copy-start(f32[256]{0:T(256)} %copy-done.16) | copy-start | bytes 3076
  363.4 7.0 %copy-start.10 = (f32[24,768]{1,0:T(8,128)S(1)}, f32[24,768]{1,0:T(8,128)}, u32[]{:S(2)}) copy-start(f32[24,768]{1,0:T(8,128)} %get-tuple-element.131) | copy-start | bytes 221188
  363.4 7.6 %copy-start.9 = (f32[24,3072]{1,0:T(8,128)S(1)}, f32[24,3072]{1,0:T(8,128)}, u32[]{:S(2)}) copy-start(f32[24,3072]{1,0:T(8,128)} %get-tuple-element.135) | copy-start | bytes 884740
  363.4 8.3 %copy-start.8 = (f32[96,768]{1,0:T(8,128)S(1)}, f32[96,768]{1,0:T(8,128)}, u32[]{:S(2)}) copy-start(f32[96,768]{1,0:T(8,128)} %get-tuple-element.137) | copy-start | bytes 884740

commit v2 on v1

v2 whole, which is shorter than its diff:
```python
import functools

import jax
import jax.numpy as jnp
from jax import lax
from jax.experimental import pallas as pl
from jax.experimental.pallas import tpu as pltpu
from jax.sharding import PartitionSpec as P

MESH = pl.DeviceIdType.MESH
F32, BF16 = jnp.float32, jnp.bfloat16
HD = 64
HEADS = 12
BIG = 2.0**30

class Net:
    def __init__(self, nd, nb, nc):
        self.nd, self.nb, self.nc = nd, nb, nc
        self.levels = nd.bit_length() - 1
        self.d, self.b, self.c = (lax.axis_index(a) for a in ("dp", "blk", "head"))
        top = self.levels - 1
        self.stride = [(1 - self.c) * 2**k + self.c * 2 ** (top - k) for k in range(self.levels)]
        self.sibling = (self.d, self.b, self.nc - 1 - self.c)

    def flip(self, d, k):
        s = self.stride[k]
        return d + s * (1 - 2 * ((d // s) % 2))

    def flips(self, mask):
        d = self.d
        for k in range(self.levels):
            if (mask >> k) & 1:
                d = self.flip(d, k)
        return d

    def across(self, k):
        return (self.flip(self.d, k), self.b, self.c)

    def near(self, e):
        order = [sorted(range(self.nb), key=lambda j: (abs(j - i), -j)) for i in range(self.nb)]
        got = order[0][e]
        for i in range(1, self.nb):
            got = jnp.where(self.b == i, order[i][e], got)
        return got

    def near_at(self, e):
        got = self.near(0)
        for i in range(1, self.nb):
            got = jnp.where(e == i, self.near(i), got)
        return got

    def slot(self, mask, blk):
        return (self.flips(mask) * self.nb + blk) * self.nc + self.c

    def peers(self):
        out = [(self.d, (self.b + u) % self.nb, self.c) for u in range(1, self.nb)]
        out += [self.across(k) for k in range(self.levels)]
        return out + [self.sibling]

    def barrier(self):
        bar = pltpu.get_barrier_semaphore()
        ps = self.peers()
        for p in ps:
            pl.semaphore_signal(bar, inc=1, device_id=p, device_id_type=MESH)
        pl.semaphore_wait(bar, len(ps))


def remote(src, dst, send, recv, dev):
    return pltpu.make_async_remote_copy(src_ref=src, dst_ref=dst, send_sem=send, recv_sem=recv, device_id=dev, device_id_type=MESH)


def blocks_of(full):
    return (lambda i: full.at[i]), (lambda k: full.at[pl.ds(0, k)])


def rows_of(full, rows, offset=0, stride=None):
    every = rows if stride is None else stride

    def place(i):
        return full.at[pl.ds(pl.multiple_of(i * every + offset, 8), rows)]

    return place, (lambda k: full.at[pl.ds(0, k * rows)])


class Gather:
    def __init__(self, net, mine, place, span, sems, narrow=False):
        self.net, self.mine, self.place, self.span, self.narrow = net, mine, place, span, narrow
        self.zsend, self.xsend, self.ssend, self.srecv, self.recv = sems

    def at(self, mask, blk):
        n = self.net
        if self.narrow:
            return self.place(blk * n.nc + n.c)
        return self.place(n.slot(mask, blk))

    def rsem(self, mask, blk):
        return self.recv.at[mask * self.net.nb + blk]

    def spread(self, mask, blk, src, dst):
        n = self.net
        if not self.narrow:
            for k in range(n.levels):
                if mask < (1 << k):
                    remote(src, dst, self.xsend, self.rsem(mask + (1 << k), blk), n.across(k)).start()
        remote(src, dst, self.ssend, self.srecv, n.sibling).start()

    def along(self, blk, src, dst):
        n = self.net
        sem = self.rsem(0, blk)

        @pl.when((n.b < n.nb - 1) & (blk <= n.b))
        def _():
            remote(src, dst, self.zsend, sem, (n.d, n.b + 1, n.c)).start()

        @pl.when((n.b > 0) & (blk >= n.b))
        def _():
            remote(src, dst, self.zsend, sem, (n.d, n.b - 1, n.c)).start()

    def own_line(self):
        self.along(self.net.b, self.mine, self.at(0, self.net.b))

    def own_spread(self):
        self.spread(0, self.net.b, self.mine, self.at(0, self.net.b))

    def z(self, e):
        blk = self.net.near(e)
        dst = self.at(0, blk)
        pltpu.make_async_copy(dst, dst, self.rsem(0, blk)).wait()
        self.along(blk, dst, dst)
        self.spread(0, blk, dst, dst)

    def x(self, mask, e):
        n = self.net
        blk = n.near(e)
        dst = self.at(mask, blk)
        pltpu.make_async_copy(dst, dst, self.rsem(mask, blk)).wait()
        self.spread(mask, blk, dst, dst)

    def own(self, sem):
        n = self.net
        return pltpu.make_async_copy(self.mine, self.at(0, n.b), sem)

    def wait_sibling(self):
        n = self.net
        half = self.span(n.nb if self.narrow else n.nd * n.nb)
        pltpu.make_async_copy(half, half, self.srecv).wait()

    def drain(self):
        n = self.net
        half = self.span(n.nb if self.narrow else n.nd * n.nb)
        pltpu.make_async_copy(half, half, self.ssend).wait()
        if not self.narrow:
            part = self.span((n.nd - 1) * n.nb)
            pltpu.make_async_copy(part, part, self.xsend).wait()
        edge = (n.b == 0) | (n.b == n.nb - 1)

        @pl.when(edge)
        def _():
            one = self.span(1)
            pltpu.make_async_copy(one, one, self.zsend).wait()

        @pl.when(jnp.logical_not(edge))
        def _():
            many = self.span(n.nb + 1)
            pltpu.make_async_copy(many, many, self.zsend).wait()


def gather_sems(n_pieces, nd, nb):
    return [pltpu.SemaphoreType.DMA((n_pieces, 4)), pltpu.SemaphoreType.DMA((n_pieces, nd * nb)), pltpu.SemaphoreType.DMA]


class Scatter:
    def __init__(self, net, parts, place, theirs, landing, span, xrecv, zrecv, out, sems, narrow=False, extra=()):
        self.net, self.parts, self.place, self.theirs, self.landing = net, parts, place, theirs, landing
        self.span, self.xbuf, self.zbuf, self.out, self.extra = span, xrecv, zrecv, out, extra
        self.sib_send, self.x_send, self.z_send, self.sib_sem, self.x_sem, self.z_sem = sems
        self.narrow, self.seen = narrow, set()
        self.nd = 1 if narrow else net.nd
        self.levels = 0 if narrow else net.levels

    def home(self, mask):
        return 0 if self.narrow else self.net.flips(mask)

    def start(self):
        for mask in range(self.nd - 1, -1, -1):
            mirrored = sum(1 << (self.levels - 1 - k) for k in range(self.levels) if (mask >> k) & 1)
            for blk in range(self.net.nb):
                self.send(self.home(mirrored) * self.net.nb + blk, mask)

    def send(self, at, sem):
        remote(self.theirs(at), self.landing(at), self.sib_send, self.sib_sem.at[sem], self.net.sibling).start()

    def arrived(self, sem, count):
        some = self.span(count)
        pltpu.make_async_copy(some, some, self.sib_sem.at[sem]).wait()

    def x_at(self, k, mask, blk):
        return ((1 << k) - 1 + mask) * self.net.nb + blk

    def z_at(self, side, blk, owner):
        return blk + side * jnp.where(blk == owner, self.net.nb - blk, 0)

    def add(self, at, more, to, extra=()):
        for pick, places in self.parts(at):
            def chosen(ref):
                return ref if pick is None else ref.at[pick]

            add_up(places + [chosen(m) for m in more] + list(extra), chosen(to))

    def reduce(self, mask, e):
        n = self.net
        blk = n.near(e)
        if self.narrow:
            self.arrived(blk, 1)
        elif mask not in self.seen:
            self.seen.add(mask)
            self.arrived(mask, n.nb)
        at = self.home(mask) * n.nb + blk
        place = self.place(at)
        more = []
        for k in range(self.levels - 1, -1, -1):
            if mask < (1 << k):
                i = self.x_at(k, mask, blk)
                got = self.xbuf.at[i]
                pltpu.make_async_copy(got, got, self.x_sem.at[i]).wait()
                more.append(got)
        if mask:
            k = mask.bit_length() - 1
            self.add(at, more, place)
            i = self.x_at(k, mask - (1 << k), blk)
            remote(place, self.xbuf.at[i], self.x_send, self.x_sem.at[i], n.across(k)).start()
            return

        def line(side, there):
            i = self.z_at(side, blk, n.b)
            got = self.zbuf.at[i]

            @pl.when(there)
            def _():
                pltpu.make_async_copy(got, got, self.z_sem.at[i]).wait()

            more.append(got)

        if e == 0:
            line(0, n.b > 0)
            line(1, n.b < n.nb - 1)
            self.add(at, more, self.out, self.extra)
            return
        side = jnp.where(blk > n.b, 0, 1)
        line(side, jnp.where(blk > n.b, n.b, n.nb - 1 - n.b) > 0)
        self.add(at, more, place)
        to = n.b + 1 - 2 * side
        i = self.z_at(side, blk, to)
        remote(place, self.zbuf.at[i], self.z_send, self.z_sem.at[i], (n.d, to, n.c)).start()

    def clear_edges(self):
        n = self.net

        def clear(i, carry):
            self.zbuf[i] = jnp.zeros(self.zbuf.shape[1:], self.zbuf.dtype)
            return carry

        @pl.when(n.b == 0)
        def _():
            lax.fori_loop(0, n.nb, clear, 0)

        @pl.when(n.b == n.nb - 1)
        def _():
            lax.fori_loop(0, n.nb - 1, clear, 0)
            clear(n.nb, 0)

    def drain(self):
        n = self.net
        some = self.span(self.nd * n.nb)
        pltpu.make_async_copy(some, some, self.sib_send).wait()
        if not self.narrow:
            some = self.xbuf.at[pl.ds(0, (n.nd - 1) * n.nb)]
            pltpu.make_async_copy(some, some, self.x_send).wait()
        some = self.zbuf.at[pl.ds(0, n.nb - 1)]
        pltpu.make_async_copy(some, some, self.z_send).wait()


def add_up(terms, to):
    shape = to.shape
    rows = shape[-2]
    step = rows
    while step % 2 == 0 and step > 32:
        step //= 2
    lead = [()] if len(shape) == 2 else [(g,) for g in range(shape[0])]
    for g in lead:
        for r in range(0, rows, step):
            at = g + (slice(r, r + step),)
            total = terms[0][at].astype(F32)
            for t in terms[1:]:
                total = total + t[at].astype(F32)
            to[at] = total.astype(to.dtype)


class AllSum:
    def __init__(self, net, value, got, send, recv):
        self.net, self.value, self.got, self.send, self.recv = net, value, got, send, recv

    def copy(self, stage, dev, src, slot):
        return remote(self.value.at[src], self.got.at[slot], self.send.at[slot], self.recv.at[slot], dev)

    def stages(self):
        n = self.net
        devs = [n.sibling] + [n.across(k) for k in range(n.levels)]
        steps = []
        for i, dev in enumerate(devs):
            steps.append(functools.partial(self.one, i, dev))
        steps.append(self.line_start)
        steps.append(self.line_end)
        return [lambda: self.copy(0, devs[0], 0, 0).start()] + steps

    def one(self, i, dev):
        n = self.net
        self.copy(i, dev, i, i).wait()
        self.value[i + 1] = self.value[i] + self.got[i]
        if i + 1 <= n.levels:
            self.copy(i + 1, n.across(i), i + 1, i + 1).start()

    def line_copy(self, u):
        n = self.net
        return self.copy(None, (n.d, (n.b + u) % n.nb, n.c), n.levels + 1, n.levels + u)

    def line_start(self):
        for u in range(1, self.net.nb):
            self.line_copy(u).start()

    def line_end(self):
        n = self.net
        for u in range(1, n.nb):
            self.line_copy(u).wait()
        total = self.value[n.levels + 1]
        for u in range(1, n.nb):
            total = total + self.got[n.levels + u]
        self.value[0] = total


def scatter_sems(n_pieces, nd, nb):
    return [
        pltpu.SemaphoreType.DMA((n_pieces, 3)),
        pltpu.SemaphoreType.DMA((n_pieces, max(nd, nb))),
        pltpu.SemaphoreType.DMA((n_pieces, (nd - 1) * nb)),
        pltpu.SemaphoreType.DMA((n_pieces, nb + 1)),
    ]


def dot(a, b, dims=((1,), (0,))):
    return lax.dot_general(a, b, (dims, ((), ())), preferred_element_type=F32)


def mask_lanes(seg_row, count):
    lanes = lax.broadcasted_iota(jnp.int32, (128, count), 0)
    return jnp.transpose(jnp.where(lanes == seg_row, -1.0, 0.0).astype(F32), (1, 0))


def project_keys(i, step, tok, wk, wv, bias_v, seg, kaug, v_scr):
    at = pl.ds(pl.multiple_of(i * step, step), step)
    piece = tok[at, :]
    keys = dot(piece, wk).astype(BF16)
    vals = (dot(piece, wv) + bias_v).astype(BF16)
    lanes = mask_lanes(seg[:, at], step).astype(BF16)
    for p in range(kaug.shape[0]):
        kaug[p, at, 0:128] = keys[:, p * 128:(p + 1) * 128]
        kaug[p, at, 128:256] = lanes
        v_scr[p, at, :] = vals[:, p * 128:(p + 1) * 128]


def project_queries(tok, wq, bias_q, seg, qaug, blk, qlen):
    mine = pl.ds(pl.multiple_of(blk * qlen, qlen), qlen)
    query = (dot(tok[mine, :], wq) + bias_q).astype(BF16)
    lane = lax.broadcasted_iota(jnp.int32, (qlen, 128), 1)
    feat = jnp.where(lane < 8, BIG * (1.0 + mask_lanes(seg[:, mine], qlen)), 0.0).astype(BF16)
    for p in range(qaug.shape[0] // 2):
        q_pair = query[:, p * 128:(p + 1) * 128].astype(F32) * HD**-0.5
        for half in range(2):
            keep = (lane >= 64) if half else (lane < 64)
            qaug[2 * p + half, :, 0:128] = jnp.where(keep, q_pair, 0.0).astype(BF16)
            qaug[2 * p + half, :, 128:256] = feat


def attend_chunk(i, qaug, kaug, v_scr, o_scr, exact_scr, lse_scr, chunk, per_head):
    h = i // per_head
    at = pl.ds(pl.multiple_of((i % per_head) * chunk, chunk), chunk)
    s = dot(qaug[h, at, :], kaug[h // 2], ((1,), (1,)))
    top = jnp.max(s, axis=-1, keepdims=True)
    p = jnp.exp(s - top)
    total = jnp.sum(p, axis=-1, keepdims=True)
    low = p.astype(BF16)
    rest = (p - low.astype(F32)).astype(BF16)
    value = v_scr[h // 2]
    o = dot(low, value)
    inverse = 1.0 / total
    o_scr[h, at, :] = o * inverse
    exact_scr[h, at, :] = (o + dot(rest, value)) * inverse
    lse_scr[h, at, :] = jnp.broadcast_to(top + jnp.log(total), (chunk, 128))


def join_heads(scr, p, at=slice(None)):
    first, second = scr[2 * p, at, :], scr[2 * p + 1, at, :]
    lane = lax.broadcasted_iota(jnp.int32, first.shape, 1)
    return jnp.where(lane < 64, first, second)


def head_columns(w, part, c, width):
    return w[:, pl.ds(pl.multiple_of((part * 2 + c) * width, 128), width)]


def fwd_kernel(tok, w, bias, seg, ctx, kaug, v_scr, qaug, lse_out, exact, lse_scr, o_scr, exact_scr, chunk=256):
    blk, c = lax.axis_index("blk"), lax.axis_index("head")
    qlen, width = ctx.shape
    total = tok.shape[0]
    step = min(512, total)
    wk, wv = head_columns(w, 1, c, width), head_columns(w, 2, c, width)

    def rows(i, carry):
        project_keys(i, step, tok, wk, wv, bias[1:2, :], seg, kaug, v_scr)
        return carry

    lax.fori_loop(0, total // step, rows, 0)
    project_queries(tok, head_columns(w, 0, c, width), bias[0:1, :], seg, qaug, blk, qlen)
    per_head = qlen // chunk

    def go(i, carry):
        attend_chunk(i, qaug, kaug, v_scr, o_scr, exact_scr, lse_scr, chunk, per_head)
        return carry

    lax.fori_loop(0, (width // HD) * per_head, go, 0)
    finish_forward(o_scr, exact_scr, lse_scr, lambda p, v: store_lanes(ctx, p, v), lse_out, exact)


def store_lanes(ref, p, value):
    ref[:, p * 128:(p + 1) * 128] = value


def finish_forward(o_scr, exact_scr, lse_scr, put, lse_out, exact):
    for p in range(o_scr.shape[0] // 2):
        put(p, join_heads(o_scr, p).astype(BF16))
        exact[p] = join_heads(exact_scr, p)
    for h in range(o_scr.shape[0]):
        lse_out[h] = jnp.transpose(lse_scr[h], (1, 0))[0:8, :]


def prepare_backward(gctx_of, exact, do_m, delta_row):
    pairs, qlen, _ = exact.shape
    lane = lax.broadcasted_iota(jnp.int32, (qlen, 128), 1)
    for p in range(pairs):
        grad = gctx_of(p)
        product = grad.astype(F32) * exact[p]
        for half in range(2):
            keep = (lane >= 64) if half else (lane < 64)
            do_m[2 * p + half] = jnp.where(keep, grad, jnp.zeros_like(grad))
            across = jnp.transpose(jnp.where(keep, product, 0.0), (1, 0))
            delta_row[2 * p + half] = jnp.broadcast_to(jnp.sum(across, axis=0, keepdims=True), (8, qlen))


def bwd_pair(pair, qaug, k_part, v_part, do_m, lse_row, delta_row, dq_scr, put, first, qs=slice(None)):
    dk = dv = None
    for half in range(2):
        h = 2 * pair + half
        q_part, do_part = qaug[h, qs, :], do_m[h, qs, :]
        s = dot(k_part, q_part, ((1,), (1,)))
        p = jnp.exp(s - lse_row[h, 0:1, qs])
        dp = dot(v_part, do_part, ((1,), (1,)))
        ds = (p * (dp - delta_row[h, 0:1, qs])).astype(BF16)
        v_term = dot(p.astype(BF16), do_part)
        k_term = dot(ds, q_part[:, 0:128])
        dv = v_term if dv is None else dv + v_term
        dk = k_term if dk is None else dk + k_term
        dq = dot(k_part[:, 0:128], ds, ((0,), (0,)))
        if first is None:
            dq_scr[h, :, qs] += dq
        else:
            dq_scr[h, :, qs] = jnp.where(first, dq, dq_scr[h, :, qs] + dq)
    put(dk, dv)


def join_dq(dq_scr, p):
    qlen = dq_scr.shape[2]
    lane = lax.broadcasted_iota(jnp.int32, (qlen, 128), 1)
    first, second = jnp.transpose(dq_scr[2 * p], (1, 0)), jnp.transpose(dq_scr[2 * p + 1], (1, 0))
    return (jnp.where(lane < 64, first, second) * HD**-0.5).astype(BF16)


VMEM = pl.BlockSpec(memory_space=pltpu.VMEM)
HBM = pl.BlockSpec(memory_space=pl.ANY)


def params(limit, collective=None):
    more = {} if collective is None else dict(collective_id=collective, has_side_effects=True)
    return pltpu.CompilerParams(vmem_limit_bytes=limit << 20, **more)


def lane_mean(x):
    return jnp.mean(x, axis=-1, keepdims=True)


def norm_parts(hidden):
    centered = hidden - lane_mean(hidden)
    scale = lax.rsqrt(lane_mean(centered * centered) + 1e-12)
    return centered * scale, scale


def norm_back(grad, unit, scale, gain):
    scaled = grad * gain
    return scale * (scaled - lane_mean(scaled) - unit * lane_mean(scaled * unit))


def gelu_and_slope(pre):
    cdf = 0.5 * (1.0 + lax.erf(pre * 0.7071067811865476))
    return pre * cdf, cdf + pre * (0.3989422804014327 * jnp.exp(-0.5 * pre * pre))


def column_sum(x):
    return jnp.sum(x, axis=0, keepdims=True)


def ffn_kernel(
    ctx, tok, cot, vecs, bias_in, w_out_h, w_in_h, w_down_h,
    out, resid_grad, gctx, dw_down_h, dw_in_h, dw_out_h, sums,
    w_out, w_in, w_down, act, slope, dw_a, dw_b, dw_c, in_sem, out_sem,
):
    groups, rows, half = ctx.shape
    width, ff = w_in.shape
    step = width
    loads = [
        pltpu.make_async_copy(src, dst, in_sem.at[i])
        for i, (src, dst) in enumerate([(w_out_h, w_out), (w_in_h, w_in), (w_down_h, w_down)])
    ]
    for load in loads:
        load.start()
    bias_out, gain_one, shift_one = vecs[2:3, :], vecs[3:4, :], vecs[4:5, :]
    bias_down, gain_two, shift_two = vecs[5:6, :], vecs[6:7, :], vecs[7:8, :]
    context = jnp.concatenate([ctx[g] for g in range(groups)], axis=1)
    loads[0].wait()
    resid_one = tok[...].astype(F32) + (dot(context, w_out[...]) + bias_out)
    unit_one, scale_one = norm_parts(resid_one)
    normed = unit_one * gain_one + shift_one
    normed_low = normed.astype(BF16)
    loads[1].wait()
    chunks = [slice(i, i + step) for i in range(0, ff, step)]
    for at in chunks:
        pre = dot(normed_low, w_in[:, at]) + bias_in[0:1, at]
        value, grad = gelu_and_slope(pre)
        act[:, at] = value.astype(BF16)
        slope[:, at] = grad
    loads[2].wait()
    resid_two = normed + (dot(act[...], w_down[...]) + bias_down)
    unit_two, scale_two = norm_parts(resid_two)
    out[...] = (unit_two * gain_two + shift_two).astype(BF16)
    grad_out = cot[...].astype(F32)
    grad_two = norm_back(grad_out, unit_two, scale_two, gain_two)
    grad_ffn = grad_two.astype(BF16)
    sums[0:2, :] = jnp.zeros((2, width), F32)
    sums[5:6, :] = column_sum(grad_ffn.astype(F32))
    sums[6:7, :] = column_sum(grad_out * unit_two)
    sums[7:8, :] = column_sum(grad_out)
    stores = []

    def store(src, dst):
        copy = pltpu.make_async_copy(src, dst, out_sem.at[len(stores)])
        copy.start()
        stores.append(copy)

    for at in chunks:
        dw_a[at, :] = dot(act[:, at], grad_ffn, ((0,), (0,))).astype(BF16)
        store(dw_a.at[at], dw_down_h.at[at])
    grad_normed = grad_two
    for i, at in enumerate(chunks):
        grad_act = dot(grad_ffn, w_down[at, :], ((1,), (1,)))
        grad_pre = (grad_act * slope[:, at]).astype(BF16)
        sums[8 + i:9 + i, :] = column_sum(grad_pre.astype(F32))
        dw_b[:, at] = dot(normed_low, grad_pre, ((0,), (0,))).astype(BF16)
        grad_normed = grad_normed + dot(grad_pre, w_in[:, at], ((1,), (1,)))
    store(dw_b, dw_in_h)
    sums[8 + len(chunks):, :] = jnp.zeros((sums.shape[0] - 8 - len(chunks), width), F32)
    sums[3:4, :] = column_sum(grad_normed * unit_one)
    sums[4:5, :] = column_sum(grad_normed)
    grad_one = norm_back(grad_normed, unit_one, scale_one, gain_one)
    resid_grad[...] = grad_one
    grad_attn = grad_one.astype(BF16)
    sums[2:3, :] = column_sum(grad_attn.astype(F32))
    dw_c[...] = dot(context, grad_attn, ((0,), (0,))).astype(BF16)
    store(dw_c, dw_out_h)
    grad_context = dot(grad_attn, w_out[...], ((1,), (1,))).astype(BF16)
    for g in range(groups):
        gctx[g] = grad_context[:, g * half:(g + 1) * half]
    for copy in stores:
        copy.wait()


def feed_forward(ctx, tok, cot, vecs, bias_in, w_out, w_in, w_down):
    groups, rows, half = ctx.shape
    width, ff = w_in.shape
    n_sums = 8 + -(-(ff // width) // 8) * 8
    return pl.pallas_call(
        ffn_kernel,
        out_shape=[
            jax.ShapeDtypeStruct((rows, width), BF16),
            jax.ShapeDtypeStruct((rows, width), F32),
            jax.ShapeDtypeStruct((groups, rows, half), BF16),
            jax.ShapeDtypeStruct((ff, width), BF16),
            jax.ShapeDtypeStruct((width, ff), BF16),
            jax.ShapeDtypeStruct((width, width), BF16),
            jax.ShapeDtypeStruct((n_sums, width), F32),
        ],
        in_specs=[VMEM] * 5 + [HBM] * 3,
        out_specs=[VMEM] * 3 + [HBM] * 3 + [VMEM],
        scratch_shapes=[
            pltpu.VMEM((width, width), BF16),
            pltpu.VMEM((width, ff), BF16),
            pltpu.VMEM((ff, width), BF16),
            pltpu.VMEM((rows, ff), BF16),
            pltpu.VMEM((rows, ff), F32),
            pltpu.VMEM((ff, width), BF16),
            pltpu.VMEM((width, ff), BF16),
            pltpu.VMEM((width, width), BF16),
            pltpu.SemaphoreType.DMA((3,)),
            pltpu.SemaphoreType.DMA((ff // width + 2,)),
        ],
        compiler_params=params(56),
    )(ctx, tok, cot, vecs, bias_in, w_out, w_in, w_down)


def gather_order(keys, narrow, nd, nb):
    events = []
    for p, (begin, dz, dx) in enumerate(keys):
        for e in range(nb):
            events.append((begin + e * dz, ("z", p, e)))
            if not narrow[p]:
                for mask in range(1, nd):
                    events.append((begin + e * dz + dx * mask.bit_length(), ("x", p, mask, e)))
    events.sort(key=lambda q: q[0])
    return [ev for _, ev in events]


def gather_all(shards, narrow, keys, nd, nb, nc):
    count = len(shards)

    def kernel(*refs):
        mine, full = refs[:count], refs[count:2 * count]
        four, recv, own_sem = refs[2 * count:]
        net = Net(nd, nb, nc)
        pieces = [
            Gather(net, mine[p], *blocks_of(full[p]), [four.at[p, i] for i in range(4)] + [recv.at[p]], narrow[p]) for p in range(count)
        ]
        net.barrier()
        for ev in gather_order(keys, narrow, nd, nb):
            if ev[0] == "z" and ev[2] == 0:
                pieces[ev[1]].own_line()
                pieces[ev[1]].own_spread()
            elif ev[0] == "z":
                pieces[ev[1]].z(ev[2])
            else:
                pieces[ev[1]].x(ev[2], ev[3])
        for piece in pieces:
            own = piece.own(own_sem)
            own.start()
            own.wait()
        for piece in pieces:
            piece.wait_sibling()
        for piece in pieces:
            piece.drain()

    outs = [
        jax.ShapeDtypeStruct(((nb * nc if thin else nd * nb * nc),) + s.shape, s.dtype) for s, thin in zip(shards, narrow)
    ]
    return pl.pallas_call(
        kernel,
        out_shape=outs,
        in_specs=[VMEM] * count,
        out_specs=[HBM] * count,
        scratch_shapes=gather_sems(count, nd, nb),
        compiler_params=params(56, 0),
    )(*shards)


def attend_forward(tok, w, bias, seg, qlen, width):
    total = tok.shape[0]
    heads = width // HD
    chunk = min(256, qlen)
    while chunk * total > 256 * 4096:
        chunk //= 2
    return pl.pallas_call(
        functools.partial(fwd_kernel, chunk=chunk),
        out_shape=[
            jax.ShapeDtypeStruct((qlen, width), BF16),
            jax.ShapeDtypeStruct((width // 128, total, 256), BF16),
            jax.ShapeDtypeStruct((width // 128, total, 128), BF16),
            jax.ShapeDtypeStruct((heads, qlen, 256), BF16),
            jax.ShapeDtypeStruct((heads, 8, qlen), F32),
            jax.ShapeDtypeStruct((heads // 2, qlen, 128), F32),
        ],
        in_specs=[VMEM] * 4,
        out_specs=[VMEM] * 6,
        scratch_shapes=[pltpu.VMEM((heads, qlen, 128), F32)] * 3,
        compiler_params=params(58),
    )(tok, w, bias, seg)


def pair_bwd_kernel(qaug, kaug, v_scr, lse, exact, gctx, dk, dv, dq, do_m, delta_row, dq_scr):
    step = pl.program_id(1)

    @pl.when(step == 0)
    def _():
        prepare_backward(lambda p: gctx[...], exact, do_m, delta_row)

    def put(k_term, v_term):
        dk[...] = k_term.astype(BF16)
        dv[...] = v_term.astype(BF16)

    bwd_pair(0, qaug, kaug[0], v_scr[0], do_m, lse, delta_row, dq_scr, put, step == 0)

    @pl.when(step == pl.num_programs(1) - 1)
    def _():
        dq[...] = join_dq(dq_scr, 0)


def finish_kernel(tok, dk, dv, tok_mine, dq, w, dtok, dw, dbias, own):
    i, c = pl.program_id(0), lax.axis_index("head")
    blk = lax.axis_index("blk")
    step, width = dk.shape
    qlen = dq.shape[0]

    def cols(part):
        return w[:, pl.ds(pl.multiple_of((part * 2 + c) * width, 128), width)]

    piece, grad_k, grad_v = tok[...], dk[...], dv[...]

    @pl.when(i == 0)
    def _():
        dw[:, 0:width] = dot(tok_mine[...], dq[...], ((0,), (0,)))
        dw[:, width:3 * width] = jnp.zeros((dw.shape[0], 2 * width), F32)
        dbias[0:1, :] = jnp.sum(dq[...].astype(F32), axis=0, keepdims=True)
        dbias[1:2, :] = jnp.zeros((1, width), F32)
        own[...] = dot(dq[...], cols(0), ((1,), (1,)))

    dw[:, width:2 * width] += dot(piece, grad_k, ((0,), (0,)))
    dw[:, 2 * width:3 * width] += dot(piece, grad_v, ((0,), (0,)))
    dbias[1:2, :] += jnp.sum(grad_v.astype(F32), axis=0, keepdims=True)
    grad = dot(grad_k, cols(1), ((1,), (1,))) + dot(grad_v, cols(2), ((1,), (1,)))
    per = qlen // step
    mine = i // per == blk
    at = pl.ds(pl.multiple_of((i % per) * step, step), step)
    dtok[...] = (grad + jnp.where(mine, own[at, :], 0.0)).astype(BF16)


def attend_backward(tok, tok_mine, w, qaug, kaug, v_scr, lse, exact, gctx):
    heads, qlen, _ = qaug.shape
    total, d_model = tok.shape
    width = heads * HD
    kc = min(512, total)
    dk, dv, dq = pl.pallas_call(
        pair_bwd_kernel,
        grid=(heads // 2, total // kc),
        out_shape=[
            jax.ShapeDtypeStruct((total, width), BF16),
            jax.ShapeDtypeStruct((total, width), BF16),
            jax.ShapeDtypeStruct((qlen, width), BF16),
        ],
        in_specs=[
            pl.BlockSpec((2, qlen, 256), lambda p, j: (p, 0, 0)),
            pl.BlockSpec((1, kc, 256), lambda p, j: (p, j, 0)),
            pl.BlockSpec((1, kc, 128), lambda p, j: (p, j, 0)),
            pl.BlockSpec((2, 8, qlen), lambda p, j: (p, 0, 0)),
            pl.BlockSpec((1, qlen, 128), lambda p, j: (p, 0, 0)),
            pl.BlockSpec((qlen, 128), lambda p, j: (0, p)),
        ],
        out_specs=[pl.BlockSpec((kc, 128), lambda p, j: (j, p))] * 2 + [pl.BlockSpec((qlen, 128), lambda p, j: (0, p))],
        scratch_shapes=[
            pltpu.VMEM((2, qlen, 128), BF16),
            pltpu.VMEM((2, 8, qlen), F32),
            pltpu.VMEM((2, 128, qlen), F32),
        ],
        compiler_params=params(56),
    )(qaug, kaug, v_scr, lse, exact, gctx)
    step = min(512, qlen)
    whole = lambda i: (0, 0)
    rows = lambda i: (i, 0)
    return pl.pallas_call(
        finish_kernel,
        grid=(total // step,),
        out_shape=[
            jax.ShapeDtypeStruct((total, d_model), BF16),
            jax.ShapeDtypeStruct((d_model, 3 * width), F32),
            jax.ShapeDtypeStruct((2, width), F32),
        ],
        in_specs=[
            pl.BlockSpec((step, d_model), rows),
            pl.BlockSpec((step, width), rows),
            pl.BlockSpec((step, width), rows),
            pl.BlockSpec((qlen, d_model), whole),
            pl.BlockSpec((qlen, width), whole),
            pl.BlockSpec((d_model, w.shape[1]), whole),
        ],
        out_specs=[
            pl.BlockSpec((step, d_model), rows),
            pl.BlockSpec((d_model, 3 * width), whole),
            pl.BlockSpec((2, width), whole),
        ],
        scratch_shapes=[pltpu.VMEM((qlen, d_model), F32)],
        compiler_params=params(56),
    )(tok, dk, dv, tok_mine, dq, w)


SPACE = (0.25, 1.0, 0.2)


def send_blocks(piece, nb):
    for blk in range(nb):
        piece.send(blk, blk)


def scatter_all(arrays, narrow, joined, small, nd, nb, nc):
    count = len(arrays)
    flat = []
    for a, j in zip(arrays, joined):
        flat += list(a) if j else [a]
    n_in = len(flat) + 1

    def kernel(*refs):
        ins, small_in = list(refs[:n_in - 1]), refs[n_in - 1]
        outs, small_out = refs[n_in:n_in + count], refs[n_in + count]
        rest = list(refs[n_in + count + 1:])
        net = Net(nd, nb, nc)
        s3, sib_sem, x_sem, z_sem, sum_send, sum_recv = rest[-6:]
        value, got = rest[-8:-6]
        bufs = rest[:-8]
        pieces = []
        for p in range(count):
            first = ins.pop(0)
            sib = ins.pop(0) if joined[p] else bufs.pop(0)
            xbuf = None if narrow[p] else bufs.pop(0)
            zbuf = bufs.pop(0)
            sems = [s3.at[p, i] for i in range(3)] + [sib_sem.at[p], x_sem.at[p], z_sem.at[p]]
            if joined[p]:
                parts = lambda at, first=first: [(None, [first.at[at]])]
                place = lambda at, first=first: first.at[at]
                theirs = lambda at, sib=sib: sib.at[at]
                landing = lambda at, first=first: first.at[at, net.c]
            else:
                place = lambda at, first=first: first.at[at * nc + net.c]
                parts = lambda at, place=place, sib=sib: [(None, [place(at), sib.at[at]])]
                theirs = lambda at, first=first: first.at[at * nc + nc - 1 - net.c]
                landing = lambda at, sib=sib: sib.at[at]
            span = lambda k, sib=sib: sib.at[pl.ds(0, k)]
            pieces.append(Scatter(net, parts, place, theirs, landing, span, xbuf, zbuf, outs[p], sems, narrow[p]))
        sums = AllSum(net, value, got, sum_send, sum_recv)
        for piece in pieces:
            piece.clear_edges()
        value[0] = small_in[...]
        net.barrier()
        events = []
        for p, piece in enumerate(pieces):
            t = SPACE[0] * p
            begin = functools.partial(send_blocks, piece, nb) if narrow[p] else piece.start
            events.append((t - 0.4, begin))
            for mask in range(piece.nd - 1, -1, -1):
                for e in range(nb - 1, -1, -1):
                    when = t + SPACE[1] * (piece.levels - mask.bit_length()) + SPACE[2] * (nb - 1 - e)
                    events.append((when, functools.partial(piece.reduce, mask, e)))
        for i, s in enumerate(sums.stages()):
            events.append((0.3 * i, s))
        events.sort(key=lambda q: q[0])
        for _, ev in events:
            ev()
        small_out[...] = value[0]
        for piece in pieces:
            piece.drain()

    outs, scratch = [], []
    for a, thin, j in zip(arrays, narrow, joined):
        full = a[0] if j else a
        block = full.shape[1:]
        outs.append(jax.ShapeDtypeStruct(block, F32))
        n_dp = 1 if thin else nd
        if not j:
            scratch.append(pltpu.VMEM((n_dp * nb,) + block, BF16))
        if not thin:
            scratch.append(pltpu.VMEM(((nd - 1) * nb,) + block, BF16))
        scratch.append(pltpu.VMEM((nb + 1,) + block, BF16))
    levels = nd.bit_length() - 1
    scratch += [pltpu.VMEM((levels + 2,) + small.shape, F32), pltpu.VMEM((levels + nb,) + small.shape, F32)]
    scratch += scatter_sems(count, nd, nb)
    scratch += [pltpu.SemaphoreType.DMA((levels + nb,))] * 2
    outs.append(jax.ShapeDtypeStruct(small.shape, F32))
    return pl.pallas_call(
        kernel,
        out_shape=outs,
        in_specs=[VMEM] * n_in,
        out_specs=[VMEM] * (count + 1),
        scratch_shapes=scratch,
        compiler_params=params(60, 1),
    )(*flat, small)


def unpack_vectors(small, vecs, bias_in, r, r_ff):
    n = small.shape[0]
    width, ff = vecs.shape[1], bias_in.shape[1]

    def gathered(rows, per, count):
        lane = lax.broadcasted_iota(jnp.int32, (8, 128), 1)
        tiles = [jnp.zeros((8, 128), F32) for _ in range(count // 128)]
        for i in range(n):
            piece = small[i, rows, :].astype(F32)
            shift, tile = per * i % 128, per * i // 128
            if shift:
                piece = pltpu.roll(piece, shift, 1)
            if shift + per <= 128:
                tiles[tile] = tiles[tile] + piece
            else:
                tiles[tile] = tiles[tile] + jnp.where(lane >= shift, piece, 0.0)
                tiles[tile + 1] = tiles[tile + 1] + jnp.where(lane < shift, piece, 0.0)
        return tiles

    for t, tile in enumerate(gathered(slice(0, 8), r, width)):
        vecs[:, t * 128:(t + 1) * 128] = tile
    for t, tile in enumerate(gathered(slice(8, 16), r_ff, ff)):
        bias_in[:, t * 128:(t + 1) * 128] = tile[0:1, :]


def pack_vectors(vectors, bias_in):
    row = lax.broadcasted_iota(jnp.int32, (16, 128), 0)
    packed = jnp.zeros((16, 128), F32)
    for i, v in enumerate(list(vectors) + [bias_in]):
        line = jnp.pad(v.astype(F32), (0, 128 - v.shape[0]))
        packed = jnp.where(row == i, line[None, :], packed)
    return packed.astype(BF16)


FRONT = {
    "small": (21, 16, ((21, 29, 32, 39), (34, 55, 60, 63), (35, 54, 59, 64), (58, 73, 75, 76))),
    "q": (2, 0, ((2, 8, 10, 20), (6, 17, 23, 42), (7, 19, 25, 43), (14, 37, 49, 68))),
    "t0": (3, 4, ((3, 9, 15, 27),)),
    "t1": (26, 1, ((26, 41, 48, 52),)),
    "t2": (44, 40, ((44, 53, 67, 77),)),
    "t3": (45, 31, ((45, 65, 71, 80),)),
    "o": (11, 22, ((11, 18, 24, 30), (46, 36, 50, 57), (47, 38, 51, 56), (69, 66, 72, 74))),
    "i": (91, 33, ((91, 101, 104, 107), (61, 110, 113, 118), (62, 109, 114, 119), (78, 121, 122, 124))),
    "d": (70, 5, ((70, 81, 83, 89), (12, 85, 94, 99), (13, 86, 93, 100), (28, 96, 103, 111))),
    "work": (79, 82, 84, 87, 88, 90, 92, 95, 97, 98, 102, 105, 106, 108, 112, 115, 116, 117, 120, 123),
}


def front_time(nd, nb, kind, what, e=0):
    if (nd, nb) == (4, 4) and (kind != "work" or e == len(FRONT["work"])):
        row = FRONT[kind]
        if kind == "work":
            return row[what]
        if what == "line":
            return row[0]
        if what == "spread":
            return row[1]
        return row[2][what][e]
    first = ["small", "q", "t0", "t1", "t2", "t3", "o", "i", "d"].index(kind) * 10 if kind != "work" else 0
    if kind == "work":
        return (40 if what == 0 else 200) + what
    if what in ("line", "spread"):
        return first
    return first + 3 * e + (4 * what.bit_length() if what else 0)


def front(small, w_qkv, tok, w_out, w_in, w_down, seg, nd, nb, nc):
    n = nd * nb * nc
    rows, width = tok.shape
    half, qlen, total = width // nc, nc * rows, nb * nc * rows
    heads = half // HD
    pairs = heads // 2
    r, r_ff, ff = w_qkv.shape[0], w_down.shape[0], w_in.shape[1]
    quarters = 4
    part = rows // quarters
    chunk = min(256, qlen)
    per_head = qlen // chunk
    step = min(512, total)

    def kernel(
        small_in, q_in, tok_in, o_in, i_in, d_in, seg_in,
        ctx2, vecs, bias_in, lse_out, exact, q_h, tok_h, o_h, i_h, d_h, kaug_h, v_h, qaug_h,
        small_all, w_v, tok_v, kaug, v_scr, qaug, o_scr, exact_scr, lse_scr, ctx_loc,
        four, recv, own_sem, load_sem, save_sem, swap_sem,
    ):
        net = Net(nd, nb, nc)
        c = net.c
        specs = [("small", small_in, blocks_of(small_all), False), ("q", q_in, rows_of(q_h, r), False)]
        for i in range(quarters):
            mine = tok_in.at[pl.ds(i * part, part)]
            specs.append((("t", i), mine, rows_of(tok_h, part, i * part, rows), True))
        specs += [("o", o_in, rows_of(o_h, r), False), ("i", i_in, rows_of(i_h, r), False), ("d", d_in, rows_of(d_h, r_ff), False)]
        piece, own = {}, {}
        for p, (name, mine, (place, span), narrow) in enumerate(specs):
            sems = [four.at[p, i] for i in range(4)] + [recv.at[p]]
            piece[name] = Gather(net, mine, place, span, sems, narrow)
            own[name] = piece[name].own(own_sem.at[p])
        tokens = [("t", i) for i in range(quarters)]
        for name in piece:
            own[name].start()
        net.barrier()

        def unpack():
            piece["small"].wait_sibling()
            own["small"].wait()
            unpack_vectors(small_all, vecs, bias_in, r, r_ff)

        def load():
            copies = []
            for name in ["q"] + tokens:
                piece[name].wait_sibling()
                own[name].wait()
            for k in range(3):
                lanes = pl.ds(pl.multiple_of((k * nc + c) * half, 128), half)
                copies.append(pltpu.make_async_copy(q_h.at[:, lanes], w_v.at[:, pl.ds(k * half, half)], load_sem.at[k]))
            copies.append(pltpu.make_async_copy(tok_h, tok_v, load_sem.at[3]))
            for copy in copies:
                copy.start()
            for copy in copies:
                copy.wait()

        lanes = pl.ds(pl.multiple_of(c * half, 128), half)

        def keys(i):
            project_keys(i, step, tok_v, w_v[:, half:2 * half], w_v[:, 2 * half:3 * half], vecs[1:2, lanes], seg_in, kaug, v_scr)

        saves = [
            pltpu.make_async_copy(src, dst, save_sem.at[i])
            for i, (src, dst) in enumerate([(kaug, kaug_h), (v_scr, v_h), (qaug, qaug_h)])
        ]

        def queries():
            project_queries(tok_v, w_v[:, 0:half], vecs[0:1, lanes], seg_in, qaug, net.b, qlen)
            for save in saves:
                save.start()

        swap = remote(ctx_loc.at[nc - 1 - c], ctx2.at[c], swap_sem.at[0], swap_sem.at[1], net.sibling)

        def finish():
            def put(p, value):
                for g in range(nc):
                    ctx_loc[g, :, p * 128:(p + 1) * 128] = value[g * rows:(g + 1) * rows]

            finish_forward(o_scr, exact_scr, lse_scr, put, lse_out, exact)
            swap.start()
            ctx2[c] = ctx_loc[c]

        steps = heads * per_head
        order = []
        for name in piece:
            kind = "t" + str(name[1]) if name in tokens else name
            order.append((front_time(nd, nb, kind, "line"), piece[name].own_line, None))
            order.append((front_time(nd, nb, kind, "spread"), piece[name].own_spread, None))
            for e in range(1, nb):
                order.append((front_time(nd, nb, kind, 0, e), functools.partial(piece[name].z, e), None))
            for mask in range(1, 1 if name in tokens else nd):
                for e in range(nb):
                    order.append((front_time(nd, nb, kind, mask, e), functools.partial(piece[name].x, mask, e), None))
        work = [unpack, load] + [functools.partial(keys, i) for i in range(total // step)] + [queries]
        work += [None] * steps + [finish]
        for i, act in enumerate(work):
            index = i - (len(work) - steps - 1) if act is None else None
            order.append((front_time(nd, nb, "work", i, len(work)), act, index))
        order.sort(key=lambda q: q[0])
        begin = next(i for i, q in enumerate(order) if q[2] == 0)
        end = next(i for i, q in enumerate(order) if q[2] == steps - 1)
        for _, act, _ in order[:begin]:
            act()
        beside = {}
        for _, act, i in order[begin:end + 1]:
            if act is None:
                at_step = i
            else:
                beside.setdefault(at_step, []).append(act)

        def attention(i, carry):
            attend_chunk(i, qaug, kaug, v_scr, o_scr, exact_scr, lse_scr, chunk, per_head)
            for g, acts in beside.items():

                @pl.when(i == g)
                def _(acts=acts):
                    for act in acts:
                        act()

            return carry

        lax.fori_loop(0, steps, attention, 0)
        for _, act, _ in order[end + 1:]:
            act()
        for name in ("o", "i", "d"):
            piece[name].wait_sibling()
            own[name].wait()
        for name in piece:
            piece[name].drain()
        for save in saves:
            save.wait()
        swap.wait()

    count = 5 + quarters
    return pl.pallas_call(
        kernel,
        out_shape=[
            jax.ShapeDtypeStruct((nc, rows, half), BF16),
            jax.ShapeDtypeStruct((8, width), F32),
            jax.ShapeDtypeStruct((1, ff), F32),
            jax.ShapeDtypeStruct((heads, 8, qlen), F32),
            jax.ShapeDtypeStruct((pairs, qlen, 128), F32),
            jax.ShapeDtypeStruct((n * r, 3 * width), BF16),
            jax.ShapeDtypeStruct((total, width), BF16),
            jax.ShapeDtypeStruct((n * r, width), BF16),
            jax.ShapeDtypeStruct((n * r, ff), BF16),
            jax.ShapeDtypeStruct((n * r_ff, width), BF16),
            jax.ShapeDtypeStruct((pairs, total, 256), BF16),
            jax.ShapeDtypeStruct((pairs, total, 128), BF16),
            jax.ShapeDtypeStruct((heads, qlen, 256), BF16),
        ],
        in_specs=[VMEM] * 7,
        out_specs=[VMEM] * 5 + [HBM] * 8,
        scratch_shapes=[
            pltpu.VMEM((n, 16, 128), BF16),
            pltpu.VMEM((width, 3 * half), BF16),
            pltpu.VMEM((total, width), BF16),
            pltpu.VMEM((pairs, total, 256), BF16),
            pltpu.VMEM((pairs, total, 128), BF16),
            pltpu.VMEM((heads, qlen, 256), BF16),
            pltpu.VMEM((heads, qlen, 128), F32),
            pltpu.VMEM((heads, qlen, 128), F32),
            pltpu.VMEM((heads, qlen, 128), F32),
            pltpu.VMEM((nc, rows, half), BF16),
            pltpu.SemaphoreType.DMA((count, 4)),
            pltpu.SemaphoreType.DMA((count, nd * nb)),
            pltpu.SemaphoreType.DMA((count,)),
            pltpu.SemaphoreType.DMA((4,)),
            pltpu.SemaphoreType.DMA((3,)),
            pltpu.SemaphoreType.DMA((2,)),
        ],
        compiler_params=params(56, 2),
    )(small, w_qkv, tok, w_out, w_in, w_down, seg)


BACK = {
    "d": (0, ((77, 67, 62, 57), (15, 16, 26, 27), (2, 3, 4, 5), (6, 7, 8, 9))),
    "i": (13, ((85, 75, 74, 73), (33, 34, 37, 39), (19, 21, 23, 25), (18, 20, 22, 24))),
    "o": (42, ((88, 82, 81, 79), (56, 58, 59, 61), (44, 45, 46, 47), (48, 49, 50, 51))),
    "q": (53, ((91, 90, 89, 86), (76, 78, 80, 83), (60, 64, 65, 66), (63, 69, 70, 71))),
    "t": (0, ((68, 40, 35, 28),)),
    "work": (1, 10, 11, 12, 14, 17, 29, 30, 31, 32, 36, 38, 41, 43, 53, 54, 52, 52.1, 55, 72, 84, 84.1, 87),
}


def back_time(nd, nb, kind, what, e=0):
    if (nd, nb) == (4, 4) and (kind != "work" or e == len(BACK["work"])):
        row = BACK[kind]
        if kind == "work":
            return row[what]
        return row[0] if what == "start" else row[1][what][e]
    if kind == "work":
        return 20 + 10 * what + (100 if what > e - 10 else 0)
    first = {"d": 0, "i": 10, "o": 20, "t": 300, "q": 400}[kind]
    if what == "start":
        return first
    return first + 30 - 5 * what.bit_length() + (nb - 1 - e)


def back(dw_down, dw_in, dw_out, tok, w_qkv, kaug_in, v_in, qaug_in, lse, exact_in, gctx, resid_grad, sums, nd, nb, nc):
    owners = nd * nb
    n = owners * nc
    rows, width = resid_grad.shape
    total = tok.shape[0]
    half, qlen = width // nc, nc * rows
    heads = half // HD
    pairs = heads // 2
    r, ff = dw_in.shape[2], dw_in.shape[3]
    r_ff = dw_down.shape[2]
    levels = nd.bit_length() - 1
    names = ["d", "i", "o", "t", "q"]

    def kernel(
        d_h, i_h, o_h, tok_h, w_h, kaug_h, v_h, qaug_h, lse_row, exact, gctx_in, resid, sums_in,
        g_tok, g_qkv, g_out, g_in, g_down, g_small,
        d_own, i_own, o_own, d_sib, i_sib, o_sib, t_sib, q_sib, d_x, i_x, o_x, q_x, d_z, i_z, o_z, t_z, q_z,
        t_part, q_part, q_full, q_out, tok_v, tok_t, w_v, kaug, v_scr, qaug, gctx_all, do_m, delta_row, dq_scr, dkv, grad_q,
        value, got,
        own_sem, load_sem, swap_sem, s3, sib_sem, x_sem, z_sem, sum_send, sum_recv,
    ):
        net = Net(nd, nb, nc)
        c, other = net.c, nc - 1 - net.c
        copies = {}
        for i, (name, src, dst) in enumerate([("d", d_h, d_own), ("i", i_h, i_own), ("o", o_h, o_own)]):
            copies[name] = pltpu.make_async_copy(src.at[:, c], dst, own_sem.at[i])
        loads = [(kaug_h, kaug), (v_h, v_scr), (qaug_h, qaug), (tok_h, tok_v)]
        for k in range(3):
            lanes = pl.ds(pl.multiple_of((k * nc + c) * half, 128), half)
            loads.append((w_h.at[:, lanes], w_v.at[:, pl.ds(k * half, half)]))
        loads = [pltpu.make_async_copy(src, dst, load_sem.at[i]) for i, (src, dst) in enumerate(loads)]
        for copy in list(copies.values()) + loads:
            copy.start()
        piece = {}
        for p, (name, src, own, sib, xbuf, zbuf, out) in enumerate(
            [
                ("d", d_h, d_own, d_sib, d_x, d_z, g_down),
                ("i", i_h, i_own, i_sib, i_x, i_z, g_in),
                ("o", o_h, o_own, o_sib, o_x, o_z, g_out),
                ("t", None, None, t_sib, None, t_z, g_tok),
                ("q", None, None, q_sib, q_x, q_z, q_out),
            ]
        ):
            sems = [s3.at[p, i] for i in range(3)] + [sib_sem.at[p], x_sem.at[p], z_sem.at[p]]
            landing = lambda at, sib=sib: sib.at[at]
            span = lambda k, sib=sib: sib.at[pl.ds(0, k)]
            extra = ()
            if name == "t":
                place = lambda at: t_part.at[at, c]
                parts = lambda at: [(None, [t_part.at[at, c], t_sib.at[at]])]
                theirs = lambda at: t_part.at[at, other]
                extra = (resid,)
            elif name == "q":
                place = lambda at: q_full.at[at]
                parts = lambda at: [(c, [q_part.at[at, c]]), (other, [q_sib.at[at]])]
                theirs = lambda at: q_part.at[at, other]
            else:
                place = lambda at, own=own: own.at[at]
                parts = lambda at, own=own, sib=sib: [(None, [own.at[at], sib.at[at]])]
                theirs = lambda at, src=src: src.at[at, other]
            piece[name] = Scatter(net, parts, place, theirs, landing, span, xbuf, zbuf, out, sems, name == "t", extra)
            piece[name].clear_edges()
        whole = AllSum(net, value, got, sum_send, sum_recv)
        swap = remote(gctx_in.at[other], gctx_all.at[c], swap_sem.at[0], swap_sem.at[1], net.sibling)
        net.barrier()
        swap.start()
        gctx_all[c] = gctx_in[c]

        def begin(name):
            piece[name].start()
            copies[name].wait()

        def prepare():
            for copy in loads:
                copy.wait()
            swap.wait()
            tok_t[...] = jnp.transpose(tok_v[...], (1, 0))
            lane = lambda p: slice(p * 128, (p + 1) * 128)
            prepare_backward(
                lambda p: jnp.concatenate([gctx_all[g, :, lane(p)] for g in range(nc)], axis=0), exact, do_m, delta_row
            )

        def token_grad(blk):
            at = pl.ds(pl.multiple_of(blk * qlen, qlen), qlen)
            return dot(dkv[at, :], w_v[:, half:3 * half], ((1,), (1,)))

        def put_tokens(blk, grad):
            for g in range(nc):
                t_part[blk, g] = grad[g * rows:(g + 1) * rows].astype(BF16)
            piece["t"].send(blk, blk)

        def weights():
            grad_q[...] = jnp.concatenate([join_dq(dq_scr, p) for p in range(pairs)], axis=1)
            mine = pl.ds(pl.multiple_of(net.b * qlen, qlen), qlen)
            for k in range(3):
                if k:
                    grad = dot(tok_t[...], dkv[:, (k - 1) * half:k * half])
                else:
                    grad = dot(tok_t[:, mine], grad_q[...])
                for at in range(owners):
                    for g in range(nc):
                        i = at * nc + g
                        q_part[at, g, :, k * half:(k + 1) * half] = grad[i * r:(i + 1) * r].astype(BF16)

        def own_tokens():
            put_tokens(net.b, token_grad(net.b) + dot(grad_q[...], w_v[:, 0:half], ((1,), (1,))))

        def small_sums():
            lanes = pl.ds(pl.multiple_of(c * half, 128), half)
            value[0] = sums_in[...]
            value[0, 0:1, lanes] = column_sum(grad_q[...].astype(F32))
            value[0, 1:2, lanes] = column_sum(dkv[:, half:2 * half].astype(F32))

        order = []
        for name in names:
            p = piece[name]
            if name in copies:
                order.append((back_time(nd, nb, name, "start"), functools.partial(begin, name), None))
            for mask in range(p.nd):
                for e in range(nb):
                    order.append((back_time(nd, nb, name, mask, e), functools.partial(p.reduce, mask, e), None))
        steps = nb * pairs
        work = [prepare] + [None] * steps + [weights, piece["q"].start, own_tokens, small_sums] + whole.stages()
        for i, act in enumerate(work):
            order.append((back_time(nd, nb, "work", i, len(work)), act, i - 1 if act is None else None))
        order.sort(key=lambda q: q[0])
        first = next(i for i, q in enumerate(order) if q[2] == 0)
        last = next(i for i, q in enumerate(order) if q[2] == steps - 1)
        for _, act, _ in order[:first]:
            act()
        beside = {}
        for _, act, i in order[first:last + 1]:
            if act is None:
                at_step = i
            else:
                beside.setdefault(at_step, []).append(act)

        def attention(i, carry):
            pair = i % pairs
            blk = net.near_at(nb - 1 - i // pairs)
            at = pl.ds(pl.multiple_of(blk * qlen, qlen), qlen)

            def put(dk, dv):
                dkv[at, pl.ds(pl.multiple_of(pair * 128, 128), 128)] = dk.astype(BF16)
                dkv[at, pl.ds(pl.multiple_of(half + pair * 128, 128), 128)] = dv.astype(BF16)

            bwd_pair(pair, qaug, kaug[pair, at, :], v_scr[pair, at, :], do_m, lse_row, delta_row, dq_scr, put, i < pairs)

            @pl.when((pair == pairs - 1) & (i < steps - 1))
            def _():
                put_tokens(blk, token_grad(blk))

            for g, acts in beside.items():

                @pl.when(i == g)
                def _(acts=acts):
                    for act in acts:
                        act()

            return carry

        lax.fori_loop(0, steps, attention, 0)
        for _, act, _ in order[last + 1:]:
            act()
        for k in range(3):
            for g in range(nc):
                lanes = slice((k * nc + g) * half, (k * nc + g + 1) * half)
                g_qkv[:, lanes] = q_out[g, :, k * half:(k + 1) * half]
        me = (net.d * nb + net.b) * nc + c
        feature = lax.broadcasted_iota(jnp.int32, (width, 128), 0)
        lane = lax.broadcasted_iota(jnp.int32, (width, 128), 1)
        pick = jnp.where((feature == me * r + lane) & (lane < r), 1.0, 0.0).astype(F32)
        in_row, in_lane = (me * r_ff) // width, (me * r_ff) % width
        pick_in = jnp.where((feature == in_lane + lane) & (lane < r_ff), 1.0, 0.0).astype(F32)
        exactly = dict(precision=lax.Precision.HIGHEST, preferred_element_type=F32)
        g_small[0:8, :] = jnp.dot(value[0, 0:8, :], pick, **exactly)
        found = jnp.dot(value[0, 8:16, :], pick_in, **exactly)
        row = lax.broadcasted_iota(jnp.int32, found.shape, 0)
        g_small[8:16, :] = jnp.broadcast_to(column_sum(jnp.where(row == in_row, found, 0.0)), (8, 128))
        for name in names:
            piece[name].drain()

    block = {"d": (r_ff, width), "i": (r, ff), "o": (r, width), "t": (rows, width)}
    joined = (nc, r, 3 * half)
    vmem = lambda shape, kind=BF16: pltpu.VMEM(shape, kind)
    scratch = [vmem((owners,) + block[k]) for k in "dio"] + [vmem((owners,) + block[k]) for k in "dio"]
    scratch += [vmem((nb,) + block["t"]), vmem((owners, r, 3 * half))]
    scratch += [vmem(((nd - 1) * nb,) + block[k]) for k in "dio"] + [vmem(((nd - 1) * nb,) + joined)]
    scratch += [vmem((nb + 1,) + block[k]) for k in "diot"] + [vmem((nb + 1,) + joined)]
    scratch += [
        vmem((nb, nc, rows, width)),
        vmem((owners,) + joined),
        vmem((owners,) + joined),
        vmem(joined, F32),
        vmem((total, width)),
        vmem((width, total)),
        vmem((width, 3 * half)),
        vmem((pairs, total, 256)),
        vmem((pairs, total, 128)),
        vmem((heads, qlen, 256)),
        vmem((nc, rows, half)),
        vmem((heads, qlen, 128)),
        vmem((heads, 8, qlen), F32),
        vmem((heads, 128, qlen), F32),
        vmem((total, 2 * half)),
        vmem((qlen, half)),
        vmem((levels + 2,) + sums.shape, F32),
        vmem((levels + nb,) + sums.shape, F32),
        pltpu.SemaphoreType.DMA((3,)),
        pltpu.SemaphoreType.DMA((7,)),
        pltpu.SemaphoreType.DMA((2,)),
    ]
    scratch += scatter_sems(5, nd, nb) + [pltpu.SemaphoreType.DMA((levels + nb,))] * 2
    return pl.pallas_call(
        kernel,
        out_shape=[
            jax.ShapeDtypeStruct((rows, width), F32),
            jax.ShapeDtypeStruct((r, 3 * width), F32),
            jax.ShapeDtypeStruct((r, width), F32),
            jax.ShapeDtypeStruct((r, ff), F32),
            jax.ShapeDtypeStruct((r_ff, width), F32),
            jax.ShapeDtypeStruct((16, 128), F32),
        ],
        in_specs=[HBM] * 8 + [VMEM] * 5,
        out_specs=[VMEM] * 6,
        scratch_shapes=scratch,
        compiler_params=params(62, 3),
    )(dw_down, dw_in, dw_out, tok, w_qkv, kaug_in, v_in, qaug_in, lse, exact_in, gctx, resid_grad, sums)


def body(
    tokens,
    segment,
    w_qkv,
    bias_query,
    bias_value,
    w_out,
    bias_out,
    gain_attn,
    shift_attn,
    w_in,
    bias_in,
    w_down,
    bias_down,
    gain_ffn,
    shift_ffn,
    cotangent,
):
    nd, nb, nc = lax.axis_size("dp"), lax.axis_size("blk"), lax.axis_size("head")
    n_dev = nd * nb * nc
    d_idx, b_idx, c_idx = lax.axis_index("dp"), lax.axis_index("blk"), lax.axis_index("head")
    me = (d_idx * nb + b_idx) * nc + c_idx
    seqs, rows, width = tokens.shape
    ff = w_in.shape[1]
    half_w = width // nc
    qlen = nc * rows
    r = w_qkv.shape[0]
    r_ff = w_down.shape[0]
    flat_in = tokens.reshape(rows, width)
    cot = cotangent.reshape(rows, width)
    vectors = [bias_query, bias_value, bias_out, gain_attn, shift_attn, bias_down, gain_ffn, shift_ffn]
    if nb * qlen <= 2048 and r % 8 == 0 and ff // width <= 8:
        small = pack_vectors(vectors, bias_in)
        ctx2, vecs, full_bin, lse, exact, f_qkv, tok_all, f_out, f_in, f_down, kaug, v_all, qaug = front(
            small, w_qkv, flat_in, w_out, w_in, w_down, segment, nd, nb, nc
        )
        out, resid_grad, gctx2, dw_down, dw_in, dw_out, sums = feed_forward(
            ctx2, flat_in, cot, vecs, full_bin, f_out, f_in, f_down
        )
        g_tok, o_qkv, o_out, o_in, o_down, g_small = back(
            dw_down.reshape(nd * nb, nc, r_ff, width),
            dw_in.reshape(nd * nb, nc, r, ff),
            dw_out.reshape(nd * nb, nc, r, width),
            tok_all, f_qkv, kaug, v_all, qaug, lse, exact, gctx2, resid_grad, sums, nd, nb, nc,
        )
        g_bq, g_bv, g_bo, g_g1, g_s1, g_bd, g_g2, g_s2 = (g_small[i, :r] for i in range(8))
        return (
            out.reshape(seqs, rows, width), g_tok.reshape(seqs, rows, width),
            o_qkv, g_bq, g_bv, o_out, g_bo, g_g1, g_s1, o_in, g_small[8, :r_ff], o_down, g_bd, g_g2, g_s2,
        )
    packed = jnp.concatenate(vectors + [bias_in])
    used = packed.shape[0]
    lanes = -(-used // 128) * 128
    packed = jnp.broadcast_to(jnp.pad(packed, (0, lanes - used))[None], (8, lanes))
    n4 = 4
    parts = [flat_in[i * (rows // n4):(i + 1) * (rows // n4)] for i in range(n4)]
    shards = [packed, w_qkv] + parts + [w_out, w_in, w_down]
    narrow = [False, False] + [True] * n4 + [False] * 3
    keys = [(-1, 3, 3), (0, 3, 3), (7, 9, 0), (10, 9, 0), (13, 9, 0), (16, 9, 0), (2, 4, 4), (9, 6, 5), (22, 6, 5)]
    small, g_qkv, t0, t1, t2, t3, g_out, g_in, g_down = gather_all(shards, narrow, keys, nd, nb, nc)
    full_small = small[:, 0, :used]
    vecs = full_small[:, :8 * r].reshape(n_dev, 8, r).transpose(1, 0, 2).reshape(8, width).astype(F32)
    full_bin = full_small[:, 8 * r:].reshape(ff).astype(F32)
    bq, bv, bout, gain_one, shift_one, bdown, gain_two, shift_two = (vecs[i] for i in range(8))
    full_qkv = g_qkv.reshape(width, 3 * width)
    full_wout = g_out.reshape(width, width)
    full_win = g_in.reshape(width, ff)
    full_wdown = g_down.reshape(ff, width)
    tok_all = jnp.stack([t0, t1, t2, t3], axis=1).reshape(nb * qlen, width)
    my_bias = lax.dynamic_slice(vecs, (0, c_idx * half_w), (2, half_w))
    ctx, kaug, v_scr, qaug, lse, exact = attend_forward(tok_all, full_qkv, my_bias, segment, qlen, half_w)
    context_low = ctx.reshape(seqs, qlen, 1, half_w)
    back_tokens = lax.all_to_all(context_low, "head", split_axis=1, concat_axis=2, tiled=True)
    ctx2 = back_tokens.reshape(rows, nc, half_w).transpose(1, 0, 2)
    out, grad_resid_one, gctx2, dw_down, dw_in, dw_out, sums = feed_forward(
        ctx2, flat_in, cot, vecs, full_bin.reshape(1, ff), full_wout, full_win, full_wdown
    )
    output = out.reshape(seqs, rows, width)
    grad_context = gctx2.transpose(1, 0, 2)
    grad_headed = lax.all_to_all(
        grad_context.reshape(seqs, rows, nc, half_w), "head", split_axis=2, concat_axis=1, tiled=True
    )
    gctx = grad_headed.reshape(qlen, half_w)
    tok_mine = lax.dynamic_slice(tok_all, (b_idx * qlen, 0), (qlen, width))
    dtok, dw, dbias = attend_backward(tok_all, tok_mine, full_qkv, qaug, kaug, v_scr, lse, exact, gctx)
    dw = dw.astype(BF16).reshape(nd * nb, nc, r, 3 * half_w)
    ours = lax.dynamic_index_in_dim(dw, c_idx, 1, keepdims=False)
    theirs = lax.dynamic_index_in_dim(dw, 1 - c_idx, 1, keepdims=False)
    joined_full = jnp.stack([ours, ours], axis=1)
    sums = lax.dynamic_update_slice(sums, dbias, (0, c_idx * half_w))
    o_down, o_in, o_out, o_tok, o_qkv, total = scatter_all(
        [
            dw_down.reshape(n_dev, r_ff, width),
            dw_in.reshape(n_dev, r, ff),
            dw_out.reshape(n_dev, r, width),
            dtok.reshape(nb * nc, rows, width),
            (joined_full, theirs),
        ],
        [False, False, False, True, False],
        [False, False, False, False, True],
        sums,
        nd,
        nb,
        nc,
    )
    grad_tokens = (grad_resid_one + o_tok).reshape(seqs, rows, width)
    o_qkv = o_qkv.reshape(2, r, 3, half_w).transpose(1, 2, 0, 3).reshape(r, 3 * width)
    mine = lax.dynamic_slice(total, (0, me * r), (8, r))
    mine_in = lax.dynamic_slice(total[8:8 + ff // width].reshape(ff), (me * r_ff,), (r_ff,))
    g_bq, g_bv, g_bo, g_g1, g_s1, g_bd, g_g2, g_s2 = (mine[i] for i in range(8))
    return (
        output,
        grad_tokens,
        o_qkv,
        g_bq,
        g_bv,
        o_out,
        g_bo,
        g_g1,
        g_s1,
        o_in,
        mine_in,
        o_down,
        g_bd,
        g_g2,
        g_s2,
    )


def solution(mesh):
    weight, vector = P(("dp", "blk", "head"), None), P(("dp", "blk", "head"))
    token = P("dp", ("blk", "head"), None)
    return jax.shard_map(
        body,
        mesh=mesh,
        in_specs=(
            token,
            P("dp", None),
            weight,
            vector,
            vector,
            weight,
            vector,
            vector,
            vector,
            weight,
            vector,
            weight,
            vector,
            vector,
            vector,
            token,
        ),
        out_specs=(
            token,
            token,
            weight,
            vector,
            vector,
            weight,
            vector,
            vector,
            vector,
            weight,
            vector,
            weight,
            vector,
            vector,
            vector,
        ),
        check_vma=False,
    )
```

time: 373 us -> 225 us (0.60)
  Pallas kernels: 279 us -> 209 us
  matrix products: 37.1 us -> 0 us
  local copies, waits for them, and re-layouts: 31 us -> 14.7 us
  other arithmetic: 15.4 us -> 0.71 us
  starting transfers between devices: 7.15 us -> 0 us
    pallas_call x5 -> x3, Pallas kernels: 279 us -> 209 us  [the longest x1 100 us: back(): pl.pallas_call(kernel, out_shape=[jax.ShapeDtypeStruct((rows, width), F32...]
    dot_general x9 -> x0, matrix products: 37.1 us -> none  [the longest x6 20.8 us: dot(): return lax.dot_general(a, b, (dims, ((), ())), preferred_element_type=F32)]
    all_to_all x2 -> x0, starting transfers between devices: 7.15 us -> none  [the longest x1 3.69 us: body(): lax.all_to_all(grad_context.reshape(seqs, rows, nc, half_w), 'head', spli...]
    concatenate x2 -> x0, local copies, waits for them, and re-layouts: 6.16 us -> none  [the longest x1 6.1 us: body(): packed = jnp.concatenate(vectors + [bias_in])]
    reshape x11 -> x0, local copies, waits for them, and re-layouts: 5.41 us -> none  [the longest x2 1.89 us: body(): grad_context.reshape(seqs, rows, nc, half_w)]
    reduce_sum x8 -> x0, other arithmetic: 4.4 us -> none  [the longest x2 1.45 us: layer_norm(): centered = hidden - jnp.mean(hidden, axis=-1, keepdims=True)]
    dynamic_slice x4 -> x0, local copies, waits for them, and re-layouts: 4.01 us -> none  [the longest x1 2.06 us: body(): tok_mine = lax.dynamic_slice(tok_all, (b_idx * qlen, 0), (qlen, width))]
    slice x4 -> x0, local copies, waits for them, and re-layouts: 3.77 us -> none  [the longest x1 1.78 us: body(): flat_in[i * (rows // n4):(i + 1) * (rows // n4)]]
  transfers between devices with their start and end apart: 2 -> 0, of which waited for: 1 -> 0; matrix products, arithmetic and copies ran while one was open for 4% -> 0% of each run, Pallas kernels for 0% -> 0%
where the time goes in v2:
time: 225 us
  Pallas kernels  209 us (93%)
  local copies, waits for them, and re-layouts  14.7 us (7%)
    pallas_call x1, Pallas kernels, back(): pl.pallas_call(kernel, out_shape=[jax.ShapeDtypeStruct((rows, width), F32...  100 us
    pallas_call x1, Pallas kernels, front(): pl.pallas_call(kernel, out_shape=[jax.ShapeDtypeStruct((nc, rows, half),...  90.4 us
    pallas_call x1, Pallas kernels, feed_forward(): pl.pallas_call(ffn_kernel, out_shape=[jax.ShapeDtypeStruct((rows, width),...  17.8 us
    unnamed x5, local copies, waits for them, and re-layouts  8.6 us

profile of v2, /device:TPU:0, one launch (start us, length us, event | category | flops | bytes accessed | tf_op | source)
XLA Modules:
  0.0 224.8 jit_solution(12606546412696778054)
XLA Ops:
  0.6 0.7 pad_convert_fusion.8
  1.3 0.7 pad_convert_fusion
  2.0 0.7 pad_convert_fusion.2
  2.7 0.7 pad_convert_fusion.4
  3.3 0.7 pad_convert_fusion.6
  4.1 0.7 select_convert_fusion.small_in
  4.7 90.4 %shard_map.271 = (bf16[2,256,384]{2,1,0:T(8,128)(2,1)}, f32[8,768]{1,0:T(8,128)}, f32[1,3072]{1,0:T(1,128)}, f32[6,8,512]{2,1,0:T(8,128)}, f32[3,512,128]{2,1,0:...) custom-call(bf16[16,128]{1,0:T(8,128)(2,1)} %select_convert_fusion.s, ...), custom_call_target="tpu_custom_call" | custom-call | tf_op jit(solution)/shard_map/pallas_call | solution.py:1098
  95.2 17.8 %shard_map.272 = (bf16[256,768]{1,0:T(8,128)(2,1)}, f32[256,768]{1,0:T(8,128)}, bf16[2,256,384]{2,1,0:T(8,128)(2,1)}, bf16[3072,768]{1,0:T(8,128)(2,1)}, bf16[76...) custom-call(bf16[2,256,384]{2,1,0:T(8,128)(2,1)} %get-tuple-element.41.ctx, ...), custom_call_target="tpu_custom_call" | custom-call | tf_op jit(solution)/shard_map/pallas_call | solution.py:598
  113.0 100.5 %shard_map.273 = (f32[256,768]{1,0:T(8,128)}, f32[24,2304]{1,0:T(8,128)}, f32[24,768]{1,0:T(8,128)}, f32[24,3072]{1,0:T(8,128)}, f32[96,768]{1,0:T(8,128)}, /*index=5*/f32[16,128]{1,0:T(8,128)}) custom-call(bf16[16,2,96,768]{3,2,1,0:T(8,128)(2,1)} %bitcast.25, bf16[16,2,24,3072]{3,2,1,0:T(8,128)(2,1)} %bitcast.26, bf16[16,2,24,768]{3,2,1,0:T(8,128)(2,1)} %bitcast.29, ...), custom_call_target="tpu_custom_call" | custom-call | tf_op jit(solution)/shard_map/pallas_call | solution.py:1376
  213.5 1.2 slice_bitcast_fusion.3
  214.6 1.5 slice_bitcast_fusion
  216.2 2.1 copy.36
  218.2 1.6 copy.37
  219.9 1.5 copy.38
  221.4 1.7 copy.39
  223.1 1.7 copy.40
  (5 shorter events, 0.0 us)

commit v3 on v2

--- a/solution.py
+++ b/solution.py
@@ -21,22 +21,22 @@
         top = self.levels - 1
         self.stride = [(1 - self.c) * 2**k + self.c * 2 ** (top - k) for k in range(self.levels)]
         self.sibling = (self.d, self.b, self.nc - 1 - self.c)
-
-    def flip(self, d, k):
-        s = self.stride[k]
-        return d + s * (1 - 2 * ((d // s) % 2))
+        steps = [s * (1 - 2 * ((self.d // s) % 2)) for s in self.stride]
+        self.flipped = [self.d]
+        for step in steps:
+            self.flipped += [d + step for d in self.flipped]
+        self.nearest = [self.find_near(e) for e in range(self.nb)]
 
     def flips(self, mask):
-        d = self.d
-        for k in range(self.levels):
-            if (mask >> k) & 1:
-                d = self.flip(d, k)
-        return d
+        return self.flipped[mask]
 
     def across(self, k):
-        return (self.flip(self.d, k), self.b, self.c)
+        return (self.flipped[1 << k], self.b, self.c)
 
     def near(self, e):
+        return self.nearest[e]
+
+    def find_near(self, e):
         order = [sorted(range(self.nb), key=lambda j: (abs(j - i), -j)) for i in range(self.nb)]
         got = order[0][e]
         for i in range(1, self.nb):
@@ -170,11 +170,11 @@
 
 
 class Scatter:
-    def __init__(self, net, parts, place, theirs, landing, span, xrecv, zrecv, out, sems, narrow=False, extra=()):
+    def __init__(self, net, parts, place, theirs, landing, span, xrecv, zrecv, out, sems, narrow=False, extra=(), early=False):
         self.net, self.parts, self.place, self.theirs, self.landing = net, parts, place, theirs, landing
         self.span, self.xbuf, self.zbuf, self.out, self.extra = span, xrecv, zrecv, out, extra
         self.sib_send, self.x_send, self.z_send, self.sib_sem, self.x_sem, self.z_sem = sems
-        self.narrow, self.seen = narrow, set()
+        self.narrow, self.seen, self.early = narrow, set(), early
         self.nd = 1 if narrow else net.nd
         self.levels = 0 if narrow else net.levels
 
@@ -183,9 +183,11 @@
 
     def start(self):
         for mask in range(self.nd - 1, -1, -1):
-            mirrored = sum(1 << (self.levels - 1 - k) for k in range(self.levels) if (mask >> k) & 1)
-            for blk in range(self.net.nb):
-                self.send(self.home(mirrored) * self.net.nb + blk, mask)
+            self.start_home(self.home(mask))
+
+    def start_home(self, d):
+        for blk in range(self.net.nb):
+            self.send(d * self.net.nb + blk, d)
 
     def send(self, at, sem):
         remote(self.theirs(at), self.landing(at), self.sib_send, self.sib_sem.at[sem], self.net.sibling).start()
@@ -193,6 +195,10 @@
     def arrived(self, sem, count):
         some = self.span(count)
         pltpu.make_async_copy(some, some, self.sib_sem.at[sem]).wait()
+
+    def sent(self):
+        some = self.span(self.nd * self.net.nb)
+        pltpu.make_async_copy(some, some, self.sib_send).wait()
 
     def x_at(self, k, mask, blk):
         return ((1 << k) - 1 + mask) * self.net.nb + blk
@@ -214,7 +220,7 @@
             self.arrived(blk, 1)
         elif mask not in self.seen:
             self.seen.add(mask)
-            self.arrived(mask, n.nb)
+            self.arrived(self.home(mask), n.nb)
         at = self.home(mask) * n.nb + blk
         place = self.place(at)
         more = []
@@ -271,8 +277,8 @@
 
     def drain(self):
         n = self.net
-        some = self.span(self.nd * n.nb)
-        pltpu.make_async_copy(some, some, self.sib_send).wait()
+        if not self.early:
+            self.sent()
         if not self.narrow:
             some = self.xbuf.at[pl.ds(0, (n.nd - 1) * n.nb)]
             pltpu.make_async_copy(some, some, self.x_send).wait()
@@ -485,7 +491,7 @@
 
 
 VMEM = pl.BlockSpec(memory_space=pltpu.VMEM)
-HBM = pl.BlockSpec(memory_space=pl.ANY)
+HBM = pl.BlockSpec(memory_space=pltpu.HBM)
 
 
 def params(limit, collective=None):
@@ -896,6 +902,31 @@
     )(*flat, small)
 
 
+def hand_out(arrays, small, r, r_ff):
+    count = len(arrays)
+
+    def kernel(*refs):
+        ins, small_in = refs[:count], refs[count]
+        outs, vectors, sems = refs[count + 1:2 * count + 1], refs[2 * count + 1:-1], refs[-1]
+        copies = [pltpu.make_async_copy(a, b, sems.at[i]) for i, (a, b) in enumerate(zip(ins, outs))]
+        for copy in copies:
+            copy.start()
+        for i, out in enumerate(vectors):
+            out[...] = small_in[i, 0:out.shape[0]]
+        for copy in copies:
+            copy.wait()
+
+    sizes = [r] * 8 + [r_ff]
+    return pl.pallas_call(
+        kernel,
+        out_shape=[jax.ShapeDtypeStruct(a.shape, a.dtype) for a in arrays] + [jax.ShapeDtypeStruct((s,), F32) for s in sizes],
+        in_specs=[VMEM] * (count + 1),
+        out_specs=[HBM] * count + [VMEM] * 9,
+        scratch_shapes=[pltpu.SemaphoreType.DMA((count,))],
+        compiler_params=params(60),
+    )(*arrays, small)
+
+
 def unpack_vectors(small, vecs, bias_in, r, r_ff):
     n = small.shape[0]
     width, ff = vecs.shape[1], bias_in.shape[1]
@@ -922,25 +953,25 @@
 
 
 def pack_vectors(vectors, bias_in):
-    row = lax.broadcasted_iota(jnp.int32, (16, 128), 0)
-    packed = jnp.zeros((16, 128), F32)
-    for i, v in enumerate(list(vectors) + [bias_in]):
-        line = jnp.pad(v.astype(F32), (0, 128 - v.shape[0]))
-        packed = jnp.where(row == i, line[None, :], packed)
-    return packed.astype(BF16)
+    shape = (16,) + vectors[0].shape
+    row = lax.broadcasted_iota(jnp.int32, shape, 0)
+    few = jnp.zeros(shape, BF16)
+    for i, v in enumerate(vectors):
+        few = jnp.where(row == i, v[None, :], few)
+    return few, jnp.broadcast_to(bias_in[None, :], (16,) + bias_in.shape)
 
 
 FRONT = {
-    "small": (21, 16, ((21, 29, 32, 39), (34, 55, 60, 63), (35, 54, 59, 64), (58, 73, 75, 76))),
-    "q": (2, 0, ((2, 8, 10, 20), (6, 17, 23, 42), (7, 19, 25, 43), (14, 37, 49, 68))),
-    "t0": (3, 4, ((3, 9, 15, 27),)),
-    "t1": (26, 1, ((26, 41, 48, 52),)),
-    "t2": (44, 40, ((44, 53, 67, 77),)),
-    "t3": (45, 31, ((45, 65, 71, 80),)),
-    "o": (11, 22, ((11, 18, 24, 30), (46, 36, 50, 57), (47, 38, 51, 56), (69, 66, 72, 74))),
-    "i": (91, 33, ((91, 101, 104, 107), (61, 110, 113, 118), (62, 109, 114, 119), (78, 121, 122, 124))),
-    "d": (70, 5, ((70, 81, 83, 89), (12, 85, 94, 99), (13, 86, 93, 100), (28, 96, 103, 111))),
-    "work": (79, 82, 84, 87, 88, 90, 92, 95, 97, 98, 102, 105, 106, 108, 112, 115, 116, 117, 120, 123),
+    "small": (2, 55, ((2, 6, 11, 30), (71, 15, 26, 41), (72, 14, 25, 40), (78, 28, 35, 62))),
+    "q": (0, 51, ((0, 5, 9, 22), (67, 13, 21, 36), (68, 12, 20, 37), (77, 27, 32, 52))),
+    "t0": (29, 23, ((29, 47, 53, 66),)),
+    "t1": (49, 65, ((49, 69, 76, 85),)),
+    "t2": (3, 61, ((3, 10, 18, 34),)),
+    "t3": (4, 82, ((4, 16, 24, 42),)),
+    "o": (17, 33, ((17, 31, 44, 48), (45, 39, 58, 63), (46, 38, 57, 64), (56, 54, 70, 73))),
+    "i": (80, 43, ((80, 93, 96, 103), (60, 106, 110, 117), (59, 105, 109, 115), (74, 118, 121, 123))),
+    "d": (50, 1, ((50, 75, 79, 88), (8, 84, 86, 101), (7, 83, 89, 100), (19, 91, 98, 113))),
+    "work": (81, 87, 90, 92, 94, 95, 97, 99, 102, 104, 107, 108, 111, 112, 114, 116, 119, 120, 122, 124),
 }
 
 
@@ -962,7 +993,7 @@
     return first + 3 * e + (4 * what.bit_length() if what else 0)
 
 
-def front(small, w_qkv, tok, w_out, w_in, w_down, seg, nd, nb, nc):
+def front(few, many, w_qkv, tok, w_out, w_in, w_down, seg, nd, nb, nc):
     n = nd * nb * nc
     rows, width = tok.shape
     half, qlen, total = width // nc, nc * rows, nb * nc * rows
@@ -976,13 +1007,17 @@
     step = min(512, total)
 
     def kernel(
-        small_in, q_in, tok_in, o_in, i_in, d_in, seg_in,
-        ctx2, vecs, bias_in, lse_out, exact, q_h, tok_h, o_h, i_h, d_h, kaug_h, v_h, qaug_h,
-        small_all, w_v, tok_v, kaug, v_scr, qaug, o_scr, exact_scr, lse_scr, ctx_loc,
+        few_in, many_in, q_in, tok_in, o_in, i_in, d_in, seg_in,
+        ctx2, vecs, bias_in, lse_out, exact, q_h, tok_h, o_h, i_h, d_h, kaug_h, v_h, qaug_h, tok_t_h,
+        small_in, small_all, w_v, tok_v, tok_t, kaug, v_scr, qaug, o_scr, exact_scr, lse_scr, ctx_loc,
         four, recv, own_sem, load_sem, save_sem, swap_sem,
     ):
         net = Net(nd, nb, nc)
         c = net.c
+        small_in[...] = jnp.zeros((16, 128), BF16)
+        small_in[:, 0:r] = few_in[...]
+        row = lax.broadcasted_iota(jnp.int32, (16, r_ff), 0)
+        small_in[:, 0:r_ff] = jnp.where(row == 8, many_in[...], small_in[:, 0:r_ff])
         specs = [("small", small_in, blocks_of(small_all), False), ("q", q_in, rows_of(q_h, r), False)]
         for i in range(quarters):
             mine = tok_in.at[pl.ds(i * part, part)]
@@ -1024,11 +1059,12 @@
 
         saves = [
             pltpu.make_async_copy(src, dst, save_sem.at[i])
-            for i, (src, dst) in enumerate([(kaug, kaug_h), (v_scr, v_h), (qaug, qaug_h)])
+            for i, (src, dst) in enumerate([(kaug, kaug_h), (v_scr, v_h), (qaug, qaug_h), (tok_t, tok_t_h)])
         ]
 
         def queries():
             project_queries(tok_v, w_v[:, 0:half], vecs[0:1, lanes], seg_in, qaug, net.b, qlen)
+            tok_t[...] = jnp.transpose(tok_v[...], (1, 0))
             for save in saves:
                 save.start()
 
@@ -1111,13 +1147,16 @@
             jax.ShapeDtypeStruct((pairs, total, 256), BF16),
             jax.ShapeDtypeStruct((pairs, total, 128), BF16),
             jax.ShapeDtypeStruct((heads, qlen, 256), BF16),
+            jax.ShapeDtypeStruct((width, total), BF16),
         ],
-        in_specs=[VMEM] * 7,
-        out_specs=[VMEM] * 5 + [HBM] * 8,
+        in_specs=[VMEM] * 8,
+        out_specs=[VMEM] * 5 + [HBM] * 9,
         scratch_shapes=[
+            pltpu.VMEM((16, 128), BF16),
             pltpu.VMEM((n, 16, 128), BF16),
             pltpu.VMEM((width, 3 * half), BF16),
             pltpu.VMEM((total, width), BF16),
+            pltpu.VMEM((width, total), BF16),
             pltpu.VMEM((pairs, total, 256), BF16),
             pltpu.VMEM((pairs, total, 128), BF16),
             pltpu.VMEM((heads, qlen, 256), BF16),
@@ -1129,20 +1168,20 @@
             pltpu.SemaphoreType.DMA((count, nd * nb)),
             pltpu.SemaphoreType.DMA((count,)),
             pltpu.SemaphoreType.DMA((4,)),
-            pltpu.SemaphoreType.DMA((3,)),
+            pltpu.SemaphoreType.DMA((4,)),
             pltpu.SemaphoreType.DMA((2,)),
         ],
         compiler_params=params(56, 2),
-    )(small, w_qkv, tok, w_out, w_in, w_down, seg)
+    )(few, many, w_qkv, tok, w_out, w_in, w_down, seg)
 
 
 BACK = {
-    "d": (0, ((77, 67, 62, 57), (15, 16, 26, 27), (2, 3, 4, 5), (6, 7, 8, 9))),
-    "i": (13, ((85, 75, 74, 73), (33, 34, 37, 39), (19, 21, 23, 25), (18, 20, 22, 24))),
-    "o": (42, ((88, 82, 81, 79), (56, 58, 59, 61), (44, 45, 46, 47), (48, 49, 50, 51))),
-    "q": (53, ((91, 90, 89, 86), (76, 78, 80, 83), (60, 64, 65, 66), (63, 69, 70, 71))),
-    "t": (0, ((68, 40, 35, 28),)),
-    "work": (1, 10, 11, 12, 14, 17, 29, 30, 31, 32, 36, 38, 41, 43, 53, 54, 52, 52.1, 55, 72, 84, 84.1, 87),
+    "d": (0, ((63, 50, 41, 35), (49, 38, 27, 19), (32, 22, 16, 15), (33, 23, 12, 11))),
+    "i": (0, ((103, 94, 89, 78), (81, 77, 66, 57), (72, 64, 53, 43), (73, 65, 54, 44))),
+    "o": (0, ((91, 76, 69, 61), (67, 58, 47, 40), (55, 45, 36, 30), (56, 46, 37, 31))),
+    "q": (0, ((108, 107, 106, 102), (104, 99, 97, 95), (100, 92, 87, 86), (101, 93, 88, 85))),
+    "t": (0, ((96, 79, 70, 52),)),
+    "work": (0, 1, 2, 3, 4, 5, 6, 7, 8, 9, 10, 13, 14, 17, 18, 20, 21, 24, 25, 26, 28, 29, 34, 39, 42, 48, 51, 59, 60, 62, 68, 71, 74, 75, 82, 84, 80, 80.1, 83, 90, 98, 98.1, 105),
 }
 
 
@@ -1160,47 +1199,40 @@
     return first + 30 - 5 * what.bit_length() + (nb - 1 - e)
 
 
-def back(dw_down, dw_in, dw_out, tok, w_qkv, kaug_in, v_in, qaug_in, lse, exact_in, gctx, resid_grad, sums, nd, nb, nc):
+def back(
+    ctx, tok, cot, vecs, bias_in, w_out, w_in, w_down,
+    tok_t_in, w_qkv, kaug_in, v_in, qaug_in, lse, exact_in, nd, nb, nc,
+):
     owners = nd * nb
-    n = owners * nc
-    rows, width = resid_grad.shape
-    total = tok.shape[0]
+    rows, width = tok.shape
+    total = tok_t_in.shape[1]
+    ff = w_in.shape[1]
     half, qlen = width // nc, nc * rows
     heads = half // HD
     pairs = heads // 2
-    r, ff = dw_in.shape[2], dw_in.shape[3]
-    r_ff = dw_down.shape[2]
+    r, r_ff = width // (owners * nc), ff // (owners * nc)
     levels = nd.bit_length() - 1
     names = ["d", "i", "o", "t", "q"]
+    chunks = [slice(i, i + width) for i in range(0, ff, width)]
+    n_sums = 8 + -(-len(chunks) // 8) * 8
 
     def kernel(
-        d_h, i_h, o_h, tok_h, w_h, kaug_h, v_h, qaug_h, lse_row, exact, gctx_in, resid, sums_in,
-        g_tok, g_qkv, g_out, g_in, g_down, g_small,
+        ctx_in, tok_in, cot_in, vecs_in, bias_in, wo_h, wi_h, wd_h, tok_t_h, w_h, kaug_h, v_h, qaug_h, lse_row, exact,
+        out, g_tok, g_qkv, g_out, g_in, g_down, g_small,
         d_own, i_own, o_own, d_sib, i_sib, o_sib, t_sib, q_sib, d_x, i_x, o_x, q_x, d_z, i_z, o_z, t_z, q_z,
-        t_part, q_part, q_full, q_out, tok_v, tok_t, w_v, kaug, v_scr, qaug, gctx_all, do_m, delta_row, dq_scr, dkv, grad_q,
-        value, got,
-        own_sem, load_sem, swap_sem, s3, sib_sem, x_sem, z_sem, sum_send, sum_recv,
+        q_out, resid, gctx, gctx_all, grad_q, value, got,
+        load_sem, swap_sem, s3, sib_sem, x_sem, z_sem, sum_send, sum_recv,
     ):
         net = Net(nd, nb, nc)
         c, other = net.c, nc - 1 - net.c
-        copies = {}
-        for i, (name, src, dst) in enumerate([("d", d_h, d_own), ("i", i_h, i_own), ("o", o_h, o_own)]):
-            copies[name] = pltpu.make_async_copy(src.at[:, c], dst, own_sem.at[i])
-        loads = [(kaug_h, kaug), (v_h, v_scr), (qaug_h, qaug), (tok_h, tok_v)]
-        for k in range(3):
-            lanes = pl.ds(pl.multiple_of((k * nc + c) * half, 128), half)
-            loads.append((w_h.at[:, lanes], w_v.at[:, pl.ds(k * half, half)]))
-        loads = [pltpu.make_async_copy(src, dst, load_sem.at[i]) for i, (src, dst) in enumerate(loads)]
-        for copy in list(copies.values()) + loads:
-            copy.start()
-        piece = {}
-        for p, (name, src, own, sib, xbuf, zbuf, out) in enumerate(
+        piece, held = {}, {}
+        for p, (name, own, sib, xbuf, zbuf, result) in enumerate(
             [
-                ("d", d_h, d_own, d_sib, d_x, d_z, g_down),
-                ("i", i_h, i_own, i_sib, i_x, i_z, g_in),
-                ("o", o_h, o_own, o_sib, o_x, o_z, g_out),
-                ("t", None, None, t_sib, None, t_z, g_tok),
-                ("q", None, None, q_sib, q_x, q_z, q_out),
+                ("d", d_own, d_sib, d_x, d_z, g_down),
+                ("i", i_own, i_sib, i_x, i_z, g_in),
+                ("o", o_own, o_sib, o_x, o_z, g_out),
+                ("t", None, t_sib, None, t_z, g_tok),
+                ("q", None, q_sib, q_x, q_z, q_out),
             ]
         ):
             sems = [s3.at[p, i] for i in range(3)] + [sib_sem.at[p], x_sem.at[p], z_sem.at[p]]
@@ -1208,174 +1240,319 @@
             span = lambda k, sib=sib: sib.at[pl.ds(0, k)]
             extra = ()
             if name == "t":
-                place = lambda at: t_part.at[at, c]
-                parts = lambda at: [(None, [t_part.at[at, c], t_sib.at[at]])]
-                theirs = lambda at: t_part.at[at, other]
+                place = lambda at: held["t"].at[at, c]
+                parts = lambda at: [(None, [held["t"].at[at, c], t_sib.at[at]])]
+                theirs = lambda at: held["t"].at[at, other]
                 extra = (resid,)
             elif name == "q":
-                place = lambda at: q_full.at[at]
-                parts = lambda at: [(c, [q_part.at[at, c]]), (other, [q_sib.at[at]])]
-                theirs = lambda at: q_part.at[at, other]
+                place = lambda at: held["q_full"].at[at]
+                parts = lambda at: [(c, [held["q"].at[at, c]]), (other, [q_sib.at[at]])]
+                theirs = lambda at: held["q"].at[at, other]
             else:
                 place = lambda at, own=own: own.at[at]
                 parts = lambda at, own=own, sib=sib: [(None, [own.at[at], sib.at[at]])]
-                theirs = lambda at, src=src: src.at[at, other]
-            piece[name] = Scatter(net, parts, place, theirs, landing, span, xbuf, zbuf, out, sems, name == "t", extra)
-            piece[name].clear_edges()
+                theirs = lambda at, name=name: held[name].at[at]
+            piece[name] = Scatter(
+                net, parts, place, theirs, landing, span, xbuf, zbuf, result, sems, name == "t", extra, name in "dio"
+            )
         whole = AllSum(net, value, got, sum_send, sum_recv)
-        swap = remote(gctx_in.at[other], gctx_all.at[c], swap_sem.at[0], swap_sem.at[1], net.sibling)
-        net.barrier()
-        swap.start()
-        gctx_all[c] = gctx_in[c]
-
-        def begin(name):
-            piece[name].start()
-            copies[name].wait()
-
-        def prepare():
-            for copy in loads:
-                copy.wait()
-            swap.wait()
-            tok_t[...] = jnp.transpose(tok_v[...], (1, 0))
-            lane = lambda p: slice(p * 128, (p + 1) * 128)
-            prepare_backward(
-                lambda p: jnp.concatenate([gctx_all[g, :, lane(p)] for g in range(nc)], axis=0), exact, do_m, delta_row
-            )
-
-        def token_grad(blk):
-            at = pl.ds(pl.multiple_of(blk * qlen, qlen), qlen)
-            return dot(dkv[at, :], w_v[:, half:3 * half], ((1,), (1,)))
-
-        def put_tokens(blk, grad):
-            for g in range(nc):
-                t_part[blk, g] = grad[g * rows:(g + 1) * rows].astype(BF16)
-            piece["t"].send(blk, blk)
-
-        def weights():
-            grad_q[...] = jnp.concatenate([join_dq(dq_scr, p) for p in range(pairs)], axis=1)
-            mine = pl.ds(pl.multiple_of(net.b * qlen, qlen), qlen)
-            for k in range(3):
-                if k:
-                    grad = dot(tok_t[...], dkv[:, (k - 1) * half:k * half])
-                else:
-                    grad = dot(tok_t[:, mine], grad_q[...])
-                for at in range(owners):
-                    for g in range(nc):
-                        i = at * nc + g
-                        q_part[at, g, :, k * half:(k + 1) * half] = grad[i * r:(i + 1) * r].astype(BF16)
-
-        def own_tokens():
-            put_tokens(net.b, token_grad(net.b) + dot(grad_q[...], w_v[:, 0:half], ((1,), (1,))))
-
-        def small_sums():
-            lanes = pl.ds(pl.multiple_of(c * half, 128), half)
-            value[0] = sums_in[...]
-            value[0, 0:1, lanes] = column_sum(grad_q[...].astype(F32))
-            value[0, 1:2, lanes] = column_sum(dkv[:, half:2 * half].astype(F32))
-
+        swap = remote(gctx.at[other], gctx_all.at[c], swap_sem.at[0], swap_sem.at[1], net.sibling)
+        st = {}
+
+        def split(name, at, first, second):
+            mine = c == 0
+            own = {"d": d_own, "i": i_own, "o": o_own}[name]
+            own[at] = jnp.where(mine, first, second).astype(BF16)
+            held[name][at] = jnp.where(mine, second, first).astype(BF16)
+
+        def split_rows(name, d, grad, per):
+            for a in range(nb):
+                at = 2 * a * per
+                split(name, d * nb + a, grad[at:at + per], grad[at + per:at + 2 * per])
+            piece[name].start_home(d)
+
+        def feed_forward_steps(w_o, w_i, w_d, act, slope, pre_grad, norm_t, ctx_t, d_out, i_out, o_out):
+            held.update(d=d_out, i=i_out, o=o_out)
+            loads = [
+                pltpu.make_async_copy(src, dst, load_sem.at[i])
+                for i, (src, dst) in enumerate([(wo_h, w_o), (wi_h, w_i), (wd_h, w_d)])
+            ]
+            for load in loads:
+                load.start()
+            bias_out, gain_one, shift_one = vecs_in[2:3, :], vecs_in[3:4, :], vecs_in[4:5, :]
+            bias_down, gain_two, shift_two = vecs_in[5:6, :], vecs_in[6:7, :], vecs_in[7:8, :]
+
+            def enter():
+                for p in piece.values():
+                    p.clear_edges()
+                net.barrier()
+                context = jnp.concatenate([ctx_in[g] for g in range(nc)], axis=1)
+                ctx_t[...] = jnp.transpose(context, (1, 0))
+                loads[0].wait()
+                resid_one = tok_in[...].astype(F32) + (dot(context, w_o[...]) + bias_out)
+                st["unit_one"], st["scale_one"] = norm_parts(resid_one)
+                st["normed"] = st["unit_one"] * gain_one + shift_one
+                st["low"] = st["normed"].astype(BF16)
+                norm_t[...] = jnp.transpose(st["low"], (1, 0))
+                loads[1].wait()
+
+            def expand(at):
+                pre = dot(st["low"], w_i[:, at]) + bias_in[0:1, at]
+                result, grad = gelu_and_slope(pre)
+                act[:, at] = result.astype(BF16)
+                slope[:, at] = grad
+
+            def turn():
+                loads[2].wait()
+                unit, scale = norm_parts(st["normed"] + (dot(act[...], w_d[...]) + bias_down))
+                out[...] = (unit * gain_two + shift_two).astype(BF16)
+                grad_out = cot_in[...].astype(F32)
+                st["two"] = norm_back(grad_out, unit, scale, gain_two)
+                st["ffn"] = st["two"].astype(BF16)
+                value[0] = jnp.zeros((n_sums, width), F32)
+                value[0, 5:6, :] = column_sum(st["ffn"].astype(F32))
+                value[0, 6:7, :] = column_sum(grad_out * unit)
+                value[0, 7:8, :] = column_sum(grad_out)
+
+            def down(mask):
+                d = net.flips(mask)
+                lanes = pl.ds(pl.multiple_of(d * (ff // nd), 128), ff // nd)
+                split_rows("d", d, dot(act[:, lanes], st["ffn"], ((0,), (0,))), r_ff)
+
+            def pre(i, at):
+                grad = (dot(st["ffn"], w_d[at, :], ((1,), (1,))) * slope[:, at]).astype(BF16)
+                pre_grad[:, at] = grad
+                value[0, 8 + i:9 + i, :] = column_sum(grad.astype(F32))
+                st["two"] = st["two"] + dot(grad, w_i[:, at], ((1,), (1,)))
+
+            def norm_one():
+                grad = st["two"]
+                value[0, 3:4, :] = column_sum(grad * st["unit_one"])
+                value[0, 4:5, :] = column_sum(grad)
+                grad = norm_back(grad, st["unit_one"], st["scale_one"], gain_one)
+                resid[...] = grad
+                st["attn"] = grad.astype(BF16)
+                value[0, 2:3, :] = column_sum(st["attn"].astype(F32))
+                grad = dot(st["attn"], w_o[...], ((1,), (1,))).astype(BF16)
+                for g in range(nc):
+                    gctx[g] = grad[:, g * half:(g + 1) * half]
+                swap.start()
+                gctx_all[c] = gctx[c]
+
+            def weight_in(mask):
+                d = net.flips(mask)
+                at = pl.ds(pl.multiple_of(d * (width // nd), 8), width // nd)
+                split_rows("i", d, dot(norm_t[at, :], pre_grad[...]), r)
+
+            def weight_out():
+                for d in range(nd):
+                    at = slice(d * (width // nd), (d + 1) * (width // nd))
+                    split_rows("o", d, dot(ctx_t[at, :], st["attn"]), r)
+
+            masks = range(nd - 1, -1, -1)
+            acts = [enter] + [functools.partial(expand, at) for at in chunks] + [turn]
+            acts += [functools.partial(down, m) for m in masks]
+            acts += [functools.partial(pre, i, at) for i, at in enumerate(chunks)] + [norm_one]
+            return acts + [functools.partial(weight_in, m) for m in masks] + [weight_out]
+
+        n_ffn = 4 + 2 * len(chunks) + 2 * nd
+        steps = nb * pairs
+        n_work = n_ffn + 1 + steps + 4 + len(whole.stages())
         order = []
         for name in names:
             p = piece[name]
-            if name in copies:
-                order.append((back_time(nd, nb, name, "start"), functools.partial(begin, name), None))
             for mask in range(p.nd):
                 for e in range(nb):
                     order.append((back_time(nd, nb, name, mask, e), functools.partial(p.reduce, mask, e), None))
-        steps = nb * pairs
-        work = [prepare] + [None] * steps + [weights, piece["q"].start, own_tokens, small_sums] + whole.stages()
-        for i, act in enumerate(work):
-            order.append((back_time(nd, nb, "work", i, len(work)), act, i - 1 if act is None else None))
+        for i in range(n_work):
+            order.append((back_time(nd, nb, "work", i, n_work), None, i))
         order.sort(key=lambda q: q[0])
-        first = next(i for i, q in enumerate(order) if q[2] == 0)
-        last = next(i for i, q in enumerate(order) if q[2] == steps - 1)
-        for _, act, _ in order[:first]:
-            act()
-        beside = {}
-        for _, act, i in order[first:last + 1]:
-            if act is None:
-                at_step = i
-            else:
-                beside.setdefault(at_step, []).append(act)
-
-        def attention(i, carry):
-            pair = i % pairs
-            blk = net.near_at(nb - 1 - i // pairs)
-            at = pl.ds(pl.multiple_of(blk * qlen, qlen), qlen)
-
-            def put(dk, dv):
-                dkv[at, pl.ds(pl.multiple_of(pair * 128, 128), 128)] = dk.astype(BF16)
-                dkv[at, pl.ds(pl.multiple_of(half + pair * 128, 128), 128)] = dv.astype(BF16)
-
-            bwd_pair(pair, qaug, kaug[pair, at, :], v_scr[pair, at, :], do_m, lse_row, delta_row, dq_scr, put, i < pairs)
-
-            @pl.when((pair == pairs - 1) & (i < steps - 1))
-            def _():
-                put_tokens(blk, token_grad(blk))
-
-            for g, acts in beside.items():
-
-                @pl.when(i == g)
-                def _(acts=acts):
-                    for act in acts:
-                        act()
-
-            return carry
-
-        lax.fori_loop(0, steps, attention, 0)
-        for _, act, _ in order[last + 1:]:
-            act()
-        for k in range(3):
-            for g in range(nc):
-                lanes = slice((k * nc + g) * half, (k * nc + g + 1) * half)
-                g_qkv[:, lanes] = q_out[g, :, k * half:(k + 1) * half]
-        me = (net.d * nb + net.b) * nc + c
-        feature = lax.broadcasted_iota(jnp.int32, (width, 128), 0)
-        lane = lax.broadcasted_iota(jnp.int32, (width, 128), 1)
-        pick = jnp.where((feature == me * r + lane) & (lane < r), 1.0, 0.0).astype(F32)
-        in_row, in_lane = (me * r_ff) // width, (me * r_ff) % width
-        pick_in = jnp.where((feature == in_lane + lane) & (lane < r_ff), 1.0, 0.0).astype(F32)
-        exactly = dict(precision=lax.Precision.HIGHEST, preferred_element_type=F32)
-        g_small[0:8, :] = jnp.dot(value[0, 0:8, :], pick, **exactly)
-        found = jnp.dot(value[0, 8:16, :], pick_in, **exactly)
-        row = lax.broadcasted_iota(jnp.int32, found.shape, 0)
-        g_small[8:16, :] = jnp.broadcast_to(column_sum(jnp.where(row == in_row, found, 0.0)), (8, 128))
-        for name in names:
-            piece[name].drain()
+        index = [i for i, q in enumerate(order) if q[2] is not None]
+        first, last = index[n_ffn + 1], index[n_ffn + steps]
+
+        def run(entries, acts, base):
+            for _, act, i in entries:
+                (act if i is None else acts[i - base])()
+
+        def feed_forward_scope(*refs):
+            run(order[:index[n_ffn - 1] + 1], feed_forward_steps(*refs), 0)
+            for name in "dio":
+                piece[name].sent()
+
+        def attention_scope(tok_t, w_v, kaug, v_scr, qaug, do_m, delta_row, dq_scr, dkv, t_part, q_part, q_full):
+            held.update(t=t_part, q=q_part, q_full=q_full)
+            loads = [(qaug_h, qaug)]
+            for k in range(3):
+                lanes = pl.ds(pl.multiple_of((k * nc + c) * half, 128), half)
+                loads.append((w_h.at[:, lanes], w_v.at[:, pl.ds(k * half, half)]))
+            loads.append((tok_t_h, tok_t))
+            loads = [pltpu.make_async_copy(src, dst, load_sem.at[3 + i]) for i, (src, dst) in enumerate(loads)]
+
+            def block_loads(blk):
+                at = pl.ds(pl.multiple_of(blk * qlen, qlen), qlen)
+                return [
+                    pltpu.make_async_copy(kaug_h.at[:, at], kaug.at[:, at], load_sem.at[8 + blk]),
+                    pltpu.make_async_copy(v_h.at[:, at], v_scr.at[:, at], load_sem.at[8 + nb + blk]),
+                ]
+
+            loads[0].start()
+            for e in range(nb - 1, -1, -1):
+                for copy in block_loads(net.near(e)):
+                    copy.start()
+            for copy in loads[1:]:
+                copy.start()
+
+            def prepare():
+                swap.wait()
+                lane = lambda p: slice(p * 128, (p + 1) * 128)
+                prepare_backward(
+                    lambda p: jnp.concatenate([gctx_all[g, :, lane(p)] for g in range(nc)], axis=0), exact, do_m, delta_row
+                )
+                for copy in loads:
+                    copy.wait()
+
+            def token_grad(blk):
+                at = pl.ds(pl.multiple_of(blk * qlen, qlen), qlen)
+                return dot(dkv[at, :], w_v[:, half:3 * half], ((1,), (1,)))
+
+            def put_tokens(blk, grad):
+                for g in range(nc):
+                    t_part[blk, g] = grad[g * rows:(g + 1) * rows].astype(BF16)
+                piece["t"].send(blk, blk)
+
+            def weights():
+                grad_q[...] = jnp.concatenate([join_dq(dq_scr, p) for p in range(pairs)], axis=1)
+                mine = pl.ds(pl.multiple_of(net.b * qlen, qlen), qlen)
+                for k in range(3):
+                    if k:
+                        grad = dot(tok_t[...], dkv[:, (k - 1) * half:k * half])
+                    else:
+                        grad = dot(tok_t[:, mine], grad_q[...])
+                    for at in range(owners):
+                        for g in range(nc):
+                            i = at * nc + g
+                            q_part[at, g, :, k * half:(k + 1) * half] = grad[i * r:(i + 1) * r].astype(BF16)
+
+            def own_tokens():
+                put_tokens(net.b, token_grad(net.b) + dot(grad_q[...], w_v[:, 0:half], ((1,), (1,))))
+
+            def small_sums():
+                lanes = pl.ds(pl.multiple_of(c * half, 128), half)
+                value[0, 0:1, lanes] = column_sum(grad_q[...].astype(F32))
+                value[0, 1:2, lanes] = column_sum(dkv[:, half:2 * half].astype(F32))
+
+            acts = [prepare] + [None] * steps + [weights, piece["q"].start, own_tokens, small_sums] + whole.stages()
+            run(order[index[n_ffn - 1] + 1:first], acts, n_ffn)
+            beside = {}
+            for _, act, i in order[first:last + 1]:
+                if i is not None:
+                    at_step = i - n_ffn - 1
+                else:
+                    beside.setdefault(at_step, []).append(act)
+
+            def attention(i, carry):
+                pair = i % pairs
+                blk = net.near_at(nb - 1 - i // pairs)
+                at = pl.ds(pl.multiple_of(blk * qlen, qlen), qlen)
+
+                @pl.when(pair == 0)
+                def _():
+                    for copy in block_loads(blk):
+                        copy.wait()
+
+                def put(dk, dv):
+                    dkv[at, pl.ds(pl.multiple_of(pair * 128, 128), 128)] = dk.astype(BF16)
+                    dkv[at, pl.ds(pl.multiple_of(half + pair * 128, 128), 128)] = dv.astype(BF16)
+
+                bwd_pair(pair, qaug, kaug[pair, at, :], v_scr[pair, at, :], do_m, lse_row, delta_row, dq_scr, put, i < pairs)
+
+                @pl.when((pair == pairs - 1) & (i < steps - 1))
+                def _():
+                    put_tokens(blk, token_grad(blk))
+
+                for g, acts in beside.items():
+
+                    @pl.when(i == g)
+                    def _(acts=acts):
+                        for act in acts:
+                            act()
+
+                return carry
+
+            lax.fori_loop(0, steps, attention, 0)
+            run(order[last + 1:], acts, n_ffn)
+            for k in range(3):
+                for g in range(nc):
+                    lanes = slice((k * nc + g) * half, (k * nc + g + 1) * half)
+                    g_qkv[:, lanes] = q_out[g, :, k * half:(k + 1) * half]
+            me = (net.d * nb + net.b) * nc + c
+            feature = lax.broadcasted_iota(jnp.int32, (width, 128), 0)
+            lane = lax.broadcasted_iota(jnp.int32, (width, 128), 1)
+            pick = jnp.where((feature == me * r + lane) & (lane < r), 1.0, 0.0).astype(F32)
+            in_row, in_lane = (me * r_ff) // width, (me * r_ff) % width
+            pick_in = jnp.where((feature == in_lane + lane) & (lane < r_ff), 1.0, 0.0).astype(F32)
+            exactly = dict(precision=lax.Precision.HIGHEST, preferred_element_type=F32)
+            g_small[0:8, :] = jnp.dot(value[0, 0:8, :], pick, **exactly)
+            found = jnp.dot(value[0, 8:16, :], pick_in, **exactly)
+            row = lax.broadcasted_iota(jnp.int32, found.shape, 0)
+            g_small[8:16, :] = jnp.broadcast_to(column_sum(jnp.where(row == in_row, found, 0.0)), (8, 128))
+            for name in names:
+                piece[name].drain()
+
+        pl.run_scoped(feed_forward_scope, *scopes[0])
+        pl.run_scoped(attention_scope, *scopes[1])
 
     block = {"d": (r_ff, width), "i": (r, ff), "o": (r, width), "t": (rows, width)}
     joined = (nc, r, 3 * half)
     vmem = lambda shape, kind=BF16: pltpu.VMEM(shape, kind)
+    held_out = [vmem((owners,) + block[k]) for k in "dio"]
+    scopes = (
+        [
+            vmem((width, width)),
+            vmem((width, ff)),
+            vmem((ff, width)),
+            vmem((rows, ff)),
+            vmem((rows, ff), F32),
+            vmem((rows, ff)),
+            vmem((width, rows)),
+            vmem((width, rows)),
+        ]
+        + held_out,
+        [
+            vmem((width, total)),
+            vmem((width, 3 * half)),
+            vmem((pairs, total, 256)),
+            vmem((pairs, total, 128)),
+            vmem((heads, qlen, 256)),
+            vmem((heads, qlen, 128)),
+            vmem((heads, 8, qlen), F32),
+            vmem((heads, 128, qlen), F32),
+            vmem((total, 2 * half)),
+            vmem((nb, nc, rows, width)),
+            vmem((owners,) + joined),
+            vmem((owners,) + joined),
+        ],
+    )
     scratch = [vmem((owners,) + block[k]) for k in "dio"] + [vmem((owners,) + block[k]) for k in "dio"]
     scratch += [vmem((nb,) + block["t"]), vmem((owners, r, 3 * half))]
     scratch += [vmem(((nd - 1) * nb,) + block[k]) for k in "dio"] + [vmem(((nd - 1) * nb,) + joined)]
     scratch += [vmem((nb + 1,) + block[k]) for k in "diot"] + [vmem((nb + 1,) + joined)]
     scratch += [
-        vmem((nb, nc, rows, width)),
-        vmem((owners,) + joined),
-        vmem((owners,) + joined),
         vmem(joined, F32),
-        vmem((total, width)),
-        vmem((width, total)),
-        vmem((width, 3 * half)),
-        vmem((pairs, total, 256)),
-        vmem((pairs, total, 128)),
-        vmem((heads, qlen, 256)),
+        vmem((rows, width), F32),
         vmem((nc, rows, half)),
-        vmem((heads, qlen, 128)),
-        vmem((heads, 8, qlen), F32),
-        vmem((heads, 128, qlen), F32),
-        vmem((total, 2 * half)),
+        vmem((nc, rows, half)),
         vmem((qlen, half)),
-        vmem((levels + 2,) + sums.shape, F32),
-        vmem((levels + nb,) + sums.shape, F32),
-        pltpu.SemaphoreType.DMA((3,)),
-        pltpu.SemaphoreType.DMA((7,)),
+        vmem((levels + 2, n_sums, width), F32),
+        vmem((levels + nb, n_sums, width), F32),
+        pltpu.SemaphoreType.DMA((8 + 2 * nb,)),
         pltpu.SemaphoreType.DMA((2,)),
     ]
     scratch += scatter_sems(5, nd, nb) + [pltpu.SemaphoreType.DMA((levels + nb,))] * 2
     return pl.pallas_call(
         kernel,
         out_shape=[
+            jax.ShapeDtypeStruct((rows, width), BF16),
             jax.ShapeDtypeStruct((rows, width), F32),
             jax.ShapeDtypeStruct((r, 3 * width), F32),
             jax.ShapeDtypeStruct((r, width), F32),
@@ -1383,11 +1560,11 @@
             jax.ShapeDtypeStruct((r_ff, width), F32),
             jax.ShapeDtypeStruct((16, 128), F32),
         ],
-        in_specs=[HBM] * 8 + [VMEM] * 5,
-        out_specs=[VMEM] * 6,
+        in_specs=[VMEM] * 5 + [HBM] * 8 + [VMEM] * 2,
+        out_specs=[VMEM] * 7,
         scratch_shapes=scratch,
         compiler_params=params(62, 3),
-    )(dw_down, dw_in, dw_out, tok, w_qkv, kaug_in, v_in, qaug_in, lse, exact_in, gctx, resid_grad, sums)
+    )(ctx, tok, cot, vecs, bias_in, w_out, w_in, w_down, tok_t_in, w_qkv, kaug_in, v_in, qaug_in, lse, exact_in)
 
 
 def body(
@@ -1422,23 +1599,20 @@
     cot = cotangent.reshape(rows, width)
     vectors = [bias_query, bias_value, bias_out, gain_attn, shift_attn, bias_down, gain_ffn, shift_ffn]
     if nb * qlen <= 2048 and r % 8 == 0 and ff // width <= 8:
-        small = pack_vectors(vectors, bias_in)
-        ctx2, vecs, full_bin, lse, exact, f_qkv, tok_all, f_out, f_in, f_down, kaug, v_all, qaug = front(
-            small, w_qkv, flat_in, w_out, w_in, w_down, segment, nd, nb, nc
+        few, many = pack_vectors(vectors, bias_in)
+        ctx2, vecs, full_bin, lse, exact, f_qkv, _, f_out, f_in, f_down, kaug, v_all, qaug, tok_t = front(
+            few, many, w_qkv, flat_in, w_out, w_in, w_down, segment, nd, nb, nc
         )
-        out, resid_grad, gctx2, dw_down, dw_in, dw_out, sums = feed_forward(
-            ctx2, flat_in, cot, vecs, full_bin, f_out, f_in, f_down
+        out, g_tok, o_qkv, o_out, o_in, o_down, g_small = back(
+            ctx2, flat_in, cot, vecs, full_bin, f_out, f_in, f_down,
+            tok_t, f_qkv, kaug, v_all, qaug, lse, exact, nd, nb, nc,
         )
-        g_tok, o_qkv, o_out, o_in, o_down, g_small = back(
-            dw_down.reshape(nd * nb, nc, r_ff, width),
-            dw_in.reshape(nd * nb, nc, r, ff),
-            dw_out.reshape(nd * nb, nc, r, width),
-            tok_all, f_qkv, kaug, v_all, qaug, lse, exact, gctx2, resid_grad, sums, nd, nb, nc,
+        out, g_tok, o_qkv, o_out, o_in, o_down, g_bq, g_bv, g_bo, g_g1, g_s1, g_bd, g_g2, g_s2, g_bin = hand_out(
+            [out, g_tok, o_qkv, o_out, o_in, o_down], g_small, r, r_ff
         )
-        g_bq, g_bv, g_bo, g_g1, g_s1, g_bd, g_g2, g_s2 = (g_small[i, :r] for i in range(8))
         return (
             out.reshape(seqs, rows, width), g_tok.reshape(seqs, rows, width),
-            o_qkv, g_bq, g_bv, o_out, g_bo, g_g1, g_s1, o_in, g_small[8, :r_ff], o_down, g_bd, g_g2, g_s2,
+            o_qkv, g_bq, g_bv, o_out, g_bo, g_g1, g_s1, o_in, g_bin, o_down, g_bd, g_g2, g_s2,
         )
     packed = jnp.concatenate(vectors + [bias_in])
     used = packed.shape[0]

time: 225 us -> 196 us (0.87)
  Pallas kernels: 209 us -> 191 us
  local copies, waits for them, and re-layouts: 14.7 us -> 1.25 us
    pallas_call x2, Pallas kernels: 118 us -> 105 us  [the longest x1 102 us: back(): pl.pallas_call(kernel, out_shape=[jax.ShapeDtypeStruct((rows, width), BF1...]
    unnamed x5 -> x0, local copies, waits for them, and re-layouts: 8.6 us -> none
    pallas_call x1, Pallas kernels: 90.4 us -> 85.7 us  [front(): pl.pallas_call(kernel, out_shape=[jax.ShapeDtypeStruct((nc, rows, half),...]
    pad x5 -> x0, local copies, waits for them, and re-layouts: 3.36 us -> none  [pack_vectors(): line = jnp.pad(v.astype(F32), (0, 128 - v.shape[0]))]
    squeeze x2 -> x0, local copies, waits for them, and re-layouts: 2.7 us -> none  [the longest x1 1.52 us: body(): g_small[i, :r]]
where the time goes in v3:
time: 196 us; the launch traced here: 194 us
  Pallas kernels  191 us (97%)
    pallas_call x1, Pallas kernels, back(): pl.pallas_call(kernel, out_shape=[jax.ShapeDtypeStruct((rows, width), BF1...  102 us
    pallas_call x1, Pallas kernels, front(): pl.pallas_call(kernel, out_shape=[jax.ShapeDtypeStruct((nc, rows, half),...  85.7 us

profile of v3, /device:TPU:0, one launch (start us, length us, event | category | flops | bytes accessed | tf_op | source)
XLA Modules:
  0.0 194.4 jit_solution(4068182204689206517)
XLA Ops:
  0.7 1.5 select_select_fusion.few_in
  2.1 1.2 broadcast_in_dim.69.many_in
  3.4 85.7 %shard_map.271 = (bf16[2,256,384]{2,1,0:T(8,128)(2,1)}, f32[8,768]{1,0:T(8,128)}, f32[1,3072]{1,0:T(1,128)}, f32[6,8,512]{2,1,0:T(8,128)}, f32[3,512,128]{2,1,0:...) custom-call(bf16[16,24]{1,0:T(8,128)(2,1)} %select_select_fusion.few, ...), custom_call_target="tpu_custom_call" | custom-call | tf_op jit(solution)/shard_map/pallas_call | solution.py:1134
  89.1 101.6 %shard_map.272 = (bf16[256,768]{1,0:T(8,128)(2,1)}, f32[256,768]{1,0:T(8,128)}, f32[24,2304]{1,0:T(8,128)}, f32[24,768]{1,0:T(8,128)}, f32[24,3072]{1,0:T(8,128)}, /*index=5*/f32[96,768]{1,0:T(8,128)}, f32[16,128]{1,0:T(8,128)}) custom-call(bf16[2,256,384]{2,1,0:T(8,128)(2,1)} %get-tuple-element.50.ctx_in, bf16[256,768]{1,0:T(8,128)(2,1)} %bitcast.5, ...), custom_call_target="tpu_custom_call" | custom-call | tf_op jit(solution)/shard_map/pallas_call | solution.py:1552
  190.8 3.4 %shard_map.273 = (bf16[256,768]{1,0:T(8,128)(2,1)}, f32[256,768]{1,0:T(8,128)}, f32[24,2304]{1,0:T(8,128)}, f32[24,768]{1,0:T(8,128)}, f32[24,3072]{1,0:T(8,128)...) custom-call(bf16[256,768]{1,0:T(8,128)(2,1)} %get-tuple-element.63.r, ...), custom_call_target="tpu_custom_call" | custom-call | tf_op jit(solution)/shard_map/pallas_call | solution.py:920
  (4 shorter events, 0.0 us)
